TPU v7x, 256 devices: a whole 4x4x8 slice. The times are simulated.
256 devices in a mesh: seq: 64 (over z, y_hi, x), tp: 4 (over y_lo, core).
Axes of the slice: x: 4, y: 4 (y_hi: 2, y_lo: 2; y = y_hi * 2 + y_lo), z: 8, core: 2. Of those that a mesh axis runs over, the one named last changes fastest.
Arguments:
- query_rows: bfloat16 [32768, 1536], P('seq', 'tp'), may hold values from -48 to 48
- key_rows: bfloat16 [32768, 1536], P('seq', 'tp'), may hold values from -8 to 8
- value_rows: bfloat16 [32768, 1536], P('seq', 'tp'), may hold values from -6 to 6
- frame_counts: int32 [12], replicated, may hold values from 1 to 16, 128 in all
- out_weight: bfloat16 [1536, 3072], P('tp'), may hold values from -0.15625 to 0.15625
Outputs:
- mixed: bfloat16 [32768, 3072], P('seq', 'tp')
Inputs may be any that keep to these rules, and one draw needn't show every extreme that they name: `frame_counts`: the 12 clips' frame counts sum to 128; the longest has exactly 16 frames.
All inputs are finite; a program needn't handle non-finite values.
Results may differ from a plain program's by a relative error of at most 0.015.
Values may be sent and summed in bfloat16 or wider, within the bound.
No kernel may reach another device: no remote copies, remote signals or barrier semaphores. Data moves between devices by JAX's collectives and lax.ppermute only.
A program may use at most 64 MiB of HBM per device.

v0:
```python
import math

import jax
import jax.numpy as jnp
from jax import lax
from jax.sharding import PartitionSpec as P

RT = 16
RH = 56
RW = 56
PH = 16
PW = 16
HEAD_DIM = 128


NEG_FILL = -1e30
ROPE_BASE = 256.0


def from_behind(value, axis, by):
    count = lax.axis_size(axis)
    return lax.ppermute(value, axis, [(i, (i + by) % count) for i in range(count)])


def clip_layout(frame_counts, token_index):
    clip_sizes = frame_counts * (PH * PW)
    clip_ends = jnp.cumsum(clip_sizes)
    passed = token_index[:, None] >= clip_ends[None, :]
    clip_id = jnp.sum(passed.astype(jnp.int32), axis=1)
    clip_start = jnp.sum(jnp.where(passed, clip_sizes[None, :], 0), axis=1)
    return (clip_id, token_index - clip_start)


def rotate(features, offset):
    frame_size = PH * PW
    coordinates = (offset // frame_size, offset % frame_size // PW, offset % PW)
    pieces = []
    section_start = 0
    for section_width, coordinate in zip((RT, RH, RW), coordinates):
        half_width = section_width // 2
        section = features[:, :, section_start : section_start + section_width]
        first_half = section[..., :half_width]
        second_half = section[..., half_width:]
        frequency = jnp.exp(
            -(2.0 * jnp.arange(half_width, dtype=jnp.float32) / section_width) * math.log(ROPE_BASE)
        )
        phase_angle = coordinate.astype(jnp.float32)[:, None] * frequency[None, :]
        cosine = jnp.cos(phase_angle)[:, None, :]
        sine_part = jnp.sin(phase_angle)[:, None, :]
        pieces.append(first_half * cosine - second_half * sine_part)
        pieces.append(second_half * cosine + first_half * sine_part)
        section_start = section_start + section_width
    return jnp.concatenate(pieces, axis=2)


def per_device(query_rows, key_rows, value_rows, frame_counts, out_weight):
    tok_count = query_rows.shape[0]
    head_count = query_rows.shape[1] // HEAD_DIM
    cycle_size = lax.axis_size("seq")
    position = lax.axis_index("seq")
    offsets = jnp.arange(tok_count, dtype=jnp.int32)
    local_index = position * tok_count + offsets
    query_clip, query_offset = clip_layout(frame_counts, local_index)
    rotated_q = rotate(
        query_rows.astype(jnp.float32).reshape(tok_count, head_count, HEAD_DIM), query_offset
    ).astype(jnp.bfloat16)
    rotated_k = rotate(
        key_rows.astype(jnp.float32).reshape(tok_count, head_count, HEAD_DIM), query_offset
    ).astype(jnp.bfloat16)
    rotated_k = rotated_k.reshape(tok_count, head_count * HEAD_DIM)
    scale_factor = HEAD_DIM ** (-0.5)
    frame_total = tok_count * cycle_size // (PH * PW)
    longest = frame_total // 8 * PH * PW
    reach_count = min((longest + tok_count - 1) // tok_count, cycle_size - 1)

    def absorb(state, key_block, value_block, key_index, key_valid):
        run_max, run_total, accum = state
        block_len = key_block.shape[0]
        key_heads = key_block.reshape(block_len, head_count, HEAD_DIM)
        value_heads = value_block.reshape(block_len, head_count, HEAD_DIM)
        key_clip, unused_offset = clip_layout(frame_counts, key_index)
        scores = (
            jnp.einsum("thd,shd->hts", rotated_q, key_heads, preferred_element_type=jnp.float32)
            * scale_factor
        )
        allowed = (query_clip[:, None] == key_clip[None, :]) & key_valid[None, :]
        scores = jnp.where(allowed[None], scores, NEG_FILL)
        new_max = jnp.maximum(run_max, jnp.max(scores, axis=2))
        expo = jnp.where(allowed[None], jnp.exp(scores - new_max[:, :, None]), 0.0)
        rescale = jnp.exp(run_max - new_max)
        run_total = run_total * rescale + jnp.sum(expo, axis=2)
        accum = accum * rescale[:, :, None] + jnp.einsum(
            "hts,shd->htd",
            expo.astype(jnp.bfloat16),
            value_heads,
            preferred_element_type=jnp.float32,
        )
        return (new_max, run_total, accum)

    start_state = (
        jnp.full((head_count, tok_count), NEG_FILL, jnp.float32),
        jnp.zeros((head_count, tok_count), jnp.float32),
        jnp.zeros((head_count, tok_count, HEAD_DIM), jnp.float32),
    )
    stacked = jnp.stack([rotated_k, value_rows])
    always_valid = jnp.ones((tok_count,), jnp.bool_)
    ahead = from_behind(stacked, "seq", -reach_count)
    ahead_source = (position + reach_count) % cycle_size
    first_state = absorb(
        start_state, ahead[0], ahead[1], ahead_source * tok_count + offsets, always_valid
    )

    def onward(distance, carry):
        pair, state = carry
        pair = from_behind(pair, "seq", 1)
        source = (position + reach_count - distance + cycle_size) % cycle_size
        state = absorb(state, pair[0], pair[1], source * tok_count + offsets, always_valid)
        return (pair, state)

    final_state = lax.fori_loop(1, 2 * reach_count + 1, onward, (ahead, first_state))[1]
    run_max, run_total, accum = final_state
    attended = (
        (accum / run_total[:, :, None])
        .transpose(1, 0, 2)
        .reshape(tok_count, head_count * HEAD_DIM)
        .astype(jnp.bfloat16)
    )
    head_terms = jnp.dot(attended, out_weight, preferred_element_type=jnp.float32)
    mixed = lax.psum_scatter(head_terms.astype(jnp.bfloat16), "tp", scatter_dimension=1, tiled=True)
    return mixed


def solution(mesh):
    return jax.shard_map(
        per_device,
        mesh=mesh,
        in_specs=(P("seq", "tp"), P("seq", "tp"), P("seq", "tp"), P(), P("tp", None)),
        out_specs=P("seq", "tp"),
        check_vma=False,
    )
```

profile of v0, /device:TPU:1, one launch (start us, length us, event | category | flops | bytes accessed | tf_op | source)
XLA Modules:
  0.0 512.1 jit_solution(16693287515472825750)
XLA Ops:
  13.7 2.1 copy.89
  17.1 2.2 copy.95
  19.2 2.1 copy.96
  31.7 2.7 multiply_cosine_fusion
  34.4 3.3 add_convert_fusion
  37.7 1.5 add_convert_fusion.1
  39.9 1.4 add_convert_fusion.2
  41.3 3.0 concatenate.8
  46.6 6.4 %collective-permute-start.1 = (bf16[2,512,384]{1,2,0:T(8,128)(2,1)}, bf16[2,512,384]{1,2,0:T(8,128)(2,1)}, u32[]{:S(2)}, u32[]{:S(2)}) collective-permute-start(bf16[2,512,384]{1,2,0:T(8,128)(2,1)} %pad_maximum_fusion), channel_id=1, source_target_pairs={{0,224},{4,228},{8,232},{12,236},{16,240},{20,244},{24,248},{28,25... | collective-permute-start | bytes 2359304 | tf_op jit(solution)/shard_map/ppermute | solution.py:22
  53.0 2.9 concatenate.9
  56.2 13.4 %collective-permute-done.1 = bf16[2,512,384]{1,2,0:T(8,128)(2,1)} collective-permute-done((bf16[2,512,384]{1,2,0:T(8,128)(2,1)}, bf16[2,512,384]{1,2,0:T(8,128)(2,1)}, u32[]{:S(2)}, u32[]{:S(2)}) %collective-permute-start.1) | collective-permute-done | bytes 786464 | tf_op jit(solution)/shard_map/ppermute | solution.py:22
  72.4 2.2 fusion.20
  74.6 374.9 %while.22 = (s32[]{:T(128)}, bf16[2,512,384]{1,2,0:T(8,128)(2,1)}, f32[3,512]{1,0:T(4,128)S(1)}, f32[3,512]{1,0:T(4,128)S(1)}, f32[3,512,128]{2,1,0:T(8,128)}, /...) while((s32[]{:T(128)}, bf16[2,512,384]{1,2,0:T(8,128)(2,1)}, ...), condition=%wide.region_11.12_spmd.clone, body=%wide.region_6.11_spmd.clone.sunk | while | flops 413553824 | bytes 25930348 | solution.py:120
  77.0 1.4 reduce-window.21
  80.0 19.4 %collective-permute-done = bf16[2,512,384]{1,2,0:T(8,128)(2,1)S(1)} collective-permute-done((bf16[2,512,384]{1,2,0:T(8,128)(2,1)}, bf16[2,512,384]{1,2,0:T(8,128)(2,1)S(1)}, u32[]{:S(2)}, u32[]{:S(2)}) %collective-permute-start) | collective-permute-done | bytes 786464 | tf_op jit(solution)/shard_map/while/body/eval_jaxpr/ppermute | solution.py:22
  101.1 1.5 fusion.67
  104.9 1.4 reduce-window.21
  107.9 18.6 %collective-permute-done = bf16[2,512,384]{1,2,0:T(8,128)(2,1)S(1)} collective-permute-done((bf16[2,512,384]{1,2,0:T(8,128)(2,1)}, bf16[2,512,384]{1,2,0:T(8,128)(2,1)S(1)}, u32[]{:S(2)}, u32[]{:S(2)}) %collective-permute-start) | collective-permute-done | bytes 786464 | tf_op jit(solution)/shard_map/while/body/eval_jaxpr/ppermute | solution.py:22
  128.2 1.5 fusion.67
  132.0 1.4 reduce-window.21
  135.0 17.7 %collective-permute-done = bf16[2,512,384]{1,2,0:T(8,128)(2,1)S(1)} collective-permute-done((bf16[2,512,384]{1,2,0:T(8,128)(2,1)}, bf16[2,512,384]{1,2,0:T(8,128)(2,1)S(1)}, u32[]{:S(2)}, u32[]{:S(2)}) %collective-permute-start) | collective-permute-done | bytes 786464 | tf_op jit(solution)/shard_map/while/body/eval_jaxpr/ppermute | solution.py:22
  154.4 1.5 fusion.67
  158.2 1.4 reduce-window.21
  161.2 16.8 %collective-permute-done = bf16[2,512,384]{1,2,0:T(8,128)(2,1)S(1)} collective-permute-done((bf16[2,512,384]{1,2,0:T(8,128)(2,1)}, bf16[2,512,384]{1,2,0:T(8,128)(2,1)S(1)}, u32[]{:S(2)}, u32[]{:S(2)}) %collective-permute-start) | collective-permute-done | bytes 786464 | tf_op jit(solution)/shard_map/while/body/eval_jaxpr/ppermute | solution.py:22
  179.7 1.5 fusion.67
  183.5 1.4 reduce-window.21
  186.5 15.8 %collective-permute-done = bf16[2,512,384]{1,2,0:T(8,128)(2,1)S(1)} collective-permute-done((bf16[2,512,384]{1,2,0:T(8,128)(2,1)}, bf16[2,512,384]{1,2,0:T(8,128)(2,1)S(1)}, u32[]{:S(2)}, u32[]{:S(2)}) %collective-permute-start) | collective-permute-done | bytes 786464 | tf_op jit(solution)/shard_map/while/body/eval_jaxpr/ppermute | solution.py:22
  204.1 1.5 fusion.67
  207.9 1.4 reduce-window.21
  210.9 14.9 %collective-permute-done = bf16[2,512,384]{1,2,0:T(8,128)(2,1)S(1)} collective-permute-done((bf16[2,512,384]{1,2,0:T(8,128)(2,1)}, bf16[2,512,384]{1,2,0:T(8,128)(2,1)S(1)}, u32[]{:S(2)}, u32[]{:S(2)}) %collective-permute-start) | collective-permute-done | bytes 786464 | tf_op jit(solution)/shard_map/while/body/eval_jaxpr/ppermute | solution.py:22
  227.5 1.5 fusion.67
  231.3 1.4 reduce-window.21
  234.3 14.0 %collective-permute-done = bf16[2,512,384]{1,2,0:T(8,128)(2,1)S(1)} collective-permute-done((bf16[2,512,384]{1,2,0:T(8,128)(2,1)}, bf16[2,512,384]{1,2,0:T(8,128)(2,1)S(1)}, u32[]{:S(2)}, u32[]{:S(2)}) %collective-permute-start) | collective-permute-done | bytes 786464 | tf_op jit(solution)/shard_map/while/body/eval_jaxpr/ppermute | solution.py:22
  250.0 1.5 fusion.67
  253.8 1.4 reduce-window.21
  256.8 13.1 %collective-permute-done = bf16[2,512,384]{1,2,0:T(8,128)(2,1)S(1)} collective-permute-done((bf16[2,512,384]{1,2,0:T(8,128)(2,1)}, bf16[2,512,384]{1,2,0:T(8,128)(2,1)S(1)}, u32[]{:S(2)}, u32[]{:S(2)}) %collective-permute-start) | collective-permute-done | bytes 786464 | tf_op jit(solution)/shard_map/while/body/eval_jaxpr/ppermute | solution.py:22
  271.6 1.5 fusion.67
  275.4 1.4 reduce-window.21
  278.4 12.6 %collective-permute-done = bf16[2,512,384]{1,2,0:T(8,128)(2,1)S(1)} collective-permute-done((bf16[2,512,384]{1,2,0:T(8,128)(2,1)}, bf16[2,512,384]{1,2,0:T(8,128)(2,1)S(1)}, u32[]{:S(2)}, u32[]{:S(2)}) %collective-permute-start) | collective-permute-done | bytes 786464 | tf_op jit(solution)/shard_map/while/body/eval_jaxpr/ppermute | solution.py:22
  292.8 1.5 fusion.67
  296.6 1.4 reduce-window.21
  299.5 12.6 %collective-permute-done = bf16[2,512,384]{1,2,0:T(8,128)(2,1)S(1)} collective-permute-done((bf16[2,512,384]{1,2,0:T(8,128)(2,1)}, bf16[2,512,384]{1,2,0:T(8,128)(2,1)S(1)}, u32[]{:S(2)}, u32[]{:S(2)}) %collective-permute-start) | collective-permute-done | bytes 786464 | tf_op jit(solution)/shard_map/while/body/eval_jaxpr/ppermute | solution.py:22
  313.9 1.5 fusion.67
  317.7 1.4 reduce-window.21
  320.7 12.6 %collective-permute-done = bf16[2,512,384]{1,2,0:T(8,128)(2,1)S(1)} collective-permute-done((bf16[2,512,384]{1,2,0:T(8,128)(2,1)}, bf16[2,512,384]{1,2,0:T(8,128)(2,1)S(1)}, u32[]{:S(2)}, u32[]{:S(2)}) %collective-permute-start) | collective-permute-done | bytes 786464 | tf_op jit(solution)/shard_map/while/body/eval_jaxpr/ppermute | solution.py:22
  335.0 1.5 fusion.67
  338.8 1.4 reduce-window.21
  341.8 12.6 %collective-permute-done = bf16[2,512,384]{1,2,0:T(8,128)(2,1)S(1)} collective-permute-done((bf16[2,512,384]{1,2,0:T(8,128)(2,1)}, bf16[2,512,384]{1,2,0:T(8,128)(2,1)S(1)}, u32[]{:S(2)}, u32[]{:S(2)}) %collective-permute-start) | collective-permute-done | bytes 786464 | tf_op jit(solution)/shard_map/while/body/eval_jaxpr/ppermute | solution.py:22
  356.1 1.5 fusion.67
  359.9 1.4 reduce-window.21
  362.9 12.6 %collective-permute-done = bf16[2,512,384]{1,2,0:T(8,128)(2,1)S(1)} collective-permute-done((bf16[2,512,384]{1,2,0:T(8,128)(2,1)}, bf16[2,512,384]{1,2,0:T(8,128)(2,1)S(1)}, u32[]{:S(2)}, u32[]{:S(2)}) %collective-permute-start) | collective-permute-done | bytes 786464 | tf_op jit(solution)/shard_map/while/body/eval_jaxpr/ppermute | solution.py:22
  377.3 1.5 fusion.67
  381.1 1.4 reduce-window.21
  384.0 13.6 %collective-permute-done = bf16[2,512,384]{1,2,0:T(8,128)(2,1)S(1)} collective-permute-done((bf16[2,512,384]{1,2,0:T(8,128)(2,1)}, bf16[2,512,384]{1,2,0:T(8,128)(2,1)S(1)}, u32[]{:S(2)}, u32[]{:S(2)}) %collective-permute-start) | collective-permute-done | bytes 786464 | tf_op jit(solution)/shard_map/while/body/eval_jaxpr/ppermute | solution.py:22
  399.4 1.5 fusion.67
  403.2 1.4 reduce-window.21
  406.2 14.7 %collective-permute-done = bf16[2,512,384]{1,2,0:T(8,128)(2,1)S(1)} collective-permute-done((bf16[2,512,384]{1,2,0:T(8,128)(2,1)}, bf16[2,512,384]{1,2,0:T(8,128)(2,1)S(1)}, u32[]{:S(2)}, u32[]{:S(2)}) %collective-permute-start) | collective-permute-done | bytes 786464 | tf_op jit(solution)/shard_map/while/body/eval_jaxpr/ppermute | solution.py:22
  422.6 1.5 fusion.67
  426.4 1.4 reduce-window.21
  429.4 15.7 %collective-permute-done = bf16[2,512,384]{1,2,0:T(8,128)(2,1)S(1)} collective-permute-done((bf16[2,512,384]{1,2,0:T(8,128)(2,1)}, bf16[2,512,384]{1,2,0:T(8,128)(2,1)S(1)}, u32[]{:S(2)}, u32[]{:S(2)}) %collective-permute-start) | collective-permute-done | bytes 786464 | tf_op jit(solution)/shard_map/while/body/eval_jaxpr/ppermute | solution.py:22
  446.9 1.5 fusion.67
  449.5 1.4 copy.78
  451.0 3.5 convolution_convert_fusion
  454.5 50.8 %reduce-scatter.2.cloned.1.call-done = bf16[512,768]{1,0:T(8,128)(2,1)} async-done(((bf16[512,3072]{1,0:T(8,128)(2,1)}), bf16[512,768]{1,0:T(8,128)(2,1)}) %reduce-scatter.2.cloned.1.call-update) | async-done | bytes 786448 | tf_op jit(solution)/shard_map/reduce_scatter | solution.py:129
  (333 shorter events, 116.5 us)
Async XLA Ops:
  6.5 444.4 %copy-start = (bf16[384,3072]{1,0:T(8,128)(2,1)S(1)}, bf16[384,3072]{1,0:T(8,128)(2,1)}, u32[]{:S(2)}) copy-start(bf16[384,3072]{1,0:T(8,128)(2,1)} %param.11) | copy-start | bytes 7077892
  6.5 6.3 %copy-start.21 = (s32[12]{0:T(128)S(1)}, s32[12]{0:T(128)}, u32[]{:S(2)}) copy-start(s32[12]{0:T(128)} %param.10) | copy-start | bytes 148
  6.5 498.7 %reduce-scatter.2.cloned.1.call-start = ((), (), s32[]{:S(2)}) async-start(), calls=%async_computation.1 | async-start | bytes 3932160 | tf_op jit(solution)/shard_map/reduce_scatter | solution.py:129
  12.8 10.8 %copy-start.13 = (f32[512,3,28]{0,2,1:T(8,128)S(1)}, f32[512,3,28]{0,2,1:T(8,128)}, u32[]{:S(2)}) copy-start(f32[512,3,28]{0,2,1:T(8,128)} %get-tuple-element.322) | copy-start | bytes 516100
  13.1 42.8 %copy-start.18 = (s32[512]{0:T(512)}, s32[512]{0:T(512)S(1)}, u32[]{:S(2)}) copy-start(s32[512]{0:T(512)S(1)} %get-tuple-element.423) | copy-start | bytes 6148
  17.0 9.0 %copy-start.19 = (f32[512]{0:T(512)S(1)}, f32[512]{0:T(512)}, u32[]{:S(2)}) copy-start(f32[512]{0:T(512)} %get-tuple-element.342) | copy-start | bytes 6148
  17.0 9.0 %copy-start.20 = (f32[8]{0:T(128)S(1)}, f32[8]{0:T(128)}, u32[]{:S(2)}) copy-start(f32[8]{0:T(128)} %multiply_exponential_fusion.1) | copy-start | bytes 100
  17.1 10.9 %copy-start.15 = (f32[512,3,8]{0,2,1:T(8,128)S(1)}, f32[512,3,8]{0,2,1:T(8,128)}, u32[]{:S(2)}) copy-start(f32[512,3,8]{0,2,1:T(8,128)} %get-tuple-element.330) | copy-start | bytes 147460
  19.2 9.0 %copy-start.14 = (f32[512,3,8]{0,2,1:T(8,128)S(1)}, f32[512,3,8]{0,2,1:T(8,128)}, u32[]{:S(2)}) copy-start(f32[512,3,8]{0,2,1:T(8,128)} %get-tuple-element.331) | copy-start | bytes 147460
  21.3 8.1 %copy-start.17 = (f32[512,3,8]{0,2,1:T(8,128)S(1)}, f32[512,3,8]{0,2,1:T(8,128)}, u32[]{:S(2)}) copy-start(f32[512,3,8]{0,2,1:T(8,128)} %get-tuple-element.324) | copy-start | bytes 147460
  22.5 8.0 %copy-start.16 = (f32[512,3,8]{0,2,1:T(8,128)S(1)}, f32[512,3,8]{0,2,1:T(8,128)}, u32[]{:S(2)}) copy-start(f32[512,3,8]{0,2,1:T(8,128)} %get-tuple-element.325) | copy-start | bytes 147460
  31.7 6.0 %copy-start.4 = (f32[512,3,28]{2,0,1:T(8,128)S(1)}, f32[512,3,28]{2,0,1:T(8,128)}, u32[]{:S(2)}) copy-start(f32[512,3,28]{2,0,1:T(8,128)} %copy.87) | copy-start | bytes 516100
  31.7 6.0 %copy-start.5 = (f32[512,3,28]{2,0,1:T(8,128)S(1)}, f32[512,3,28]{2,0,1:T(8,128)}, u32[]{:S(2)}) copy-start(f32[512,3,28]{2,0,1:T(8,128)} %copy.88) | copy-start | bytes 516100
  31.7 6.0 %copy-start.6 = (f32[512,3,28]{2,0,1:T(8,128)S(1)}, f32[512,3,28]{2,0,1:T(8,128)}, u32[]{:S(2)}) copy-start(f32[512,3,28]{2,0,1:T(8,128)} %copy.93) | copy-start | bytes 516100
  31.7 6.0 %copy-start.7 = (f32[512,3,28]{2,0,1:T(8,128)S(1)}, f32[512,3,28]{2,0,1:T(8,128)}, u32[]{:S(2)}) copy-start(f32[512,3,28]{2,0,1:T(8,128)} %copy.94) | copy-start | bytes 516100
  37.6 1.5 copy-start.1
  37.6 1.8 copy-start.2
  37.6 2.2 copy-start.3
  37.6 2.2 copy-start.9
  37.6 2.3 copy-start.10
  41.3 11.7 %copy-start.8 = (bf16[512,3,28]{2,0,1:T(8,128)(2,1)S(1)}, bf16[512,3,28]{2,0,1:T(8,128)(2,1)}, u32[]{:S(2)}) copy-start(bf16[512,3,28]{2,0,1:T(8,128)(2,1)} %get-tuple-element.300) | copy-start | bytes 258052
  46.6 22.9 %collective-permute-start.1 = (bf16[2,512,384]{1,2,0:T(8,128)(2,1)}, bf16[2,512,384]{1,2,0:T(8,128)(2,1)}, u32[]{:S(2)}, u32[]{:S(2)}) collective-permute-start(bf16[2,512,384]{1,2,0:T(8,128)(2,1)} %pad_maximum_fusion), channel_id=1, source_target_pairs={{0,224},{4,228},{8,232},{12,236},{16,240},{20,244},{24,248},{28,25... | collective-permute-start | bytes 2359304 | tf_op jit(solution)/shard_map/ppermute | solution.py:22
  74.6 24.8 %collective-permute-start = (bf16[2,512,384]{1,2,0:T(8,128)(2,1)}, bf16[2,512,384]{1,2,0:T(8,128)(2,1)S(1)}, u32[]{:S(2)}, u32[]{:S(2)}) collective-permute-start(bf16[2,512,384]{1,2,0:T(8,128)(2,1)} %get-tuple-element.433), channel_id=1, source_target_pairs={{0,4},{4,8},{8,12},{12,16},{16,20},{20,24},{24,28},{28,32},{32,36}... | collective-permute-start | bytes 2359304 | tf_op jit(solution)/shard_map/while/body/eval_jaxpr/ppermute | solution.py:22
  99.4 1.7 copy-start.11
  102.5 1.1 copy-start.12
  103.7 22.8 %collective-permute-start = (bf16[2,512,384]{1,2,0:T(8,128)(2,1)}, bf16[2,512,384]{1,2,0:T(8,128)(2,1)S(1)}, u32[]{:S(2)}, u32[]{:S(2)}) collective-permute-start(bf16[2,512,384]{1,2,0:T(8,128)(2,1)} %get-tuple-element.433), channel_id=1, source_target_pairs={{0,4},{4,8},{8,12},{12,16},{16,20},{20,24},{24,28},{28,32},{32,36}... | collective-permute-start | bytes 2359304 | tf_op jit(solution)/shard_map/while/body/eval_jaxpr/ppermute | solution.py:22
  126.5 1.7 copy-start.11
  130.8 21.9 %collective-permute-start = (bf16[2,512,384]{1,2,0:T(8,128)(2,1)}, bf16[2,512,384]{1,2,0:T(8,128)(2,1)S(1)}, u32[]{:S(2)}, u32[]{:S(2)}) collective-permute-start(bf16[2,512,384]{1,2,0:T(8,128)(2,1)} %get-tuple-element.433), channel_id=1, source_target_pairs={{0,4},{4,8},{8,12},{12,16},{16,20},{20,24},{24,28},{28,32},{32,36}... | collective-permute-start | bytes 2359304 | tf_op jit(solution)/shard_map/while/body/eval_jaxpr/ppermute | solution.py:22
  152.7 1.7 copy-start.11
  157.0 20.9 %collective-permute-start = (bf16[2,512,384]{1,2,0:T(8,128)(2,1)}, bf16[2,512,384]{1,2,0:T(8,128)(2,1)S(1)}, u32[]{:S(2)}, u32[]{:S(2)}) collective-permute-start(bf16[2,512,384]{1,2,0:T(8,128)(2,1)} %get-tuple-element.433), channel_id=1, source_target_pairs={{0,4},{4,8},{8,12},{12,16},{16,20},{20,24},{24,28},{28,32},{32,36}... | collective-permute-start | bytes 2359304 | tf_op jit(solution)/shard_map/while/body/eval_jaxpr/ppermute | solution.py:22
  178.0 1.7 copy-start.11
  182.3 20.0 %collective-permute-start = (bf16[2,512,384]{1,2,0:T(8,128)(2,1)}, bf16[2,512,384]{1,2,0:T(8,128)(2,1)S(1)}, u32[]{:S(2)}, u32[]{:S(2)}) collective-permute-start(bf16[2,512,384]{1,2,0:T(8,128)(2,1)} %get-tuple-element.433), channel_id=1, source_target_pairs={{0,4},{4,8},{8,12},{12,16},{16,20},{20,24},{24,28},{28,32},{32,36}... | collective-permute-start | bytes 2359304 | tf_op jit(solution)/shard_map/while/body/eval_jaxpr/ppermute | solution.py:22
  202.4 1.7 copy-start.11
  206.7 19.1 %collective-permute-start = (bf16[2,512,384]{1,2,0:T(8,128)(2,1)}, bf16[2,512,384]{1,2,0:T(8,128)(2,1)S(1)}, u32[]{:S(2)}, u32[]{:S(2)}) collective-permute-start(bf16[2,512,384]{1,2,0:T(8,128)(2,1)} %get-tuple-element.433), channel_id=1, source_target_pairs={{0,4},{4,8},{8,12},{12,16},{16,20},{20,24},{24,28},{28,32},{32,36}... | collective-permute-start | bytes 2359304 | tf_op jit(solution)/shard_map/while/body/eval_jaxpr/ppermute | solution.py:22
  225.8 1.7 copy-start.11
  229.0 1.1 copy-start.12
  230.1 18.2 %collective-permute-start = (bf16[2,512,384]{1,2,0:T(8,128)(2,1)}, bf16[2,512,384]{1,2,0:T(8,128)(2,1)S(1)}, u32[]{:S(2)}, u32[]{:S(2)}) collective-permute-start(bf16[2,512,384]{1,2,0:T(8,128)(2,1)} %get-tuple-element.433), channel_id=1, source_target_pairs={{0,4},{4,8},{8,12},{12,16},{16,20},{20,24},{24,28},{28,32},{32,36}... | collective-permute-start | bytes 2359304 | tf_op jit(solution)/shard_map/while/body/eval_jaxpr/ppermute | solution.py:22
  248.3 1.7 copy-start.11
  251.5 1.1 copy-start.12
  252.6 17.2 %collective-permute-start = (bf16[2,512,384]{1,2,0:T(8,128)(2,1)}, bf16[2,512,384]{1,2,0:T(8,128)(2,1)S(1)}, u32[]{:S(2)}, u32[]{:S(2)}) collective-permute-start(bf16[2,512,384]{1,2,0:T(8,128)(2,1)} %get-tuple-element.433), channel_id=1, source_target_pairs={{0,4},{4,8},{8,12},{12,16},{16,20},{20,24},{24,28},{28,32},{32,36}... | collective-permute-start | bytes 2359304 | tf_op jit(solution)/shard_map/while/body/eval_jaxpr/ppermute | solution.py:22
  269.9 1.7 copy-start.11
  273.1 1.1 copy-start.12
  274.2 16.8 %collective-permute-start = (bf16[2,512,384]{1,2,0:T(8,128)(2,1)}, bf16[2,512,384]{1,2,0:T(8,128)(2,1)S(1)}, u32[]{:S(2)}, u32[]{:S(2)}) collective-permute-start(bf16[2,512,384]{1,2,0:T(8,128)(2,1)} %get-tuple-element.433), channel_id=1, source_target_pairs={{0,4},{4,8},{8,12},{12,16},{16,20},{20,24},{24,28},{28,32},{32,36}... | collective-permute-start | bytes 2359304 | tf_op jit(solution)/shard_map/while/body/eval_jaxpr/ppermute | solution.py:22
  291.1 1.7 copy-start.11
  294.2 1.1 copy-start.12
  295.4 16.8 %collective-permute-start = (bf16[2,512,384]{1,2,0:T(8,128)(2,1)}, bf16[2,512,384]{1,2,0:T(8,128)(2,1)S(1)}, u32[]{:S(2)}, u32[]{:S(2)}) collective-permute-start(bf16[2,512,384]{1,2,0:T(8,128)(2,1)} %get-tuple-element.433), channel_id=1, source_target_pairs={{0,4},{4,8},{8,12},{12,16},{16,20},{20,24},{24,28},{28,32},{32,36}... | collective-permute-start | bytes 2359304 | tf_op jit(solution)/shard_map/while/body/eval_jaxpr/ppermute | solution.py:22
  312.2 1.7 copy-start.11
  315.3 1.1 copy-start.12
  316.5 16.8 %collective-permute-start = (bf16[2,512,384]{1,2,0:T(8,128)(2,1)}, bf16[2,512,384]{1,2,0:T(8,128)(2,1)S(1)}, u32[]{:S(2)}, u32[]{:S(2)}) collective-permute-start(bf16[2,512,384]{1,2,0:T(8,128)(2,1)} %get-tuple-element.433), channel_id=1, source_target_pairs={{0,4},{4,8},{8,12},{12,16},{16,20},{20,24},{24,28},{28,32},{32,36}... | collective-permute-start | bytes 2359304 | tf_op jit(solution)/shard_map/while/body/eval_jaxpr/ppermute | solution.py:22
  333.3 1.7 copy-start.11
  336.5 1.1 copy-start.12
  337.6 16.8 %collective-permute-start = (bf16[2,512,384]{1,2,0:T(8,128)(2,1)}, bf16[2,512,384]{1,2,0:T(8,128)(2,1)S(1)}, u32[]{:S(2)}, u32[]{:S(2)}) collective-permute-start(bf16[2,512,384]{1,2,0:T(8,128)(2,1)} %get-tuple-element.433), channel_id=1, source_target_pairs={{0,4},{4,8},{8,12},{12,16},{16,20},{20,24},{24,28},{28,32},{32,36}... | collective-permute-start | bytes 2359304 | tf_op jit(solution)/shard_map/while/body/eval_jaxpr/ppermute | solution.py:22
  354.4 1.7 copy-start.11
  357.6 1.1 copy-start.12
  358.7 16.8 %collective-permute-start = (bf16[2,512,384]{1,2,0:T(8,128)(2,1)}, bf16[2,512,384]{1,2,0:T(8,128)(2,1)S(1)}, u32[]{:S(2)}, u32[]{:S(2)}) collective-permute-start(bf16[2,512,384]{1,2,0:T(8,128)(2,1)} %get-tuple-element.433), channel_id=1, source_target_pairs={{0,4},{4,8},{8,12},{12,16},{16,20},{20,24},{24,28},{28,32},{32,36}... | collective-permute-start | bytes 2359304 | tf_op jit(solution)/shard_map/while/body/eval_jaxpr/ppermute | solution.py:22
  375.6 1.7 copy-start.11
  378.7 1.1 copy-start.12
  379.9 17.8 %collective-permute-start = (bf16[2,512,384]{1,2,0:T(8,128)(2,1)}, bf16[2,512,384]{1,2,0:T(8,128)(2,1)S(1)}, u32[]{:S(2)}, u32[]{:S(2)}) collective-permute-start(bf16[2,512,384]{1,2,0:T(8,128)(2,1)} %get-tuple-element.433), channel_id=1, source_target_pairs={{0,4},{4,8},{8,12},{12,16},{16,20},{20,24},{24,28},{28,32},{32,36}... | collective-permute-start | bytes 2359304 | tf_op jit(solution)/shard_map/while/body/eval_jaxpr/ppermute | solution.py:22
  397.7 1.7 copy-start.11
  402.0 18.8 %collective-permute-start = (bf16[2,512,384]{1,2,0:T(8,128)(2,1)}, bf16[2,512,384]{1,2,0:T(8,128)(2,1)S(1)}, u32[]{:S(2)}, u32[]{:S(2)}) collective-permute-start(bf16[2,512,384]{1,2,0:T(8,128)(2,1)} %get-tuple-element.433), channel_id=1, source_target_pairs={{0,4},{4,8},{8,12},{12,16},{16,20},{20,24},{24,28},{28,32},{32,36}... | collective-permute-start | bytes 2359304 | tf_op jit(solution)/shard_map/while/body/eval_jaxpr/ppermute | solution.py:22
  420.9 1.7 copy-start.11
  425.2 19.9 %collective-permute-start = (bf16[2,512,384]{1,2,0:T(8,128)(2,1)}, bf16[2,512,384]{1,2,0:T(8,128)(2,1)S(1)}, u32[]{:S(2)}, u32[]{:S(2)}) collective-permute-start(bf16[2,512,384]{1,2,0:T(8,128)(2,1)} %get-tuple-element.433), channel_id=1, source_target_pairs={{0,4},{4,8},{8,12},{12,16},{16,20},{20,24},{24,28},{28,32},{32,36}... | collective-permute-start | bytes 2359304 | tf_op jit(solution)/shard_map/while/body/eval_jaxpr/ppermute | solution.py:22
  445.2 1.7 copy-start.11
  448.3 1.1 copy-start.12
  (6 other events, 6.8 us)
Sparse Core Ops, SparseCore 0:
  454.6 50.6 reduce-scatter.1
where the time goes:
time: 513 us; the launch traced here: 512 us
  waiting for transfers between devices  301 us (59%)
  other arithmetic  93 us (18%)
  local copies, waits for them, and re-layouts  52.7 us (10%)
  matrix products  42.7 us (8%)
  between operations  13.6 us (3%)
  starting transfers between devices  7.65 us (1%)
    ppermute x17, waiting for transfers between devices, from_behind(): lax.ppermute(value, axis, [(i, (i + by) % count) for i in range(count)])  250 us
    reduce_scatter x1, waiting for transfers between devices, per_device(): lax.psum_scatter(head_terms.astype(jnp.bfloat16), 'tp', scatter_dimension...  50.8 us
    another operation x20, other arithmetic  28.1 us
    dot_general x17, matrix products, absorb(): jnp.einsum('hts,shd->htd', expo.astype(jnp.bfloat16), value_heads, prefer...  25.4 us
    unnamed x55, local copies, waits for them, and re-layouts  20.4 us
    mul x17, other arithmetic, clip_layout(): clip_sizes = frame_counts * (PH * PW)  19.1 us
    while x96, local copies, waits for them, and re-layouts  18.3 us
    eq x17, other arithmetic, absorb(): allowed = (query_clip[:, None] == key_clip[None, :]) & key_valid[None, :]  14.1 us
  transfers between devices with their start and end apart: 18, of which 18 were waited for; matrix products, arithmetic and copies ran while one was open for 14% of the time, Pallas kernels for 0%

commit v1 on v0

v1 whole, which is shorter than its diff:
```python
import math

import jax
import jax.numpy as jnp
import numpy as np
from jax import lax
from jax.experimental import pallas as pl
from jax.experimental.pallas import tpu as pltpu
from jax.sharding import Mesh
from jax.sharding import PartitionSpec as P

RT = 16
RH = 56
RW = 56
PH = 16
PW = 16
FRAME = PH * PW
HEAD_DIM = 128
CLIPS = 12
TOK = 512
SLOTS = 16
ROPE_BASE = 256.0
NEG = -1e30
EXP_SCALE = HEAD_DIM ** (-0.5) * math.log2(math.e)

GROUPS = ((0, 1, 2),)
STEPS = (0, -1, 1, 2)


def rope_tables():
    freq = np.zeros(HEAD_DIM)
    swap = np.zeros((HEAD_DIM, HEAD_DIM), np.float32)
    sign = np.zeros(HEAD_DIM)
    base = 0
    bounds = []
    for width in (RT, RH, RW):
        half = width // 2
        f = np.exp(-(2.0 * np.arange(half) / width) * math.log(ROPE_BASE))
        freq[base : base + half] = f
        freq[base + half : base + width] = f
        sign[base : base + half] = -1.0
        sign[base + half : base + width] = 1.0
        for j in range(half):
            swap[base + half + j, base + j] = 1.0
            swap[base + j, base + half + j] = 1.0
        bounds.append((base, base + width))
        base += width
    token = np.arange(FRAME)
    angle = np.zeros((FRAME, HEAD_DIM))
    (t0, t1), (h0, h1), (w0, w1) = bounds
    angle[:, h0:h1] = (token // PW)[:, None] * freq[None, h0:h1]
    angle[:, w0:w1] = (token % PW)[:, None] * freq[None, w0:w1]
    angle_t = np.zeros((SLOTS, HEAD_DIM))
    angle_t[:, t0:t1] = np.arange(SLOTS)[:, None] * freq[None, t0:t1]
    space = np.stack([np.cos(angle), np.sin(angle) * sign]).astype(np.float32)
    time = np.stack([np.cos(angle_t), np.sin(angle_t) * sign]).astype(np.float32)
    return space, time, swap


def clip_bounds(meta_ref, frame):
    start = jnp.int32(0)
    end = jnp.int32(0)
    total = jnp.int32(0)
    for c in range(CLIPS):
        here = frame >= total
        total = total + meta_ref[c]
        start = jnp.where(here, total - meta_ref[c], start)
        end = jnp.where(here, total, end)
    return start, end


def dot_nt(a, b):
    return lax.dot_general(a, b, (((1,), (1,)), ((), ())), preferred_element_type=jnp.float32)


def dot_nn(a, b):
    return lax.dot_general(a, b, (((1,), (0,)), ((), ())), preferred_element_type=jnp.float32)


def prepare_kernel(meta_ref, q_ref, k_ref, v_ref, space_ref, time_ref, swap_ref, *outs):
    swap = swap_ref[0]
    eye = swap_ref[1]
    first = meta_ref[CLIPS] * SLOTS + meta_ref[CLIPS + 1] * 8 + meta_ref[CLIPS + 2] * 2
    lane = lax.broadcasted_iota(jnp.int32, (FRAME, HEAD_DIM), 1)
    for e in range(2):
        start, _ = clip_bounds(meta_ref, first + e)
        t = first + e - start
        tok = slice(FRAME * e, FRAME * (e + 1))
        cos = jnp.where(lane < RT, time_ref[0, pl.ds(t, 1), :], space_ref[0])
        sin = jnp.where(lane < RT, time_ref[1, pl.ds(t, 1), :], space_ref[1])
        cos_t = cos.T
        sin_t = sin.T
        for g, heads in enumerate(GROUPS):
            q_out, kv_out = outs[2 * g], outs[2 * g + 1]
            n = len(heads)
            for a, h in enumerate(heads):
                col = slice(HEAD_DIM * h, HEAD_DIM * (h + 1))
                row = slice(HEAD_DIM * a, HEAD_DIM * (a + 1))
                vrow = slice(HEAD_DIM * (n + a), HEAD_DIM * (n + a + 1))
                k = k_ref[tok, col]
                rot = (k.astype(jnp.float32) * cos + dot_nn(k, swap) * sin).astype(jnp.bfloat16)
                kv_out[row, FRAME * e : FRAME * e + 128] = rot[:128]
                kv_out[row, FRAME * e + 128 : FRAME * e + 256] = rot[128:]
                kv_out[vrow, tok] = dot_nt(eye, v_ref[tok, col]).astype(jnp.bfloat16)
                q = q_ref[tok, col]
                rot = dot_nt(eye, q) * cos_t + dot_nt(swap, q) * sin_t
                q_out[row, tok] = rot.astype(jnp.bfloat16)


def split3(value):
    hi = value.astype(jnp.bfloat16)
    rest = value - hi.astype(jnp.float32)
    mid = rest.astype(jnp.bfloat16)
    low = (rest - mid.astype(jnp.float32)).astype(jnp.bfloat16)
    return [hi, mid, low]


def attend_kernel(n, meta_ref, q0, q1, q2, q3, own, ypair, zm, zp, third, o0, o1, o2, o3, kv, sem):
    blocks = (zm, own, zp, third, ypair)
    copies = [pltpu.make_async_copy(b, kv.at[i], sem.at[i]) for i, b in enumerate(blocks)]
    for c in copies:
        c.start()
    z, yh, x = meta_ref[CLIPS], meta_ref[CLIPS + 1], meta_ref[CLIPS + 2]
    plane = z * SLOTS
    for c in copies:
        c.wait()
    for r, (q_ref, o_ref) in enumerate(zip((q0, q1, q2, q3), (o0, o1, o2, o3))):
        xq = lax.rem(x + STEPS[r] + 4, 4)
        stats = [[None, None] for _ in range(n)]
        for e in range(2):
            frame = plane + yh * 8 + xq * 2 + e
            start, end = clip_bounds(meta_ref, frame)
            places = []
            for sl in range(4):
                row = yh if sl < 2 else 1 - yh
                mid = plane + row * 8 + x * 2 + sl % 2
                before = mid - SLOTS >= start
                inside = (mid >= start) & (mid < end)
                after = mid + SLOTS < end
                if sl < 2:
                    src = jnp.where(inside, 1, jnp.where(before, 0, 2))
                else:
                    src = jnp.where(inside, 4, 3)
                valid = before | inside | after
                places.append((src, valid))
            some = places[0][1] | places[1][1] | places[2][1] | places[3][1]
            tok = slice(FRAME * e, FRAME * (e + 1))
            for a in range(n):
                row = slice(HEAD_DIM * a, HEAD_DIM * (a + 1))
                vrow = slice(HEAD_DIM * (n + a), HEAD_DIM * (n + a + 1))
                qt = q_ref[row, tok]
                scores = []
                top = None
                for sl in range(4):
                    src, valid = places[sl]
                    bias = jnp.where(valid, 0.0, NEG)
                    for half in range(2):
                        lo = FRAME * (sl % 2) + 128 * half
                        s = dot_nn(kv[src, row, lo : lo + 128], qt)
                        scores.append((s, bias))
                        peak = jnp.max(s, axis=0, keepdims=True) * EXP_SCALE + bias
                        top = peak if top is None else jnp.maximum(top, peak)
                acc = None
                total = None
                for sl in range(4):
                    src, _ = places[sl]
                    parts = []
                    for half in range(2):
                        s, bias = scores[2 * sl + half]
                        shift = jnp.where(some, bias - top, NEG)
                        p = jnp.exp2(s * EXP_SCALE + shift)
                        add = jnp.sum(p, axis=0, keepdims=True)
                        total = add if total is None else total + add
                        parts.append(p.astype(jnp.bfloat16))
                    weights = jnp.concatenate(parts, axis=0)
                    lo = FRAME * (sl % 2)
                    term = dot_nn(kv[src, vrow, lo : lo + FRAME], weights)
                    acc = term if acc is None else acc + term
                total = jnp.maximum(total, 1e-30)
                o_ref[row, tok] = (acc * (1.0 / total)).astype(jnp.bfloat16)
                stats[a][e] = jnp.where(some, top + jnp.log2(total), NEG)
        rows = []
        for a in range(n):
            rows += split3(jnp.concatenate(stats[a], axis=1))
        rows.append(jnp.zeros((16 - len(rows), TOK), jnp.bfloat16))
        o_ref[HEAD_DIM * n : HEAD_DIM * n + 16, :] = jnp.concatenate(rows, axis=0)


def merge_kernel(n, p0, p1, p2, p3, out):
    parts = (p0, p1, p2, p3)
    for a in range(n):
        row = slice(HEAD_DIM * a, HEAD_DIM * (a + 1))
        levels = []
        for p in parts:
            tail = p[HEAD_DIM * n : HEAD_DIM * n + 16, :].astype(jnp.float32)
            levels.append(tail[3 * a : 3 * a + 1] + tail[3 * a + 1 : 3 * a + 2] + tail[3 * a + 2 : 3 * a + 3])
        top = jnp.maximum(jnp.maximum(levels[0], levels[1]), jnp.maximum(levels[2], levels[3]))
        shares = [jnp.exp2(v - top) for v in levels]
        inv = 1.0 / (shares[0] + shares[1] + shares[2] + shares[3])
        acc = None
        for p, s in zip(parts, shares):
            term = p[row, :].astype(jnp.float32) * (s * inv)
            acc = term if acc is None else acc + term
        out[:, row] = acc.T.astype(jnp.bfloat16)


def project_kernel(count, *refs):
    sides, weights, out = refs[:count], refs[count : 2 * count], refs[2 * count]
    acc = None
    for s, w in zip(sides, weights):
        term = dot_nn(s[...], w[...])
        acc = term if acc is None else acc + term
    out[...] = acc.astype(jnp.bfloat16)


VMEM = pl.BlockSpec(memory_space=pltpu.VMEM)
SMEM = pl.BlockSpec(memory_space=pltpu.SMEM)
ANY = pl.BlockSpec(memory_space=pl.ANY)
PARAMS = pltpu.CompilerParams(vmem_limit_bytes=48 * 1024 * 1024)


def cost(flops, size, trans=0):
    return pl.CostEstimate(flops=flops, bytes_accessed=size, transcendentals=trans)


def shift(value, axis, by):
    count = lax.axis_size(axis)
    return lax.ppermute(value, axis, [(i, (i + by) % count) for i in range(count)])


def flip(value, axis):
    return lax.ppermute(value, axis, [(0, 1), (1, 0)])


def per_device(query_rows, key_rows, value_rows, frame_counts, out_weight):
    place = jnp.stack([lax.axis_index("z"), lax.axis_index("yh"), lax.axis_index("x"), 0])
    meta = jnp.concatenate([frame_counts, place.astype(jnp.int32)])
    space, time, swap = rope_tables()
    mats = jnp.asarray(np.stack([swap, np.eye(HEAD_DIM, dtype=np.float32)]), jnp.bfloat16)

    shapes = []
    for heads in GROUPS:
        n = len(heads)
        shapes.append(jax.ShapeDtypeStruct((n * HEAD_DIM, TOK), jnp.bfloat16))
        shapes.append(jax.ShapeDtypeStruct((2 * n * HEAD_DIM, TOK), jnp.bfloat16))
    prepared = pl.pallas_call(
        prepare_kernel,
        out_shape=shapes,
        in_specs=[SMEM] + [VMEM] * 6,
        out_specs=[VMEM] * len(shapes),
        compiler_params=PARAMS,
        cost_estimate=cost(200_000_000, 3_000_000),
        name="prepare",
    )(meta, query_rows, key_rows, value_rows, jnp.asarray(space), jnp.asarray(time), mats)

    arrived = []
    zy = [((zi * 2), ((zi + 1) % 8) * 2) for zi in range(8)]
    zy += [((zi * 2 + 1), ((zi - 1) % 8) * 2 + 1) for zi in range(8)]
    for g, heads in enumerate(GROUPS):
        q, kv = prepared[2 * g], prepared[2 * g + 1]
        ypair = flip(kv, "yh")
        zm = shift(kv, "z", 1)
        zp = shift(kv, "z", -1)
        qs = [q, shift(q, "x", 1), shift(q, "x", -1), shift(q, "x", 2)]
        third = lax.ppermute(ypair, ("z", "yh"), zy)
        arrived.append((qs, [kv, ypair, zm, zp, third]))

    tp = lax.axis_index("yl") * 2 + lax.axis_index("core")
    cols = out_weight.shape[1] // 4

    def mine(j):
        return lax.dynamic_slice_in_dim(out_weight, j * cols, cols, 1)

    w_own = mine(tp)
    w_core = flip(mine(tp ^ 1), "core")
    w_yl = flip(mine(tp ^ 2), "yl")
    w_far = lax.ppermute(mine(tp ^ 3), ("yh", "yl", "core"), [(i, 7 - i) for i in range(8)])

    sides = []
    for g, heads in enumerate(GROUPS):
        n = len(heads)
        qs, kvs = arrived[g]
        out = jax.ShapeDtypeStruct((n * HEAD_DIM + 16, TOK), jnp.bfloat16)
        partial = pl.pallas_call(
            lambda *refs, n=n: attend_kernel(n, *refs),
            out_shape=[out] * 4,
            in_specs=[SMEM] + [VMEM] * 4 + [ANY] * 5,
            out_specs=[VMEM] * 4,
            scratch_shapes=[
                pltpu.VMEM((5, 2 * n * HEAD_DIM, TOK), jnp.bfloat16),
                pltpu.SemaphoreType.DMA((5,)),
            ],
            compiler_params=PARAMS,
            cost_estimate=cost(n * 3_200_000_000, n * 2_000_000, n * 2_000_000),
            name="attend",
        )(meta, *qs, *kvs)
        back = [partial[0]] + [shift(partial[r], "x", STEPS[r]) for r in (1, 2, 3)]
        att = pl.pallas_call(
            lambda *refs, n=n: merge_kernel(n, *refs),
            out_shape=jax.ShapeDtypeStruct((TOK, n * HEAD_DIM), jnp.bfloat16),
            in_specs=[VMEM] * 4,
            out_specs=VMEM,
            compiler_params=PARAMS,
            cost_estimate=cost(n * 10_000_000, n * 700_000),
            name="merge",
        )(*back)
        att_yl = flip(att, "yl")
        att_core = flip(att, "core")
        att_far = flip(att_yl, "core")
        sides.append((att, att_core, att_yl, att_far))

    terms, weights = [], []
    for g, heads in enumerate(GROUPS):
        rows = slice(heads[0] * HEAD_DIM, (heads[-1] + 1) * HEAD_DIM)
        for s, w in zip(sides[g], (w_own, w_core, w_yl, w_far)):
            terms.append(s)
            weights.append(w if len(GROUPS) == 1 else w[rows])
    tile = 256
    return pl.pallas_call(
        lambda *refs: project_kernel(len(terms), *refs),
        grid=(TOK // tile,),
        out_shape=jax.ShapeDtypeStruct((TOK, cols), jnp.bfloat16),
        in_specs=[pl.BlockSpec((tile, s.shape[1]), lambda i: (i, 0)) for s in terms]
        + [pl.BlockSpec(w.shape, lambda i: (0, 0)) for w in weights],
        out_specs=pl.BlockSpec((tile, cols), lambda i: (i, 0)),
        compiler_params=PARAMS,
        cost_estimate=cost(1_200_000_000, 4_700_000),
        name="project",
    )(*terms, *weights)


def solution(mesh):
    fine = Mesh(mesh.devices.reshape(8, 2, 4, 2, 2), ("z", "yh", "x", "yl", "core"))
    seq, tp = ("z", "yh", "x"), ("yl", "core")
    return jax.shard_map(
        per_device,
        mesh=fine,
        in_specs=(P(seq, tp), P(seq, tp), P(seq, tp), P(), P(tp, None)),
        out_specs=P(seq, tp),
        check_vma=False,
    )
```

time: 513 us -> 114 us (0.22)
  waiting for transfers between devices: 301 us -> 52.6 us
  other arithmetic: 93 us -> 0 us
  local copies, waits for them, and re-layouts: 52.7 us -> 7.38 us
  matrix products: 42.7 us -> 0 us
  starting transfers between devices: 7.65 us -> 34.5 us
  Pallas kernels: 0 us -> 18.7 us
  between operations: 13.6 us -> 0.09 us
    ppermute x17 -> x16, waiting for transfers between devices: 250 us -> 52.6 us  [the longest x8 26.1 us: shift(): lax.ppermute(value, axis, [(i, (i + by) % count) for i in range(count)])]
    reduce_scatter x1 -> x0, waiting for transfers between devices: 50.8 us -> none  [per_device(): lax.psum_scatter(head_terms.astype(jnp.bfloat16), 'tp', scatter_dimension...]
    dot_general x35 -> x0, matrix products: 42.7 us -> none  [the longest x17 25.4 us: absorb(): jnp.einsum('hts,shd->htd', expo.astype(jnp.bfloat16), value_heads, prefer...]
    another operation x23 -> x0, other arithmetic: 29.1 us -> none
    ppermute x17 -> x16, starting transfers between devices: 7.65 us -> 34.5 us  [the longest x6 14.2 us: flip(): return lax.ppermute(value, axis, [(0, 1), (1, 0)])]
    reduce_sum x34 -> x0, other arithmetic: 25.6 us -> none  [the longest x17 13.7 us: absorb(): run_total = run_total * rescale + jnp.sum(expo, axis=2)]
    while x97 -> x0, local copies, waits for them, and re-layouts: 19.7 us -> none
    mul x17 -> x0, other arithmetic: 19.1 us -> none  [clip_layout(): clip_sizes = frame_counts * (PH * PW)]
  transfers between devices with their start and end apart: 18 -> 16, of which waited for: 18 -> 9; matrix products, arithmetic and copies ran while one was open for 14% -> 0% of each run, Pallas kernels for 0% -> 0%
where the time goes in v1:
time: 114 us; the launch traced here: 113 us
  waiting for transfers between devices  52.6 us (46%)
  starting transfers between devices  34.5 us (30%)
  Pallas kernels  18.7 us (16%)
  local copies, waits for them, and re-layouts  7.38 us (6%)
    ppermute x8, waiting for transfers between devices, shift(): lax.ppermute(value, axis, [(i, (i + by) % count) for i in range(count)])  26.1 us
    ppermute x6, waiting for transfers between devices, flip(): return lax.ppermute(value, axis, [(0, 1), (1, 0)])  15.4 us
    pallas_call x1, Pallas kernels, per_device(): pl.pallas_call(lambda *refs, n=n: attend_kernel(n, *refs), out_shape=[out...  14.4 us
    ppermute x6, starting transfers between devices, flip(): return lax.ppermute(value, axis, [(0, 1), (1, 0)])  14.2 us
    ppermute x8, starting transfers between devices, shift(): lax.ppermute(value, axis, [(i, (i + by) % count) for i in range(count)])  13.8 us
    ppermute x1, waiting for transfers between devices, per_device(): third = lax.ppermute(ypair, ('z', 'yh'), zy)  9.6 us
    unnamed x18, local copies, waits for them, and re-layouts  6.38 us
    ppermute x1, starting transfers between devices, per_device(): lax.ppermute(mine(tp ^ 3), ('yh', 'yl', 'core'), [(i, 7 - i) for i in ran...  4.13 us
  transfers between devices with their start and end apart: 16, of which 9 were waited for; matrix products, arithmetic and copies ran while one was open for 0% of the time, Pallas kernels for 0%

profile of v1, /device:TPU:1, one launch (start us, length us, event | category | flops | bytes accessed | tf_op | source)
XLA Modules:
  0.0 113.3 jit_solution(4880866178623675764)
XLA Ops:
  0.0 0.7 concatenate.3.meta_ref.refs_0_
  0.7 0.0 copy-start
  0.7 1.0 copy-done
  1.7 0.0 copy-start.1
  1.7 1.0 copy-done.1
  2.7 0.0 copy-start.2
  2.7 1.0 copy-done.2
  3.7 0.0 copy-start.3
  3.7 0.9 copy-done.3
  4.7 0.0 copy-start.4
  4.7 0.8 copy-done.4
  5.5 0.0 copy-start.5
  5.5 0.7 copy-done.5
  6.2 1.2 %prepare.1 = (bf16[384,512]{1,0:T(8,128)(2,1)S(1)}, bf16[768,512]{1,0:T(8,128)(2,1)S(1)}) custom-call(s32[16]{0:T(128)S(1)} %concatenate.3.meta_ref.refs_0_, bf16[512,384]{1,0:T(8,128)(2,1)S(1)} %copy-done, bf16[512,384]{1,0:T(8,128)(2,1)S(1)} %copy-done.1, bf16[512,384]{1,0:T(8,128)(2,1)S(1)} %copy-done.2, f32[2,256,128]{2,1,0:T(8,128)S(1)} %copy-done.3, ...), custom_call_target="tpu_custom_call" | custom-call | flops 200000000 | bytes 3000000 | tf_op jit(solution)/shard_map/prepare/pallas_call | solution.py:246
  7.4 3.8 %collective-permute-start.3 = (bf16[768,512]{1,0:T(8,128)(2,1)S(1)}, bf16[768,512]{1,0:T(8,128)(2,1)S(1)}, u32[]{:S(2)}, u32[]{:S(2)}) collective-permute-start(bf16[768,512]{1,0:T(8,128)(2,1)S(1)} %get-tuple-element.12.refs_5_), channel_id=1, source_target_pairs={{0,16},{16,0},{1,17},{17,1},{2,18},{18,2},{3,19},{19,3},{4,20},{20... | collective-permute-start | bytes 2359304 | tf_op jit(solution)/shard_map/ppermute | solution.py:232
  11.2 1.2 %collective-permute-start = (bf16[384,512]{1,0:T(8,128)(2,1)S(1)}, bf16[384,512]{1,0:T(8,128)(2,1)S(1)}, u32[]{:S(2)}, u32[]{:S(2)}) collective-permute-start(bf16[384,512]{1,0:T(8,128)(2,1)S(1)} %get-tuple-element.11.refs_1_), channel_id=1, source_target_pairs={{0,4},{4,8},{8,12},{12,0},{1,5},{5,9},{9,13},{13,1},{2,6},{6,10},{... | collective-permute-start | bytes 1179656 | tf_op jit(solution)/shard_map/ppermute | solution.py:228
  12.4 1.6 %collective-permute-start.4 = (bf16[768,512]{1,0:T(8,128)(2,1)S(1)}, bf16[768,512]{1,0:T(8,128)(2,1)S(1)}, u32[]{:S(2)}, u32[]{:S(2)}) collective-permute-start(bf16[768,512]{1,0:T(8,128)(2,1)S(1)} %get-tuple-element.12.refs_5_), channel_id=1, source_target_pairs={{0,32},{32,64},{64,96},{96,128},{128,160},{160,192},{192,224},{224... | collective-permute-start | bytes 2359304 | tf_op jit(solution)/shard_map/ppermute | solution.py:228
  14.1 3.9 %collective-permute-start.5 = (bf16[768,512]{1,0:T(8,128)(2,1)S(1)}, bf16[768,512]{1,0:T(8,128)(2,1)S(1)}, u32[]{:S(2)}, u32[]{:S(2)}) collective-permute-start(bf16[768,512]{1,0:T(8,128)(2,1)S(1)} %get-tuple-element.12.refs_5_), channel_id=1, source_target_pairs={{0,224},{32,0},{64,32},{96,64},{128,96},{160,128},{192,160},{224,1... | collective-permute-start | bytes 2359304 | tf_op jit(solution)/shard_map/ppermute | solution.py:228
  18.0 9.4 %collective-permute-done.3.refs_6_ = bf16[768,512]{1,0:T(8,128)(2,1)S(1)} collective-permute-done((bf16[768,512]{1,0:T(8,128)(2,1)S(1)}, bf16[768,512]{1,0:T(8,128)(2,1)S(1)}, u32[]{:S(2)}, u32[]{:S(2)}) %collective-permute-start.3) | collective-permute-done | bytes 786464 | tf_op jit(solution)/shard_map/ppermute | solution.py:232
  27.4 2.4 %collective-permute-start.6 = (bf16[768,512]{1,0:T(8,128)(2,1)S(1)}, bf16[768,512]{1,0:T(8,128)(2,1)S(1)}, u32[]{:S(2)}, u32[]{:S(2)}) collective-permute-start(bf16[768,512]{1,0:T(8,128)(2,1)S(1)} %collective-permute-done.3.refs_6_), channel_id=1, source_target_pairs={{0,32},{32,64},{64,96},{96,128},{128,160},{160,192},{192,224},{224... | collective-permute-start | bytes 2359304 | tf_op jit(solution)/shard_map/ppermute | solution.py:265
  29.9 2.5 %collective-permute-start.1 = (bf16[384,512]{1,0:T(8,128)(2,1)S(1)}, bf16[384,512]{1,0:T(8,128)(2,1)S(1)}, u32[]{:S(2)}, u32[]{:S(2)}) collective-permute-start(bf16[384,512]{1,0:T(8,128)(2,1)S(1)} %get-tuple-element.11.refs_1_), channel_id=1, source_target_pairs={{0,12},{4,0},{8,4},{12,8},{1,13},{5,1},{9,5},{13,9},{2,14},{6,2},{... | collective-permute-start | bytes 1179656 | tf_op jit(solution)/shard_map/ppermute | solution.py:228
  32.3 0.0 collective-permute-done.refs_2_
  32.3 0.5 collective-permute-start.2
  32.9 6.9 %collective-permute-done.1.refs_3_ = bf16[384,512]{1,0:T(8,128)(2,1)S(1)} collective-permute-done((bf16[384,512]{1,0:T(8,128)(2,1)S(1)}, bf16[384,512]{1,0:T(8,128)(2,1)S(1)}, u32[]{:S(2)}, u32[]{:S(2)}) %collective-permute-start.1) | collective-permute-done | bytes 393248 | tf_op jit(solution)/shard_map/ppermute | solution.py:228
  39.7 2.6 %collective-permute-done.2.refs_4_ = bf16[384,512]{1,0:T(8,128)(2,1)S(1)} collective-permute-done((bf16[384,512]{1,0:T(8,128)(2,1)S(1)}, bf16[384,512]{1,0:T(8,128)(2,1)S(1)}, u32[]{:S(2)}, u32[]{:S(2)}) %collective-permute-start.2) | collective-permute-done | bytes 393248 | tf_op jit(solution)/shard_map/ppermute | solution.py:228
  42.4 0.0 collective-permute-done.4.refs_7_
  42.4 0.0 collective-permute-done.5.refs_8_
  42.4 0.0 copy-start.7
  42.4 9.6 %collective-permute-done.6.refs_9_ = bf16[768,512]{1,0:T(8,128)(2,1)S(1)} collective-permute-done((bf16[768,512]{1,0:T(8,128)(2,1)S(1)}, bf16[768,512]{1,0:T(8,128)(2,1)S(1)}, u32[]{:S(2)}, u32[]{:S(2)}) %collective-permute-start.6) | collective-permute-done | bytes 786464 | tf_op jit(solution)/shard_map/ppermute | solution.py:265
  52.0 0.0 copy-done.7
  52.0 0.0 copy-start.8
  52.0 0.9 copy-done.8
  52.9 0.0 copy-start.6
  52.9 14.4 %attend.1 = (bf16[400,512]{1,0:T(8,128)(2,1)S(1)}, bf16[400,512]{1,0:T(8,128)(2,1)S(1)}, bf16[400,512]{1,0:T(8,128)(2,1)S(1)}, bf16[400,512]{1,0:T(8,128)(2,1)S(1)}) custom-call(s32[16]{0:T(128)S(1)} %concatenate.3.meta_ref.refs_0_, bf16[384,512]{1,0:T(8,128)(2,1)S(1)} %get-tuple-element.11.refs_1_, bf16[384,512]{1,0:T(8,128)(2,1)S(1)} %collective-permute-done.refs_2_, ...), custom_call_target="tpu_custom_call" | custom-call | flops 9600000000 | bytes 6000000 | tf_op jit(solution)/shard_map/attend/pallas_call | solution.py:284
  67.3 0.8 collective-permute-start.7
  68.1 0.8 collective-permute-start.8
  68.9 2.4 %collective-permute-start.9 = (bf16[400,512]{1,0:T(8,128)(2,1)S(1)}, bf16[400,512]{1,0:T(8,128)(2,1)S(1)}, u32[]{:S(2)}, u32[]{:S(2)}) collective-permute-start(bf16[400,512]{1,0:T(8,128)(2,1)S(1)} %get-tuple-element.16), channel_id=1, source_target_pairs={{0,8},{4,12},{8,0},{12,4},{1,9},{5,13},{9,1},{13,5},{2,10},{6,14},... | collective-permute-start | bytes 1228808 | tf_op jit(solution)/shard_map/ppermute | solution.py:228
  71.2 5.7 %collective-permute-done.7.refs_1_ = bf16[400,512]{1,0:T(8,128)(2,1)S(1)} collective-permute-done((bf16[400,512]{1,0:T(8,128)(2,1)S(1)}, bf16[400,512]{1,0:T(8,128)(2,1)S(1)}, u32[]{:S(2)}, u32[]{:S(2)}) %collective-permute-start.7) | collective-permute-done | bytes 409632 | tf_op jit(solution)/shard_map/ppermute | solution.py:228
  76.9 0.9 collective-permute-done.8.refs_2_
  77.8 10.0 %collective-permute-done.9.refs_3_ = bf16[400,512]{1,0:T(8,128)(2,1)S(1)} collective-permute-done((bf16[400,512]{1,0:T(8,128)(2,1)S(1)}, bf16[400,512]{1,0:T(8,128)(2,1)S(1)}, u32[]{:S(2)}, u32[]{:S(2)}) %collective-permute-start.9) | collective-permute-done | bytes 409632 | tf_op jit(solution)/shard_map/ppermute | solution.py:228
  87.8 0.5 merge.1.refs_0_
  88.3 0.1 collective-permute-start.11
  88.4 0.0 copy-done.6
  88.4 0.3 constant_dynamic-slice_fusion
  88.7 3.6 %collective-permute-start.13 = (bf16[384,768]{1,0:T(8,128)(2,1)S(1)}, bf16[384,768]{1,0:T(8,128)(2,1)S(1)}, u32[]{:S(2)}, u32[]{:S(2)}) collective-permute-start(bf16[384,768]{1,0:T(8,128)(2,1)S(1)} %get-tuple-element.18), channel_id=1, source_target_pairs={{0,1},{1,0},{2,3},{3,2},{4,5},{5,4},{6,7},{7,6},{8,9},{9,8},{10,11... | collective-permute-start | bytes 1769480 | tf_op jit(solution)/shard_map/ppermute | solution.py:232
  92.3 0.8 collective-permute-start.14
  93.1 4.1 %collective-permute-start.15 = (bf16[384,768]{1,0:T(8,128)(2,1)S(1)}, bf16[384,768]{1,0:T(8,128)(2,1)S(1)}, u32[]{:S(2)}, u32[]{:S(2)}) collective-permute-start(bf16[384,768]{1,0:T(8,128)(2,1)S(1)} %get-tuple-element.17), channel_id=1, source_target_pairs={{0,19},{1,18},{2,17},{3,16},{16,3},{17,2},{18,1},{19,0},{4,23},{5,... | collective-permute-start | bytes 1769480 | tf_op jit(solution)/shard_map/ppermute | solution.py:277
  97.2 0.1 collective-permute-start.10
  97.4 0.0 collective-permute-done.11.refs_2_
  97.4 5.7 %collective-permute-start.12 = (bf16[512,384]{1,0:T(8,128)(2,1)S(1)}, bf16[512,384]{1,0:T(8,128)(2,1)S(1)}, u32[]{:S(2)}, u32[]{:S(2)}) collective-permute-start(bf16[512,384]{1,0:T(8,128)(2,1)S(1)} %collective-permute-done.11.refs_2_), channel_id=1, source_target_pairs={{0,1},{1,0},{2,3},{3,2},{4,5},{5,4},{6,7},{7,6},{8,9},{9,8},{10,11... | collective-permute-start | bytes 1179656 | tf_op jit(solution)/shard_map/ppermute | solution.py:232
  103.0 0.0 collective-permute-done.13.refs_5_
  103.0 5.9 %collective-permute-done.14.refs_6_ = bf16[384,768]{1,0:T(8,128)(2,1)S(1)} collective-permute-done((bf16[384,768]{1,0:T(8,128)(2,1)S(1)}, bf16[384,768]{1,0:T(8,128)(2,1)S(1)}, u32[]{:S(2)}, u32[]{:S(2)}) %collective-permute-start.14) | collective-permute-done | bytes 589856 | tf_op jit(solution)/shard_map/ppermute | solution.py:232
  109.0 1.6 %collective-permute-done.15.refs_7_ = bf16[384,768]{1,0:T(8,128)(2,1)S(1)} collective-permute-done((bf16[384,768]{1,0:T(8,128)(2,1)S(1)}, bf16[384,768]{1,0:T(8,128)(2,1)S(1)}, u32[]{:S(2)}, u32[]{:S(2)}) %collective-permute-start.15) | collective-permute-done | bytes 589856 | tf_op jit(solution)/shard_map/ppermute | solution.py:277
  110.6 0.0 collective-permute-done.10.refs_1_
  110.6 0.0 collective-permute-done.12.refs_3_
  110.6 2.7 %project.1 = bf16[512,768]{1,0:T(8,128)(2,1)} custom-call(bf16[512,384]{1,0:T(8,128)(2,1)S(1)} %merge.1.refs_0_, bf16[512,384]{1,0:T(8,128)(2,1)S(1)} %collective-permute-done.10.refs_1_, bf16[512,384]{1,0:T(8,128)(2,1)S(1)} %collective-permute-done.11.refs_2_, bf16[512,384]{1,0:T(8,128)(2,1)S(1)} %collective-permute-done.12.refs_3_, ...), custom_call_target="tpu_custom_call" | custom-call | flops 1200000000 | bytes 4700000 | tf_op jit(solution)/shard_map/project/pallas_call | solution.py:319
Async XLA Ops:
  0.7 1.0 copy-start
  1.7 1.0 copy-start.1
  2.7 1.0 copy-start.2
  3.7 0.9 copy-start.3
  4.7 0.8 copy-start.4
  5.5 0.7 copy-start.5
  7.4 20.0 %collective-permute-start.3 = (bf16[768,512]{1,0:T(8,128)(2,1)S(1)}, bf16[768,512]{1,0:T(8,128)(2,1)S(1)}, u32[]{:S(2)}, u32[]{:S(2)}) collective-permute-start(bf16[768,512]{1,0:T(8,128)(2,1)S(1)} %get-tuple-element.12.refs_5_), channel_id=1, source_target_pairs={{0,16},{16,0},{1,17},{17,1},{2,18},{18,2},{3,19},{19,3},{4,20},{20... | collective-permute-start | bytes 2359304 | tf_op jit(solution)/shard_map/ppermute | solution.py:232
  11.2 21.1 %collective-permute-start = (bf16[384,512]{1,0:T(8,128)(2,1)S(1)}, bf16[384,512]{1,0:T(8,128)(2,1)S(1)}, u32[]{:S(2)}, u32[]{:S(2)}) collective-permute-start(bf16[384,512]{1,0:T(8,128)(2,1)S(1)} %get-tuple-element.11.refs_1_), channel_id=1, source_target_pairs={{0,4},{4,8},{8,12},{12,0},{1,5},{5,9},{9,13},{13,1},{2,6},{6,10},{... | collective-permute-start | bytes 1179656 | tf_op jit(solution)/shard_map/ppermute | solution.py:228
  12.4 29.9 %collective-permute-start.4 = (bf16[768,512]{1,0:T(8,128)(2,1)S(1)}, bf16[768,512]{1,0:T(8,128)(2,1)S(1)}, u32[]{:S(2)}, u32[]{:S(2)}) collective-permute-start(bf16[768,512]{1,0:T(8,128)(2,1)S(1)} %get-tuple-element.12.refs_5_), channel_id=1, source_target_pairs={{0,32},{32,64},{64,96},{96,128},{128,160},{160,192},{192,224},{224... | collective-permute-start | bytes 2359304 | tf_op jit(solution)/shard_map/ppermute | solution.py:228
  14.1 28.3 %collective-permute-start.5 = (bf16[768,512]{1,0:T(8,128)(2,1)S(1)}, bf16[768,512]{1,0:T(8,128)(2,1)S(1)}, u32[]{:S(2)}, u32[]{:S(2)}) collective-permute-start(bf16[768,512]{1,0:T(8,128)(2,1)S(1)} %get-tuple-element.12.refs_5_), channel_id=1, source_target_pairs={{0,224},{32,0},{64,32},{96,64},{128,96},{160,128},{192,160},{224,1... | collective-permute-start | bytes 2359304 | tf_op jit(solution)/shard_map/ppermute | solution.py:228
  27.4 24.5 %collective-permute-start.6 = (bf16[768,512]{1,0:T(8,128)(2,1)S(1)}, bf16[768,512]{1,0:T(8,128)(2,1)S(1)}, u32[]{:S(2)}, u32[]{:S(2)}) collective-permute-start(bf16[768,512]{1,0:T(8,128)(2,1)S(1)} %collective-permute-done.3.refs_6_), channel_id=1, source_target_pairs={{0,32},{32,64},{64,96},{96,128},{128,160},{160,192},{192,224},{224... | collective-permute-start | bytes 2359304 | tf_op jit(solution)/shard_map/ppermute | solution.py:265
  29.9 9.9 %collective-permute-start.1 = (bf16[384,512]{1,0:T(8,128)(2,1)S(1)}, bf16[384,512]{1,0:T(8,128)(2,1)S(1)}, u32[]{:S(2)}, u32[]{:S(2)}) collective-permute-start(bf16[384,512]{1,0:T(8,128)(2,1)S(1)} %get-tuple-element.11.refs_1_), channel_id=1, source_target_pairs={{0,12},{4,0},{8,4},{12,8},{1,13},{5,1},{9,5},{13,9},{2,14},{6,2},{... | collective-permute-start | bytes 1179656 | tf_op jit(solution)/shard_map/ppermute | solution.py:228
  32.3 10.0 %collective-permute-start.2 = (bf16[384,512]{1,0:T(8,128)(2,1)S(1)}, bf16[384,512]{1,0:T(8,128)(2,1)S(1)}, u32[]{:S(2)}, u32[]{:S(2)}) collective-permute-start(bf16[384,512]{1,0:T(8,128)(2,1)S(1)} %get-tuple-element.11.refs_1_), channel_id=1, source_target_pairs={{0,8},{4,12},{8,0},{12,4},{1,9},{5,13},{9,1},{13,5},{2,10},{6,14},... | collective-permute-start | bytes 1179656 | tf_op jit(solution)/shard_map/ppermute | solution.py:228
  42.4 9.6 %copy-start.7 = (bf16[768,512]{1,0:T(8,128)(2,1)}, bf16[768,512]{1,0:T(8,128)(2,1)S(1)}, u32[]{:S(2)}) copy-start(bf16[768,512]{1,0:T(8,128)(2,1)S(1)} %collective-permute-done.5.refs_8_) | copy-start | bytes 2359300
  52.0 0.9 copy-start.8
  52.9 35.5 %copy-start.6 = (bf16[384,3072]{1,0:T(8,128)(2,1)S(1)}, bf16[384,3072]{1,0:T(8,128)(2,1)}, u32[]{:S(2)}) copy-start(bf16[384,3072]{1,0:T(8,128)(2,1)} %param.12) | copy-start | bytes 7077892
  67.3 9.6 %collective-permute-start.7 = (bf16[400,512]{1,0:T(8,128)(2,1)S(1)}, bf16[400,512]{1,0:T(8,128)(2,1)S(1)}, u32[]{:S(2)}, u32[]{:S(2)}) collective-permute-start(bf16[400,512]{1,0:T(8,128)(2,1)S(1)} %get-tuple-element.14), channel_id=1, source_target_pairs={{0,12},{4,0},{8,4},{12,8},{1,13},{5,1},{9,5},{13,9},{2,14},{6,2},{... | collective-permute-start | bytes 1228808 | tf_op jit(solution)/shard_map/ppermute | solution.py:228
  68.1 9.8 %collective-permute-start.8 = (bf16[400,512]{1,0:T(8,128)(2,1)S(1)}, bf16[400,512]{1,0:T(8,128)(2,1)S(1)}, u32[]{:S(2)}, u32[]{:S(2)}) collective-permute-start(bf16[400,512]{1,0:T(8,128)(2,1)S(1)} %get-tuple-element.15), channel_id=1, source_target_pairs={{0,4},{4,8},{8,12},{12,0},{1,5},{5,9},{9,13},{13,1},{2,6},{6,10},{... | collective-permute-start | bytes 1228808 | tf_op jit(solution)/shard_map/ppermute | solution.py:228
  68.9 18.9 %collective-permute-start.9 = (bf16[400,512]{1,0:T(8,128)(2,1)S(1)}, bf16[400,512]{1,0:T(8,128)(2,1)S(1)}, u32[]{:S(2)}, u32[]{:S(2)}) collective-permute-start(bf16[400,512]{1,0:T(8,128)(2,1)S(1)} %get-tuple-element.16), channel_id=1, source_target_pairs={{0,8},{4,12},{8,0},{12,4},{1,9},{5,13},{9,1},{13,5},{2,10},{6,14},... | collective-permute-start | bytes 1228808 | tf_op jit(solution)/shard_map/ppermute | solution.py:228
  88.3 9.1 %collective-permute-start.11 = (bf16[512,384]{1,0:T(8,128)(2,1)S(1)}, bf16[512,384]{1,0:T(8,128)(2,1)S(1)}, u32[]{:S(2)}, u32[]{:S(2)}) collective-permute-start(bf16[512,384]{1,0:T(8,128)(2,1)S(1)} %merge.1.refs_0_), channel_id=1, source_target_pairs={{0,2},{2,0},{1,3},{3,1},{4,6},{6,4},{5,7},{7,5},{8,10},{10,8},{9,1... | collective-permute-start | bytes 1179656 | tf_op jit(solution)/shard_map/ppermute | solution.py:232
  88.7 14.4 %collective-permute-start.13 = (bf16[384,768]{1,0:T(8,128)(2,1)S(1)}, bf16[384,768]{1,0:T(8,128)(2,1)S(1)}, u32[]{:S(2)}, u32[]{:S(2)}) collective-permute-start(bf16[384,768]{1,0:T(8,128)(2,1)S(1)} %get-tuple-element.18), channel_id=1, source_target_pairs={{0,1},{1,0},{2,3},{3,2},{4,5},{5,4},{6,7},{7,6},{8,9},{9,8},{10,11... | collective-permute-start | bytes 1769480 | tf_op jit(solution)/shard_map/ppermute | solution.py:232
  92.3 16.7 %collective-permute-start.14 = (bf16[384,768]{1,0:T(8,128)(2,1)S(1)}, bf16[384,768]{1,0:T(8,128)(2,1)S(1)}, u32[]{:S(2)}, u32[]{:S(2)}) collective-permute-start(bf16[384,768]{1,0:T(8,128)(2,1)S(1)} %get-tuple-element.20), channel_id=1, source_target_pairs={{0,2},{2,0},{1,3},{3,1},{4,6},{6,4},{5,7},{7,5},{8,10},{10,8},{9,1... | collective-permute-start | bytes 1769480 | tf_op jit(solution)/shard_map/ppermute | solution.py:232
  93.1 17.5 %collective-permute-start.15 = (bf16[384,768]{1,0:T(8,128)(2,1)S(1)}, bf16[384,768]{1,0:T(8,128)(2,1)S(1)}, u32[]{:S(2)}, u32[]{:S(2)}) collective-permute-start(bf16[384,768]{1,0:T(8,128)(2,1)S(1)} %get-tuple-element.17), channel_id=1, source_target_pairs={{0,19},{1,18},{2,17},{3,16},{16,3},{17,2},{18,1},{19,0},{4,23},{5,... | collective-permute-start | bytes 1769480 | tf_op jit(solution)/shard_map/ppermute | solution.py:277
  97.2 13.3 %collective-permute-start.10 = (bf16[512,384]{1,0:T(8,128)(2,1)S(1)}, bf16[512,384]{1,0:T(8,128)(2,1)S(1)}, u32[]{:S(2)}, u32[]{:S(2)}) collective-permute-start(bf16[512,384]{1,0:T(8,128)(2,1)S(1)} %merge.1.refs_0_), channel_id=1, source_target_pairs={{0,1},{1,0},{2,3},{3,2},{4,5},{5,4},{6,7},{7,6},{8,9},{9,8},{10,11... | collective-permute-start | bytes 1179656 | tf_op jit(solution)/shard_map/ppermute | solution.py:232
  97.4 13.2 %collective-permute-start.12 = (bf16[512,384]{1,0:T(8,128)(2,1)S(1)}, bf16[512,384]{1,0:T(8,128)(2,1)S(1)}, u32[]{:S(2)}, u32[]{:S(2)}) collective-permute-start(bf16[512,384]{1,0:T(8,128)(2,1)S(1)} %collective-permute-done.11.refs_2_), channel_id=1, source_target_pairs={{0,1},{1,0},{2,3},{3,2},{4,5},{5,4},{6,7},{7,6},{8,9},{9,8},{10,11... | collective-permute-start | bytes 1179656 | tf_op jit(solution)/shard_map/ppermute | solution.py:232

commit v2 on v1

v2 whole, which is shorter than its diff:
```python
import math

import jax
import jax.numpy as jnp
import numpy as np
from jax import lax
from jax.experimental import pallas as pl
from jax.experimental.pallas import tpu as pltpu
from jax.sharding import Mesh
from jax.sharding import PartitionSpec as P

RT = 16
RH = 56
RW = 56
PH = 16
PW = 16
FRAME = PH * PW
HEAD_DIM = 128
CLIPS = 12
HEADS = 3
TOK = 512
SLOTS = 16
ROPE_BASE = 256.0
NEG = -1e30
EXP_SCALE = HEAD_DIM ** (-0.5) * math.log2(math.e)

STEPS = (0, -1, 1, 2)
CALLS = ((3, 0), (1, 2))


def rope_tables():
    freq = np.zeros(HEAD_DIM)
    swap = np.zeros((HEAD_DIM, HEAD_DIM), np.float32)
    sign = np.zeros(HEAD_DIM)
    base = 0
    bounds = []
    for width in (RT, RH, RW):
        half = width // 2
        f = np.exp(-(2.0 * np.arange(half) / width) * math.log(ROPE_BASE))
        freq[base : base + half] = f
        freq[base + half : base + width] = f
        sign[base : base + half] = -1.0
        sign[base + half : base + width] = 1.0
        for j in range(half):
            swap[base + half + j, base + j] = 1.0
            swap[base + j, base + half + j] = 1.0
        bounds.append((base, base + width))
        base += width
    token = np.arange(FRAME)
    angle = np.zeros((FRAME, HEAD_DIM))
    (t0, t1), (h0, h1), (w0, w1) = bounds
    angle[:, h0:h1] = (token // PW)[:, None] * freq[None, h0:h1]
    angle[:, w0:w1] = (token % PW)[:, None] * freq[None, w0:w1]
    angle_t = np.zeros((SLOTS, HEAD_DIM))
    angle_t[:, t0:t1] = np.arange(SLOTS)[:, None] * freq[None, t0:t1]
    space = np.stack([np.cos(angle), np.sin(angle) * sign]).astype(np.float32)
    time = np.stack([np.cos(angle_t), np.sin(angle_t) * sign]).astype(np.float32)
    return space, time, swap


def here():
    return lax.axis_index("z"), lax.axis_index("yh"), lax.axis_index("x")


def clip_bounds(counts_ref, frame):
    start = jnp.int32(0)
    end = jnp.int32(0)
    total = jnp.int32(0)
    for c in range(CLIPS):
        past = frame >= total
        before = total
        total = total + counts_ref[c]
        start = jnp.where(past, before, start)
        end = jnp.where(past, total, end)
    return start, end


def dot_nt(a, b):
    return lax.dot_general(a, b, (((1,), (1,)), ((), ())), preferred_element_type=jnp.float32)


def dot_nn(a, b):
    return lax.dot_general(a, b, (((1,), (0,)), ((), ())), preferred_element_type=jnp.float32)


def prepare_kernel(counts_ref, q_hbm, k_hbm, v_hbm, space_hbm, time_hbm, swap_hbm, q_out, kv_out, *refs):
    bufs, (kv_buf, q_buf, sem) = refs[:-3], refs[-3:]
    sources = (k_hbm, space_hbm, time_hbm, swap_hbm, v_hbm, q_hbm)
    copies = [pltpu.make_async_copy(s, d, sem.at[i]) for i, (s, d) in enumerate(zip(sources, bufs))]
    for c in copies:
        c.start()
    k_ref, space_ref, time_ref, swap_ref, v_ref, q_ref = bufs
    z, yh, x = here()
    first = z * SLOTS + yh * 8 + x * 2
    times = []
    for e in range(2):
        start, _ = clip_bounds(counts_ref, first + e)
        times.append(jnp.clip(first + e - start, 0, SLOTS - 1))
    for c in copies[:4]:
        c.wait()
    swap = swap_ref[0]
    eye = swap_ref[1]
    lane = lax.broadcasted_iota(jnp.int32, (FRAME, HEAD_DIM), 1)
    tables = []
    for e in range(2):
        cos = jnp.where(lane < RT, time_ref[0, pl.ds(times[e], 1), :], space_ref[0])
        sin = jnp.where(lane < RT, time_ref[1, pl.ds(times[e], 1), :], space_ref[1])
        tables.append((cos, sin))
    parts = [
        (e, h, slice(FRAME * e, FRAME * (e + 1)), slice(HEAD_DIM * h, HEAD_DIM * (h + 1)))
        for h in range(HEADS)
        for e in range(2)
    ]
    for e, h, tok, col in parts:
        cos, sin = tables[e]
        k = k_ref[tok, col]
        rot = ((k.astype(jnp.float32) * cos + dot_nn(k, swap) * sin) * EXP_SCALE).astype(jnp.bfloat16)
        kv_buf[col, FRAME * e : FRAME * e + 128] = rot[:128]
        kv_buf[col, FRAME * e + 128 : FRAME * e + 256] = rot[128:]
    outs = [pltpu.make_async_copy(kv_buf.at[pl.ds(0, HEADS * HEAD_DIM)], kv_out.at[pl.ds(0, HEADS * HEAD_DIM)], sem.at[6])]
    outs[0].start()
    copies[4].wait()
    for e, h, tok, col in parts:
        kv_buf[HEAD_DIM * (HEADS + h) : HEAD_DIM * (HEADS + h + 1), tok] = dot_nt(eye, v_ref[tok, col]).astype(jnp.bfloat16)
    values = pl.ds(HEADS * HEAD_DIM, HEADS * HEAD_DIM)
    outs.append(pltpu.make_async_copy(kv_buf.at[values], kv_out.at[values], sem.at[7]))
    outs[1].start()
    copies[5].wait()
    turned = [(cos.T, sin.T) for cos, sin in tables]
    for e, h, tok, col in parts:
        cos, sin = turned[e]
        q = q_ref[tok, col]
        q_buf[col, tok] = (dot_nt(eye, q) * cos + dot_nt(swap, q) * sin).astype(jnp.bfloat16)
    outs.append(pltpu.make_async_copy(q_buf, q_out, sem.at[8]))
    outs[2].start()
    for c in outs:
        c.wait()


def stage_kernel(q_hbm, kv_hbm, q_out, kv_out, sem):
    copies = [
        pltpu.make_async_copy(q_hbm, q_out, sem.at[0]),
        pltpu.make_async_copy(kv_hbm, kv_out, sem.at[1]),
    ]
    for c in copies:
        c.start()
    for c in copies:
        c.wait()


def split3(value):
    hi = value.astype(jnp.bfloat16)
    rest = value - hi.astype(jnp.float32)
    mid = rest.astype(jnp.bfloat16)
    low = (rest - mid.astype(jnp.float32)).astype(jnp.bfloat16)
    return [hi, mid, low]


def fold(value, op):
    out = value[0:8]
    for i in range(8, value.shape[0], 8):
        out = op(out, value[i : i + 8])
    return out


def attend_kernel(steps, final, counts_ref, *refs):
    n, count = HEADS, len(steps)
    q_refs, refs = refs[:count], refs[count:]
    kv_refs, refs = refs[:3], refs[3:]
    if final:
        near_ref, refs = refs[0], refs[1:]
        o_refs, (kv,) = refs[:count], refs[count:]
    else:
        near_ref, kv = refs

    def load(a):
        for part in range(2):
            row = slice(HEAD_DIM * (n * part + a), HEAD_DIM * (n * part + a + 1))
            if final:
                kv[0, row, :] = kv_refs[0][row, :]
                kv[1, row, :] = kv_refs[1 + part][HEAD_DIM * a : HEAD_DIM * (a + 1), :]
            else:
                for i in range(3):
                    kv[i, row, :] = kv_refs[i][row, :]

    z, yh, x = here()
    plane = z * SLOTS
    tables = []
    for r in range(count):
        xq = lax.rem(x + steps[r] + 4, 4)
        for e in range(2):
            start, end = clip_bounds(counts_ref, plane + yh * 8 + xq * 2 + e)
            places = []
            for sl in range(2):
                row = 1 - yh if final else yh
                mid = plane + row * 8 + x * 2 + sl
                before = mid - SLOTS >= start
                inside = (mid >= start) & (mid < end)
                after = mid + SLOTS < end
                if final:
                    src = jnp.where(inside, 0, 1)
                else:
                    src = jnp.where(inside, 1, jnp.where(before, 0, 2))
                valid = before | inside | after
                places.append((src, jnp.where(valid, 0.0, NEG), valid))
            tables.append((places, places[0][2] | places[1][2]))
    units = [(a, r, e) for a in range(n) for r in range(count) for e in range(2)]
    state, stats = {}, {}

    def scores(u, sl):
        a, r, e = units[u]
        if sl == 0 and r == 0 and e == 0:
            load(a)
        src, bias, _ = tables[2 * r + e][0][sl]
        row = slice(HEAD_DIM * a, HEAD_DIM * (a + 1))
        lo = FRAME * sl
        keys = jnp.concatenate([kv[src, row, lo : lo + 128], kv[src, row, lo + 128 : lo + 256]], axis=0)
        s = dot_nn(keys, q_refs[r][row, FRAME * e : FRAME * (e + 1)])
        peak = fold(s, jnp.maximum) + bias
        st = state.setdefault(u, {"s": {}})
        st["s"][sl] = s
        st["top"] = peak if sl == 0 else jnp.maximum(st["top"], peak)

    def weigh(u, sl):
        a, r, e = units[u]
        places, some = tables[2 * r + e]
        src, bias, _ = places[sl]
        st = state[u]
        p = jnp.exp2(st["s"].pop(sl) + jnp.where(some, bias - st["top"], NEG))
        add = fold(p, jnp.add)
        row = slice(HEAD_DIM * (n + a), HEAD_DIM * (n + a + 1))
        term = dot_nn(kv[src, row, FRAME * sl : FRAME * (sl + 1)], p.astype(jnp.bfloat16))
        st["total"] = add if sl == 0 else st["total"] + add
        st["acc"] = term if sl == 0 else st["acc"] + term

    def top(u):
        state[u]["top"] = jnp.max(state[u]["top"], axis=0, keepdims=True)

    for sl in range(2):
        scores(0, sl)
    top(0)
    for u, (a, r, e) in enumerate(units):
        for sl in range(2):
            if u + 1 < len(units):
                scores(u + 1, sl)
            weigh(u, sl)
        if u + 1 < len(units):
            top(u + 1)
        st = state.pop(u)
        total = jnp.sum(st["total"], axis=0, keepdims=True)
        peak = jnp.where(tables[2 * r + e][1], st["top"], NEG)
        row = slice(HEAD_DIM * a, HEAD_DIM * (a + 1))
        tok = slice(FRAME * e, FRAME * (e + 1))
        peak_row = slice(HEAD_DIM * n + 8 * a, HEAD_DIM * n + 8 * a + 1)
        total_row = slice(HEAD_DIM * n + 8 * a + 1, HEAD_DIM * n + 8 * a + 2)
        if final:
            block = STEPS.index(steps[r])
            near_peak = near_ref[block, peak_row, tok]
            both = jnp.maximum(peak, near_peak)
            far_part = jnp.exp2(peak - both)
            near_part = jnp.exp2(near_peak - both)
            total = total * far_part + near_ref[block, total_row, tok] * near_part
            total = jnp.maximum(total, 1e-30)
            inv = 1.0 / total
            acc = st["acc"] * (far_part * inv) + near_ref[block, row, tok] * (near_part * inv)
            o_refs[r][row, tok] = acc.astype(jnp.bfloat16)
            stats[r, a, e] = both + jnp.log2(total)
        else:
            near_ref[r, row, tok] = st["acc"]
            near_ref[r, peak_row, tok] = peak
            near_ref[r, total_row, tok] = total
    if final:
        for r in range(count):
            rows = []
            for a in range(n):
                rows += split3(jnp.concatenate([stats[r, a, 0], stats[r, a, 1]], axis=1))
            rows.append(jnp.zeros((16 - len(rows), TOK), jnp.bfloat16))
            o_refs[r][HEAD_DIM * n : HEAD_DIM * n + 16, :] = jnp.concatenate(rows, axis=0)


def level(ref, a):
    base = HEAD_DIM * HEADS
    tail = ref[base : base + 16, :].astype(jnp.float32)
    return tail[3 * a : 3 * a + 1] + tail[3 * a + 1 : 3 * a + 2] + tail[3 * a + 2 : 3 * a + 3]


def merge_two_kernel(p0, p1, out):
    for a in range(HEADS):
        row = slice(HEAD_DIM * a, HEAD_DIM * (a + 1))
        one, two = level(p0, a), level(p1, a)
        top = jnp.maximum(one, two)
        one, two = jnp.exp2(one - top), jnp.exp2(two - top)
        inv = 1.0 / (one + two)
        out[row, :] = p0[row, :].astype(jnp.float32) * (one * inv) + p1[row, :].astype(jnp.float32) * (two * inv)
        out[HEAD_DIM * HEADS + 8 * a : HEAD_DIM * HEADS + 8 * a + 1, :] = top + jnp.log2(one + two)


def merge_last_kernel(m, p0, p1, out):
    for a in range(HEADS):
        row = slice(HEAD_DIM * a, HEAD_DIM * (a + 1))
        base = HEAD_DIM * HEADS + 8 * a
        levels = [m[base : base + 1, :], level(p0, a), level(p1, a)]
        top = jnp.maximum(jnp.maximum(levels[0], levels[1]), levels[2])
        shares = [jnp.exp2(v - top) for v in levels]
        inv = 1.0 / (shares[0] + shares[1] + shares[2])
        acc = None
        for p, s in zip((m, p0, p1), shares):
            term = p[row, :].astype(jnp.float32) * (s * inv)
            acc = term if acc is None else acc + term
        out[:, row] = acc.T.astype(jnp.bfloat16)


def project_kernel(*refs):
    refs, out = refs[:-1], refs[-1]
    acc = None
    if len(refs) % 2:
        acc, refs = refs[0][...], refs[1:]
    for i in range(0, len(refs), 2):
        term = dot_nn(refs[i][...], refs[i + 1][...])
        acc = term if acc is None else acc + term
    out[...] = acc.astype(out.dtype)


VMEM = pl.BlockSpec(memory_space=pltpu.VMEM)
SMEM = pl.BlockSpec(memory_space=pltpu.SMEM)
HBM = pl.BlockSpec(memory_space=pltpu.HBM)


def params(mib):
    return pltpu.CompilerParams(vmem_limit_bytes=mib * 1024 * 1024)


def cost(flops, size, trans=0):
    return pl.CostEstimate(flops=flops, bytes_accessed=size, transcendentals=trans)


def shift(value, axis, by):
    count = lax.axis_size(axis)
    return lax.ppermute(value, axis, [(i, (i + by) % count) for i in range(count)])


def flip(value, axis):
    return lax.ppermute(value, axis, [(0, 1), (1, 0)])


def per_device(query_rows, key_rows, value_rows, frame_counts, out_weight):
    space, time, swap = rope_tables()
    mats = np.stack([swap, np.eye(HEAD_DIM)]).astype(jnp.bfloat16)
    feats = HEADS * HEAD_DIM
    q, kv = pl.pallas_call(
        prepare_kernel,
        out_shape=[jax.ShapeDtypeStruct((size, TOK), jnp.bfloat16) for size in (feats, 2 * feats)],
        in_specs=[SMEM] + [HBM] * 6,
        out_specs=[HBM] * 2,
        scratch_shapes=[
            pltpu.VMEM(key_rows.shape, jnp.bfloat16),
            pltpu.VMEM(space.shape, jnp.float32),
            pltpu.VMEM(time.shape, jnp.float32),
            pltpu.VMEM(mats.shape, jnp.bfloat16),
            pltpu.VMEM(key_rows.shape, jnp.bfloat16),
            pltpu.VMEM(key_rows.shape, jnp.bfloat16),
            pltpu.VMEM((2 * feats, TOK), jnp.bfloat16),
            pltpu.VMEM((feats, TOK), jnp.bfloat16),
            pltpu.SemaphoreType.DMA((9,)),
        ],
        compiler_params=params(58),
        cost_estimate=cost(200_000_000, 3_000_000),
        name="prepare",
    )(frame_counts, query_rows, key_rows, value_rows, jnp.asarray(space), jnp.asarray(time), jnp.asarray(mats))

    pair = flip(kv, "yh")
    below = shift(kv, "z", 1)
    above = shift(kv, "z", -1)
    q_left = shift(q, "x", 1)
    q_right = shift(q, "x", -1)
    q_across = shift(q, "x", 2)
    q, kv = pl.pallas_call(
        stage_kernel,
        out_shape=[jax.ShapeDtypeStruct(v.shape, v.dtype) for v in (q, kv)],
        in_specs=[HBM] * 2,
        out_specs=[VMEM] * 2,
        scratch_shapes=[pltpu.SemaphoreType.DMA((2,))],
        compiler_params=params(8),
        cost_estimate=cost(1_000_000, 2_400_000),
        name="stage",
    )(q, kv)
    tp = lax.axis_index("yl") * 2 + lax.axis_index("core")
    cols = out_weight.shape[1] // 4

    def mine(j):
        return lax.dynamic_slice_in_dim(out_weight, j * cols, cols, 1)

    w_core = flip(mine(tp ^ 1), "core")
    pair, below, above, q_left, q_right, q_across, q, kv, w_core = lax.optimization_barrier(
        (pair, below, above, q_left, q_right, q_across, q, kv, w_core)
    )
    slant = [(zi * 2, (zi + 1) % 8 * 2) for zi in range(8)]
    slant += [(zi * 2 + 1, (zi - 1) % 8 * 2 + 1) for zi in range(8)]
    v_far = lax.ppermute(pair[feats:], ("z", "yh"), slant)
    k_far = flip(jnp.where(lax.axis_index("yh") == 1, below[:feats], above[:feats]), "yh")
    qs = [q, q_left, q_right, q_across]

    near_shape = jax.ShapeDtypeStruct((4, feats + 8 * HEADS, TOK), jnp.float32)
    near = pl.pallas_call(
        lambda *refs: attend_kernel(STEPS, False, *refs),
        out_shape=near_shape,
        in_specs=[SMEM] + [VMEM] * 7,
        out_specs=VMEM,
        scratch_shapes=[pltpu.VMEM((3, 2 * feats, TOK), jnp.bfloat16)],
        compiler_params=params(24),
        cost_estimate=cost(7_000_000_000, 5_000_000, 3_000_000),
        name="attend_near",
    )(frame_counts, *qs, below, kv, above)

    out = jax.ShapeDtypeStruct((feats + 16, TOK), jnp.bfloat16)
    partial = {}
    for block in CALLS:
        count = len(block)
        steps = [STEPS[r] for r in block]
        done = pl.pallas_call(
            lambda *refs, steps=steps: attend_kernel(steps, True, *refs),
            out_shape=[out] * count,
            in_specs=[SMEM] + [VMEM] * (count + 4),
            out_specs=[VMEM] * count,
            scratch_shapes=[pltpu.VMEM((2, 2 * feats, TOK), jnp.bfloat16)],
            compiler_params=params(24),
            cost_estimate=cost((1 + 2 * count) * 1_100_000_000, 3_000_000, count * 800_000),
            name="attend_far",
        )(frame_counts, *[qs[r] for r in block], pair, k_far, v_far, near)
        partial.update(zip(block, done))
        if block != CALLS[-1]:
            near, partial[block[0]] = lax.optimization_barrier((near, partial[block[0]]))

    out_weight, partial[1] = lax.optimization_barrier((out_weight, partial[1]))
    w_own = mine(tp)
    w_yl = flip(mine(tp ^ 2), "yl")
    w_far = lax.ppermute(mine(tp ^ 3), ("yh", "yl", "core"), [(i, 7 - i) for i in range(8)])
    across = shift(partial[3], "x", 2)
    left = shift(partial[1], "x", -1)
    right = shift(partial[2], "x", 1)
    merged = pl.pallas_call(
        merge_two_kernel,
        out_shape=jax.ShapeDtypeStruct((feats + 8 * HEADS, TOK), jnp.float32),
        in_specs=[VMEM] * 2,
        out_specs=VMEM,
        compiler_params=params(8),
        cost_estimate=cost(6_000_000_000, 2_000_000),
        name="merge_two",
    )(partial[0], across)
    att = pl.pallas_call(
        merge_last_kernel,
        out_shape=jax.ShapeDtypeStruct((TOK, feats), jnp.bfloat16),
        in_specs=[VMEM] * 3,
        out_specs=VMEM,
        compiler_params=params(8),
        cost_estimate=cost(30_000_000, 2_000_000),
        name="merge_last",
    )(merged, left, right)
    att_yl = flip(att, "yl")
    att_core = flip(att, "core")
    att_yl, w_yl, w_far = lax.optimization_barrier((att_yl, w_yl, w_far))
    att_far = flip(att_yl, "core")

    def add_terms(before, pairs, dtype):
        operands = ([] if before is None else [before]) + [v for pair in pairs for v in pair]
        tile = 256
        blocks = [pl.BlockSpec((tile, v.shape[1]), lambda i: (i, 0)) for v in operands[: len(operands) % 2]]
        for _ in pairs:
            blocks += [pl.BlockSpec((tile, feats), lambda i: (i, 0)), VMEM]
        return pl.pallas_call(
            project_kernel,
            grid=(TOK // tile,),
            out_shape=jax.ShapeDtypeStruct((TOK, cols), dtype),
            in_specs=blocks,
            out_specs=pl.BlockSpec((tile, cols), lambda i: (i, 0)),
            compiler_params=params(16),
            cost_estimate=cost(600_000_000 * len(pairs), 1_000_000),
            name="project",
        )(*operands)

    total = add_terms(None, [(att, w_own), (att_core, w_core)], jnp.float32)
    total = add_terms(total, [(att_yl, w_yl)], jnp.float32)
    return add_terms(total, [(att_far, w_far)], jnp.bfloat16)


def solution(mesh):
    fine = Mesh(mesh.devices.reshape(8, 2, 4, 2, 2), ("z", "yh", "x", "yl", "core"))
    seq, tp = ("z", "yh", "x"), ("yl", "core")
    return jax.shard_map(
        per_device,
        mesh=fine,
        in_specs=(P(seq, tp), P(seq, tp), P(seq, tp), P(), P(tp, None)),
        out_specs=P(seq, tp),
        check_vma=False,
    )
```

time: 114 us -> 88.5 us (0.78)
  waiting for transfers between devices: 52.6 us -> 36.2 us
  starting transfers between devices: 34.5 us -> 25.1 us
  Pallas kernels: 18.7 us -> 22.4 us
  local copies, waits for them, and re-layouts: 7.38 us -> 4.28 us
    ppermute x6 -> x7, waiting for transfers between devices: 15.4 us -> 9.62 us  [flip(): return lax.ppermute(value, axis, [(0, 1), (1, 0)])]
    ppermute x6 -> x7, starting transfers between devices: 14.2 us -> 8.96 us  [flip(): return lax.ppermute(value, axis, [(0, 1), (1, 0)])]
    ppermute x1, waiting for transfers between devices: 9.6 us -> 4.67 us  [per_device(): v_far = lax.ppermute(pair[feats:], ('z', 'yh'), slant)]
    unnamed x18 -> x8, local copies, waits for them, and re-layouts: 6.38 us -> 2.14 us
    ppermute x8, waiting for transfers between devices: 26.1 us -> 21.9 us  [shift(): lax.ppermute(value, axis, [(i, (i + by) % count) for i in range(count)])]
    pallas_call x4 -> x10, Pallas kernels: 18.7 us -> 22.4 us  [the longest x2 7.99 us: per_device(): pl.pallas_call(lambda *refs, steps=steps: attend_kernel(steps, True, *ref...]
    ppermute x1, starting transfers between devices: 4.13 us -> 2.12 us  [per_device(): lax.ppermute(mine(tp ^ 3), ('yh', 'yl', 'core'), [(i, 7 - i) for i in ran...]
    dynamic_slice x1 -> x2, local copies, waits for them, and re-layouts: 0.26 us -> 2.11 us  [mine(): return lax.dynamic_slice_in_dim(out_weight, j * cols, cols, 1)]
  transfers between devices with their start and end apart: 16 -> 17, of which waited for: 9 -> 8; matrix products, arithmetic and copies ran while one was open for 0% -> 2% of each run, Pallas kernels for 0% -> 15%
where the time goes in v2:
time: 88.5 us; the launch traced here: 88.2 us
  waiting for transfers between devices  36.2 us (41%)
  starting transfers between devices  25.1 us (28%)
  Pallas kernels  22.4 us (25%)
  local copies, waits for them, and re-layouts  4.28 us (5%)
    ppermute x8, waiting for transfers between devices, shift(): lax.ppermute(value, axis, [(i, (i + by) % count) for i in range(count)])  21.9 us
    ppermute x8, starting transfers between devices, shift(): lax.ppermute(value, axis, [(i, (i + by) % count) for i in range(count)])  12.2 us
    ppermute x7, waiting for transfers between devices, flip(): return lax.ppermute(value, axis, [(0, 1), (1, 0)])  9.62 us
    ppermute x7, starting transfers between devices, flip(): return lax.ppermute(value, axis, [(0, 1), (1, 0)])  8.96 us
    pallas_call x2, Pallas kernels, per_device(): pl.pallas_call(lambda *refs, steps=steps: attend_kernel(steps, True, *ref...  7.99 us
    pallas_call x1, Pallas kernels, per_device(): pl.pallas_call(lambda *refs: attend_kernel(STEPS, False, *refs), out_shap...  6.56 us
    ppermute x1, waiting for transfers between devices, per_device(): v_far = lax.ppermute(pair[feats:], ('z', 'yh'), slant)  4.67 us
    pallas_call x1, Pallas kernels, per_device(): pl.pallas_call(prepare_kernel, out_shape=[jax.ShapeDtypeStruct((size, TOK...  3.56 us
  transfers between devices with their start and end apart: 17, of which 8 were waited for; matrix products, arithmetic and copies ran while one was open for 2% of the time, Pallas kernels for 15%

profile of v2, /device:TPU:1, one launch (start us, length us, event | category | flops | bytes accessed | tf_op | source)
XLA Modules:
  0.0 88.2 jit_solution(3581048906211287829)
XLA Ops:
  0.0 3.6 %prepare.1 = (bf16[384,512]{1,0:T(8,128)(2,1)}, bf16[768,512]{1,0:T(8,128)(2,1)}) custom-call(s32[12]{0:T(128)} %refs_0_.5, bf16[512,384]{1,0:T(8,128)(2,1)} %q_hbm.1, bf16[512,384]{1,0:T(8,128)(2,1)} %k_hbm.1, bf16[512,384]{1,0:T(8,128)(2,1)} %v_hbm.1, f32[2,256,128]{2,1,0:T(8,128)} %constant.28.clone.space_hbm, f32[2,16,128]{2,1,0:T(8,128)} %constant.29.clone.time_hbm, ...), custom_call_target="tpu_custom_call" | custom-call | flops 200000000 | bytes 3000000 | tf_op jit(solution)/shard_map/prepare/pallas_call | solution.py:350
  3.6 0.0 copy-start.2
  3.6 2.1 %collective-permute-start.3 = (bf16[384,512]{1,0:T(8,128)(2,1)}, bf16[384,512]{1,0:T(8,128)(2,1)S(1)}, u32[]{:S(2)}, u32[]{:S(2)}) collective-permute-start(bf16[384,512]{1,0:T(8,128)(2,1)} %get-tuple-element.30.q_hbm), channel_id=1, source_target_pairs={{0,4},{4,8},{8,12},{12,0},{1,5},{5,9},{9,13},{13,1},{2,6},{6,10},{... | collective-permute-start | bytes 1179656 | tf_op jit(solution)/shard_map/ppermute | solution.py:339
  5.7 1.4 %collective-permute-start.4 = (bf16[384,512]{1,0:T(8,128)(2,1)}, bf16[384,512]{1,0:T(8,128)(2,1)}, u32[]{:S(2)}, u32[]{:S(2)}) collective-permute-start(bf16[384,512]{1,0:T(8,128)(2,1)} %get-tuple-element.30.q_hbm), channel_id=1, source_target_pairs={{0,12},{4,0},{8,4},{12,8},{1,13},{5,1},{9,5},{13,9},{2,14},{6,2},{... | collective-permute-start | bytes 1179656 | tf_op jit(solution)/shard_map/ppermute | solution.py:339
  7.0 3.0 %collective-permute-start = (bf16[768,512]{1,0:T(8,128)(2,1)}, bf16[768,512]{1,0:T(8,128)(2,1)S(1)}, u32[]{:S(2)}, u32[]{:S(2)}) collective-permute-start(bf16[768,512]{1,0:T(8,128)(2,1)} %get-tuple-element.29.kv_hbm), channel_id=1, source_target_pairs={{0,16},{16,0},{1,17},{17,1},{2,18},{18,2},{3,19},{19,3},{4,20},{20... | collective-permute-start | bytes 2359304 | tf_op jit(solution)/shard_map/ppermute | solution.py:343
  10.1 1.6 %collective-permute-start.1 = (bf16[768,512]{1,0:T(8,128)(2,1)}, bf16[768,512]{1,0:T(8,128)(2,1)S(1)}, u32[]{:S(2)}, u32[]{:S(2)}) collective-permute-start(bf16[768,512]{1,0:T(8,128)(2,1)} %get-tuple-element.29.kv_hbm), channel_id=1, source_target_pairs={{0,32},{32,64},{64,96},{96,128},{128,160},{160,192},{192,224},{224... | collective-permute-start | bytes 2359304 | tf_op jit(solution)/shard_map/ppermute | solution.py:339
  11.7 3.9 %collective-permute-start.2 = (bf16[768,512]{1,0:T(8,128)(2,1)}, bf16[768,512]{1,0:T(8,128)(2,1)S(1)}, u32[]{:S(2)}, u32[]{:S(2)}) collective-permute-start(bf16[768,512]{1,0:T(8,128)(2,1)} %get-tuple-element.29.kv_hbm), channel_id=1, source_target_pairs={{0,224},{32,0},{64,32},{96,64},{128,96},{160,128},{192,160},{224,1... | collective-permute-start | bytes 2359304 | tf_op jit(solution)/shard_map/ppermute | solution.py:339
  15.6 1.9 %constant_dynamic-slice_fusion.3 = bf16[384,768]{1,0:T(8,128)(2,1)} fusion(bf16[384,3072]{1,0:T(8,128)(2,1)} %param.12, s32[]{:T(128)S(6)} %select_n.20), kind=kLoop, calls=%fused_computation.4 | loop fusion | bytes 1179652 | tf_op jit(solution)/shard_map/dynamic_slice | solution.py:391
  17.6 0.0 collective-permute-done.3.refs_2_.refs_1_
  17.6 1.8 %collective-permute-start.6 = (bf16[384,768]{1,0:T(8,128)(2,1)}, bf16[384,768]{1,0:T(8,128)(2,1)S(1)}, u32[]{:S(2)}, u32[]{:S(2)}) collective-permute-start(bf16[384,768]{1,0:T(8,128)(2,1)} %constant_dynamic-slice_fusion.3), channel_id=1, source_target_pairs={{0,1},{1,0},{2,3},{3,2},{4,5},{5,4},{6,7},{7,6},{8,9},{9,8},{10,11... | collective-permute-start | bytes 1769480 | tf_op jit(solution)/shard_map/ppermute | solution.py:343
  19.4 0.0 collective-permute-done.4.refs_3_.refs_2_
  19.4 1.6 %collective-permute-start.5 = (bf16[384,512]{1,0:T(8,128)(2,1)}, bf16[384,512]{1,0:T(8,128)(2,1)}, u32[]{:S(2)}, u32[]{:S(2)}) collective-permute-start(bf16[384,512]{1,0:T(8,128)(2,1)} %get-tuple-element.30.q_hbm), channel_id=1, source_target_pairs={{0,8},{4,12},{8,0},{12,4},{1,9},{5,13},{9,1},{13,5},{2,10},{6,14},... | collective-permute-start | bytes 1179656 | tf_op jit(solution)/shard_map/ppermute | solution.py:339
  21.0 0.0 copy-start
  21.0 1.1 %copy-done = bf16[768,512]{1,0:T(8,128)(2,1)S(1)} copy-done((bf16[768,512]{1,0:T(8,128)(2,1)S(1)}, bf16[768,512]{1,0:T(8,128)(2,1)}, u32[]{:S(2)}) %copy-start) | copy-done | bytes 786456
  22.1 0.0 copy-start.1
  22.1 1.0 %copy-done.1 = bf16[384,512]{1,0:T(8,128)(2,1)S(1)} copy-done((bf16[384,512]{1,0:T(8,128)(2,1)S(1)}, bf16[384,512]{1,0:T(8,128)(2,1)}, u32[]{:S(2)}) %copy-start.1) | copy-done | bytes 393240
  23.1 0.3 stage.1
  23.3 8.6 %collective-permute-done.5.refs_4_.refs_1_ = bf16[384,512]{1,0:T(8,128)(2,1)} collective-permute-done((bf16[384,512]{1,0:T(8,128)(2,1)}, bf16[384,512]{1,0:T(8,128)(2,1)}, u32[]{:S(2)}, u32[]{:S(2)}) %collective-permute-start.5) | collective-permute-done | bytes 393248 | tf_op jit(solution)/shard_map/ppermute | solution.py:339
  31.9 0.0 collective-permute-done.6.refs_3_
  31.9 0.0 collective-permute-done.refs_3_
  31.9 0.4 collective-permute-done.1.refs_5_
  32.3 0.0 collective-permute-done.2.refs_7_
  32.4 0.6 collective-permute-start.7
  33.0 1.9 %collective-permute-start.8 = (bf16[384,512]{1,0:T(8,128)(2,1)S(1)}, bf16[384,512]{1,0:T(8,128)(2,1)S(1)}, u32[]{:S(2)}, u32[]{:S(2)}) collective-permute-start(bf16[384,512]{1,0:T(8,128)(2,1)S(1)} %slice.11), channel_id=1, source_target_pairs={{0,32},{32,64},{64,96},{96,128},{128,160},{160,192},{192,224},{224... | collective-permute-start | bytes 1179656 | tf_op jit(solution)/shard_map/ppermute | solution.py:399
  34.9 0.0 copy-done.2
  34.9 6.6 %attend_near.1.refs_6_ = f32[4,408,512]{2,1,0:T(8,128)S(1)} custom-call(s32[12]{0:T(128)S(1)} %copy-done.2, bf16[384,512]{1,0:T(8,128)(2,1)S(1)} %get-tuple-element.34.refs_1_.refs_2_, bf16[384,512]{1,0:T(8,128)(2,1)S(1)} %collective-permute-done.3.refs_2_.refs_1_, bf16[384,512]{1,0:T(8,128)(2,1)} %collective-permute-done.4.refs_3_.refs_2_, ...), custom_call_target="tpu_custom_call" | custom-call | flops 7000000000 | bytes 5000000 | tf_op jit(solution)/shard_map/attend_near/pallas_call | solution.py:404
  41.5 1.0 %collective-permute-done.7.refs_4_ = bf16[384,512]{1,0:T(8,128)(2,1)S(1)} collective-permute-done((bf16[384,512]{1,0:T(8,128)(2,1)S(1)}, bf16[384,512]{1,0:T(8,128)(2,1)S(1)}, u32[]{:S(2)}, u32[]{:S(2)}) %collective-permute-start.7) | collective-permute-done | bytes 393248 | tf_op jit(solution)/shard_map/ppermute | solution.py:343
  42.5 4.7 %collective-permute-done.8.refs_5_ = bf16[384,512]{1,0:T(8,128)(2,1)S(1)} collective-permute-done((bf16[384,512]{1,0:T(8,128)(2,1)S(1)}, bf16[384,512]{1,0:T(8,128)(2,1)S(1)}, u32[]{:S(2)}, u32[]{:S(2)}) %collective-permute-start.8) | collective-permute-done | bytes 393248 | tf_op jit(solution)/shard_map/ppermute | solution.py:399
  47.2 3.9 %attend_far.2 = (bf16[400,512]{1,0:T(8,128)(2,1)S(1)}, bf16[400,512]{1,0:T(8,128)(2,1)S(1)}) custom-call(s32[12]{0:T(128)S(1)} %copy-done.2, bf16[384,512]{1,0:T(8,128)(2,1)} %collective-permute-done.5.refs_4_.refs_1_, bf16[384,512]{1,0:T(8,128)(2,1)S(1)} %get-tuple-element.34.refs_1_.refs_2_, bf16[768,512]{1,0:T(8,128)(2,1)S(1)} %collective-permute-done.refs_3_, ...), custom_call_target="tpu_custom_call" | custom-call | flops 5500000256 | bytes 3000000 | tf_op jit(solution)/shard_map/attend_far/pallas_call | solution.py:420
  51.1 0.0 copy-start.3
  51.1 0.1 collective-permute-start.9
  51.2 4.1 %attend_far.3 = (bf16[400,512]{1,0:T(8,128)(2,1)S(1)}, bf16[400,512]{1,0:T(8,128)(2,1)S(1)}) custom-call(s32[12]{0:T(128)S(1)} %copy-done.2, bf16[384,512]{1,0:T(8,128)(2,1)S(1)} %collective-permute-done.3.refs_2_.refs_1_, bf16[384,512]{1,0:T(8,128)(2,1)} %collective-permute-done.4.refs_3_.refs_2_, bf16[768,512]{1,0:T(8,128)(2,1)S(1)} %collective-permute-done.refs_3_, ...), custom_call_target="tpu_custom_call" | custom-call | flops 5500000256 | bytes 3000000 | tf_op jit(solution)/shard_map/attend_far/pallas_call | solution.py:420
  55.3 0.0 copy-done.3
  55.3 0.2 constant_dynamic-slice_fusion
  55.5 0.5 collective-permute-start.14
  56.0 2.1 %collective-permute-start.15 = (bf16[384,768]{1,0:T(8,128)(2,1)S(1)}, bf16[384,768]{1,0:T(8,128)(2,1)S(1)}, u32[]{:S(2)}, u32[]{:S(2)}) collective-permute-start(bf16[384,768]{1,0:T(8,128)(2,1)S(1)} %get-tuple-element.53), channel_id=1, source_target_pairs={{0,19},{1,18},{2,17},{3,16},{16,3},{17,2},{18,1},{19,0},{4,23},{5,... | collective-permute-start | bytes 1769480 | tf_op jit(solution)/shard_map/ppermute | solution.py:437
  58.1 0.9 collective-permute-start.10
  58.9 0.6 collective-permute-start.11
  59.6 2.3 %collective-permute-done.9.p1 = bf16[400,512]{1,0:T(8,128)(2,1)S(1)} collective-permute-done((bf16[400,512]{1,0:T(8,128)(2,1)S(1)}, bf16[400,512]{1,0:T(8,128)(2,1)S(1)}, u32[]{:S(2)}, u32[]{:S(2)}) %collective-permute-start.9) | collective-permute-done | bytes 409632 | tf_op jit(solution)/shard_map/ppermute | solution.py:339
  61.9 0.2 merge_two.1.m
  62.1 6.5 %collective-permute-done.10.p0 = bf16[400,512]{1,0:T(8,128)(2,1)S(1)} collective-permute-done((bf16[400,512]{1,0:T(8,128)(2,1)S(1)}, bf16[400,512]{1,0:T(8,128)(2,1)S(1)}, u32[]{:S(2)}, u32[]{:S(2)}) %collective-permute-start.10) | collective-permute-done | bytes 409632 | tf_op jit(solution)/shard_map/ppermute | solution.py:339
  68.6 4.1 %collective-permute-done.11.p1 = bf16[400,512]{1,0:T(8,128)(2,1)S(1)} collective-permute-done((bf16[400,512]{1,0:T(8,128)(2,1)S(1)}, bf16[400,512]{1,0:T(8,128)(2,1)S(1)}, u32[]{:S(2)}, u32[]{:S(2)}) %collective-permute-start.11) | collective-permute-done | bytes 409632 | tf_op jit(solution)/shard_map/ppermute | solution.py:339
  72.7 0.4 merge_last.1.refs_0_
  73.1 0.5 collective-permute-start.13
  73.5 1.0 %collective-permute-start.12 = (bf16[512,384]{1,0:T(8,128)(2,1)S(1)}, bf16[512,384]{1,0:T(8,128)(2,1)S(1)}, u32[]{:S(2)}, u32[]{:S(2)}) collective-permute-start(bf16[512,384]{1,0:T(8,128)(2,1)S(1)} %merge_last.1.refs_0_), channel_id=1, source_target_pairs={{0,1},{1,0},{2,3},{3,2},{4,5},{5,4},{6,7},{7,6},{8,9},{9,8},{10,11... | collective-permute-start | bytes 1179656 | tf_op jit(solution)/shard_map/ppermute | solution.py:343
  74.5 0.0 collective-permute-done.14.refs_2_
  74.5 0.0 collective-permute-done.15.refs_2_
  74.5 8.6 %collective-permute-done.13.refs_1_ = bf16[512,384]{1,0:T(8,128)(2,1)S(1)} collective-permute-done((bf16[512,384]{1,0:T(8,128)(2,1)S(1)}, bf16[512,384]{1,0:T(8,128)(2,1)S(1)}, u32[]{:S(2)}, u32[]{:S(2)}) %collective-permute-start.13) | collective-permute-done | bytes 393248 | tf_op jit(solution)/shard_map/ppermute | solution.py:343
  83.1 1.6 %collective-permute-start.16 = (bf16[512,384]{1,0:T(8,128)(2,1)S(1)}, bf16[512,384]{1,0:T(8,128)(2,1)S(1)}, u32[]{:S(2)}, u32[]{:S(2)}) collective-permute-start(bf16[512,384]{1,0:T(8,128)(2,1)S(1)} %collective-permute-done.13.refs_1_), channel_id=1, source_target_pairs={{0,1},{1,0},{2,3},{3,2},{4,5},{5,4},{6,7},{7,6},{8,9},{9,8},{10,11... | collective-permute-start | bytes 1179656 | tf_op jit(solution)/shard_map/ppermute | solution.py:343
  84.7 0.0 collective-permute-done.12.refs_2_
  84.7 1.2 %project.3.refs_0_ = f32[512,768]{1,0:T(8,128)S(1)} custom-call(bf16[512,384]{1,0:T(8,128)(2,1)S(1)} %merge_last.1.refs_0_, bf16[384,768]{1,0:T(8,128)(2,1)S(1)} %get-tuple-element.55.refs_1_, bf16[512,384]{1,0:T(8,128)(2,1)S(1)} %collective-permute-done.12.refs_2_, bf16[384,768]{1,0:T(8,128)(2,1)S(1)} %collective-permute-done.6.refs_3_), custom_call_target="tpu_custom_call" | custom-call | flops 1200000000 | bytes 1000000 | tf_op jit(solution)/shard_map/project/pallas_call | solution.py:470
  85.9 0.8 project.4.refs_0_
  86.6 0.0 collective-permute-done.16.refs_1_
  86.6 1.5 %project.5 = bf16[512,768]{1,0:T(8,128)(2,1)} custom-call(f32[512,768]{1,0:T(8,128)S(1)} %project.4.refs_0_, bf16[512,384]{1,0:T(8,128)(2,1)S(1)} %collective-permute-done.16.refs_1_, bf16[384,768]{1,0:T(8,128)(2,1)S(1)} %collective-permute-done.15.refs_2_), custom_call_target="tpu_custom_call" | custom-call | flops 600000000 | bytes 1000000 | tf_op jit(solution)/shard_map/project/pallas_call | solution.py:470
  (2 shorter events, 0.1 us)
Async XLA Ops:
  3.6 31.4 %copy-start.2 = (s32[12]{0:T(128)S(1)}, s32[12]{0:T(128)}, u32[]{:S(2)}) copy-start(s32[12]{0:T(128)} %refs_0_.5) | copy-start | bytes 148
  3.6 14.0 %collective-permute-start.3 = (bf16[384,512]{1,0:T(8,128)(2,1)}, bf16[384,512]{1,0:T(8,128)(2,1)S(1)}, u32[]{:S(2)}, u32[]{:S(2)}) collective-permute-start(bf16[384,512]{1,0:T(8,128)(2,1)} %get-tuple-element.30.q_hbm), channel_id=1, source_target_pairs={{0,4},{4,8},{8,12},{12,0},{1,5},{5,9},{9,13},{13,1},{2,6},{6,10},{... | collective-permute-start | bytes 1179656 | tf_op jit(solution)/shard_map/ppermute | solution.py:339
  5.7 13.7 %collective-permute-start.4 = (bf16[384,512]{1,0:T(8,128)(2,1)}, bf16[384,512]{1,0:T(8,128)(2,1)}, u32[]{:S(2)}, u32[]{:S(2)}) collective-permute-start(bf16[384,512]{1,0:T(8,128)(2,1)} %get-tuple-element.30.q_hbm), channel_id=1, source_target_pairs={{0,12},{4,0},{8,4},{12,8},{1,13},{5,1},{9,5},{13,9},{2,14},{6,2},{... | collective-permute-start | bytes 1179656 | tf_op jit(solution)/shard_map/ppermute | solution.py:339
  7.0 24.9 %collective-permute-start = (bf16[768,512]{1,0:T(8,128)(2,1)}, bf16[768,512]{1,0:T(8,128)(2,1)S(1)}, u32[]{:S(2)}, u32[]{:S(2)}) collective-permute-start(bf16[768,512]{1,0:T(8,128)(2,1)} %get-tuple-element.29.kv_hbm), channel_id=1, source_target_pairs={{0,16},{16,0},{1,17},{17,1},{2,18},{18,2},{3,19},{19,3},{4,20},{20... | collective-permute-start | bytes 2359304 | tf_op jit(solution)/shard_map/ppermute | solution.py:343
  10.1 22.2 %collective-permute-start.1 = (bf16[768,512]{1,0:T(8,128)(2,1)}, bf16[768,512]{1,0:T(8,128)(2,1)S(1)}, u32[]{:S(2)}, u32[]{:S(2)}) collective-permute-start(bf16[768,512]{1,0:T(8,128)(2,1)} %get-tuple-element.29.kv_hbm), channel_id=1, source_target_pairs={{0,32},{32,64},{64,96},{96,128},{128,160},{160,192},{192,224},{224... | collective-permute-start | bytes 2359304 | tf_op jit(solution)/shard_map/ppermute | solution.py:339
  11.7 20.6 %collective-permute-start.2 = (bf16[768,512]{1,0:T(8,128)(2,1)}, bf16[768,512]{1,0:T(8,128)(2,1)S(1)}, u32[]{:S(2)}, u32[]{:S(2)}) collective-permute-start(bf16[768,512]{1,0:T(8,128)(2,1)} %get-tuple-element.29.kv_hbm), channel_id=1, source_target_pairs={{0,224},{32,0},{64,32},{96,64},{128,96},{160,128},{192,160},{224,1... | collective-permute-start | bytes 2359304 | tf_op jit(solution)/shard_map/ppermute | solution.py:339
  17.6 14.3 %collective-permute-start.6 = (bf16[384,768]{1,0:T(8,128)(2,1)}, bf16[384,768]{1,0:T(8,128)(2,1)S(1)}, u32[]{:S(2)}, u32[]{:S(2)}) collective-permute-start(bf16[384,768]{1,0:T(8,128)(2,1)} %constant_dynamic-slice_fusion.3), channel_id=1, source_target_pairs={{0,1},{1,0},{2,3},{3,2},{4,5},{5,4},{6,7},{7,6},{8,9},{9,8},{10,11... | collective-permute-start | bytes 1769480 | tf_op jit(solution)/shard_map/ppermute | solution.py:343
  19.4 12.5 %collective-permute-start.5 = (bf16[384,512]{1,0:T(8,128)(2,1)}, bf16[384,512]{1,0:T(8,128)(2,1)}, u32[]{:S(2)}, u32[]{:S(2)}) collective-permute-start(bf16[384,512]{1,0:T(8,128)(2,1)} %get-tuple-element.30.q_hbm), channel_id=1, source_target_pairs={{0,8},{4,12},{8,0},{12,4},{1,9},{5,13},{9,1},{13,5},{2,10},{6,14},... | collective-permute-start | bytes 1179656 | tf_op jit(solution)/shard_map/ppermute | solution.py:339
  21.0 1.1 %copy-start = (bf16[768,512]{1,0:T(8,128)(2,1)S(1)}, bf16[768,512]{1,0:T(8,128)(2,1)}, u32[]{:S(2)}) copy-start(bf16[768,512]{1,0:T(8,128)(2,1)} %get-tuple-element.29.kv_hbm) | copy-start | bytes 2359300
  22.1 1.0 %copy-start.1 = (bf16[384,512]{1,0:T(8,128)(2,1)S(1)}, bf16[384,512]{1,0:T(8,128)(2,1)}, u32[]{:S(2)}) copy-start(bf16[384,512]{1,0:T(8,128)(2,1)} %get-tuple-element.30.q_hbm) | copy-start | bytes 1179652
  32.4 10.1 %collective-permute-start.7 = (bf16[384,512]{1,0:T(8,128)(2,1)S(1)}, bf16[384,512]{1,0:T(8,128)(2,1)S(1)}, u32[]{:S(2)}, u32[]{:S(2)}) collective-permute-start(bf16[384,512]{1,0:T(8,128)(2,1)S(1)} %slice_select_fusion), channel_id=1, source_target_pairs={{0,16},{16,0},{1,17},{17,1},{2,18},{18,2},{3,19},{19,3},{4,20},{20... | collective-permute-start | bytes 1179656 | tf_op jit(solution)/shard_map/ppermute | solution.py:343
  33.0 14.1 %collective-permute-start.8 = (bf16[384,512]{1,0:T(8,128)(2,1)S(1)}, bf16[384,512]{1,0:T(8,128)(2,1)S(1)}, u32[]{:S(2)}, u32[]{:S(2)}) collective-permute-start(bf16[384,512]{1,0:T(8,128)(2,1)S(1)} %slice.11), channel_id=1, source_target_pairs={{0,32},{32,64},{64,96},{96,128},{128,160},{160,192},{192,224},{224... | collective-permute-start | bytes 1179656 | tf_op jit(solution)/shard_map/ppermute | solution.py:399
  51.1 4.2 %copy-start.3 = (bf16[384,3072]{1,0:T(8,128)(2,1)S(1)}, bf16[384,3072]{1,0:T(8,128)(2,1)}, u32[]{:S(2)}) copy-start(bf16[384,3072]{1,0:T(8,128)(2,1)} %param.12) | copy-start | bytes 7077892
  51.1 10.8 %collective-permute-start.9 = (bf16[400,512]{1,0:T(8,128)(2,1)S(1)}, bf16[400,512]{1,0:T(8,128)(2,1)S(1)}, u32[]{:S(2)}, u32[]{:S(2)}) collective-permute-start(bf16[400,512]{1,0:T(8,128)(2,1)S(1)} %get-tuple-element.43), channel_id=1, source_target_pairs={{0,8},{4,12},{8,0},{12,4},{1,9},{5,13},{9,1},{13,5},{2,10},{6,14},... | collective-permute-start | bytes 1228808 | tf_op jit(solution)/shard_map/ppermute | solution.py:339
  55.5 19.0 %collective-permute-start.14 = (bf16[384,768]{1,0:T(8,128)(2,1)S(1)}, bf16[384,768]{1,0:T(8,128)(2,1)S(1)}, u32[]{:S(2)}, u32[]{:S(2)}) collective-permute-start(bf16[384,768]{1,0:T(8,128)(2,1)S(1)} %get-tuple-element.54), channel_id=1, source_target_pairs={{0,2},{2,0},{1,3},{3,1},{4,6},{6,4},{5,7},{7,5},{8,10},{10,8},{9,1... | collective-permute-start | bytes 1769480 | tf_op jit(solution)/shard_map/ppermute | solution.py:343
  56.0 18.6 %collective-permute-start.15 = (bf16[384,768]{1,0:T(8,128)(2,1)S(1)}, bf16[384,768]{1,0:T(8,128)(2,1)S(1)}, u32[]{:S(2)}, u32[]{:S(2)}) collective-permute-start(bf16[384,768]{1,0:T(8,128)(2,1)S(1)} %get-tuple-element.53), channel_id=1, source_target_pairs={{0,19},{1,18},{2,17},{3,16},{16,3},{17,2},{18,1},{19,0},{4,23},{5,... | collective-permute-start | bytes 1769480 | tf_op jit(solution)/shard_map/ppermute | solution.py:437
  58.1 10.5 %collective-permute-start.10 = (bf16[400,512]{1,0:T(8,128)(2,1)S(1)}, bf16[400,512]{1,0:T(8,128)(2,1)S(1)}, u32[]{:S(2)}, u32[]{:S(2)}) collective-permute-start(bf16[400,512]{1,0:T(8,128)(2,1)S(1)} %get-tuple-element.46), channel_id=1, source_target_pairs={{0,12},{4,0},{8,4},{12,8},{1,13},{5,1},{9,5},{13,9},{2,14},{6,2},{... | collective-permute-start | bytes 1228808 | tf_op jit(solution)/shard_map/ppermute | solution.py:339
  58.9 13.8 %collective-permute-start.11 = (bf16[400,512]{1,0:T(8,128)(2,1)S(1)}, bf16[400,512]{1,0:T(8,128)(2,1)S(1)}, u32[]{:S(2)}, u32[]{:S(2)}) collective-permute-start(bf16[400,512]{1,0:T(8,128)(2,1)S(1)} %get-tuple-element.47), channel_id=1, source_target_pairs={{0,4},{4,8},{8,12},{12,0},{1,5},{5,9},{9,13},{13,1},{2,6},{6,10},{... | collective-permute-start | bytes 1228808 | tf_op jit(solution)/shard_map/ppermute | solution.py:339
  73.1 10.1 %collective-permute-start.13 = (bf16[512,384]{1,0:T(8,128)(2,1)S(1)}, bf16[512,384]{1,0:T(8,128)(2,1)S(1)}, u32[]{:S(2)}, u32[]{:S(2)}) collective-permute-start(bf16[512,384]{1,0:T(8,128)(2,1)S(1)} %merge_last.1.refs_0_), channel_id=1, source_target_pairs={{0,2},{2,0},{1,3},{3,1},{4,6},{6,4},{5,7},{7,5},{8,10},{10,8},{9,1... | collective-permute-start | bytes 1179656 | tf_op jit(solution)/shard_map/ppermute | solution.py:343
  73.5 11.1 %collective-permute-start.12 = (bf16[512,384]{1,0:T(8,128)(2,1)S(1)}, bf16[512,384]{1,0:T(8,128)(2,1)S(1)}, u32[]{:S(2)}, u32[]{:S(2)}) collective-permute-start(bf16[512,384]{1,0:T(8,128)(2,1)S(1)} %merge_last.1.refs_0_), channel_id=1, source_target_pairs={{0,1},{1,0},{2,3},{3,2},{4,5},{5,4},{6,7},{7,6},{8,9},{9,8},{10,11... | collective-permute-start | bytes 1179656 | tf_op jit(solution)/shard_map/ppermute | solution.py:343
  83.1 3.5 %collective-permute-start.16 = (bf16[512,384]{1,0:T(8,128)(2,1)S(1)}, bf16[512,384]{1,0:T(8,128)(2,1)S(1)}, u32[]{:S(2)}, u32[]{:S(2)}) collective-permute-start(bf16[512,384]{1,0:T(8,128)(2,1)S(1)} %collective-permute-done.13.refs_1_), channel_id=1, source_target_pairs={{0,1},{1,0},{2,3},{3,2},{4,5},{5,4},{6,7},{7,6},{8,9},{9,8},{10,11... | collective-permute-start | bytes 1179656 | tf_op jit(solution)/shard_map/ppermute | solution.py:343

commit v3 on v2

--- a/solution.py
+++ b/solution.py
@@ -25,7 +25,8 @@
 EXP_SCALE = HEAD_DIM ** (-0.5) * math.log2(math.e)
 
 STEPS = (0, -1, 1, 2)
-CALLS = ((3, 0), (1, 2))
+CALLS = ((3,), (1, 2), (0,))
+COSTS = {0: 2, 1: 5, 3: 0.01}
 
 
 def rope_tables():
@@ -114,7 +115,7 @@
     for e, h, tok, col in parts:
         cos, sin = tables[e]
         k = k_ref[tok, col]
-        rot = ((k.astype(jnp.float32) * cos + dot_nn(k, swap) * sin) * EXP_SCALE).astype(jnp.bfloat16)
+        rot = (k.astype(jnp.float32) * cos + dot_nn(k, swap) * sin).astype(jnp.bfloat16)
         kv_buf[col, FRAME * e : FRAME * e + 128] = rot[:128]
         kv_buf[col, FRAME * e + 128 : FRAME * e + 256] = rot[128:]
     outs = [pltpu.make_async_copy(kv_buf.at[pl.ds(0, HEADS * HEAD_DIM)], kv_out.at[pl.ds(0, HEADS * HEAD_DIM)], sem.at[6])]
@@ -216,7 +217,7 @@
         lo = FRAME * sl
         keys = jnp.concatenate([kv[src, row, lo : lo + 128], kv[src, row, lo + 128 : lo + 256]], axis=0)
         s = dot_nn(keys, q_refs[r][row, FRAME * e : FRAME * (e + 1)])
-        peak = fold(s, jnp.maximum) + bias
+        peak = fold(s, jnp.maximum) * EXP_SCALE + bias
         st = state.setdefault(u, {"s": {}})
         st["s"][sl] = s
         st["top"] = peak if sl == 0 else jnp.maximum(st["top"], peak)
@@ -226,7 +227,7 @@
         places, some = tables[2 * r + e]
         src, bias, _ = places[sl]
         st = state[u]
-        p = jnp.exp2(st["s"].pop(sl) + jnp.where(some, bias - st["top"], NEG))
+        p = jnp.exp2(st["s"].pop(sl) * EXP_SCALE + jnp.where(some, bias - st["top"], NEG))
         add = fold(p, jnp.add)
         row = slice(HEAD_DIM * (n + a), HEAD_DIM * (n + a + 1))
         term = dot_nn(kv[src, row, FRAME * sl : FRAME * (sl + 1)], p.astype(jnp.bfloat16))
@@ -424,14 +425,14 @@
             out_specs=[VMEM] * count,
             scratch_shapes=[pltpu.VMEM((2, 2 * feats, TOK), jnp.bfloat16)],
             compiler_params=params(24),
-            cost_estimate=cost((1 + 2 * count) * 1_100_000_000, 3_000_000, count * 800_000),
+            cost_estimate=cost(int(COSTS[len(partial)] * 1e9), 100_000),
             name="attend_far",
         )(frame_counts, *[qs[r] for r in block], pair, k_far, v_far, near)
         partial.update(zip(block, done))
         if block != CALLS[-1]:
             near, partial[block[0]] = lax.optimization_barrier((near, partial[block[0]]))
 
-    out_weight, partial[1] = lax.optimization_barrier((out_weight, partial[1]))
+    out_weight, partial[0] = lax.optimization_barrier((out_weight, partial[0]))
     w_own = mine(tp)
     w_yl = flip(mine(tp ^ 2), "yl")
     w_far = lax.ppermute(mine(tp ^ 3), ("yh", "yl", "core"), [(i, 7 - i) for i in range(8)])

time: 88.5 us -> 86.6 us (0.979)
  waiting for transfers between devices: 36.2 us -> 28.9 us
  starting transfers between devices: 25.1 us -> 28.8 us
  Pallas kernels: 22.4 us -> 24.2 us
    ppermute x8, waiting for transfers between devices: 21.9 us -> 16.6 us  [shift(): lax.ppermute(value, axis, [(i, (i + by) % count) for i in range(count)])]
    ppermute x7, waiting for transfers between devices: 9.62 us -> 5.69 us  [flip(): return lax.ppermute(value, axis, [(0, 1), (1, 0)])]
    ppermute x7, starting transfers between devices: 8.96 us -> 11.2 us  [flip(): return lax.ppermute(value, axis, [(0, 1), (1, 0)])]
    ppermute x1, waiting for transfers between devices: 0.01 us -> 1.86 us  [per_device(): lax.ppermute(mine(tp ^ 3), ('yh', 'yl', 'core'), [(i, 7 - i) for i in ran...]
    pallas_call x2 -> x3, Pallas kernels: 7.99 us -> 9.3 us  [per_device(): pl.pallas_call(lambda *refs, steps=steps: attend_kernel(steps, True, *ref...]
    ppermute x1, starting transfers between devices: 2.12 us -> 3.29 us  [per_device(): lax.ppermute(mine(tp ^ 3), ('yh', 'yl', 'core'), [(i, 7 - i) for i in ran...]
  transfers between devices with their start and end apart: 17 -> 17, of which waited for: 8 -> 8; matrix products, arithmetic and copies ran while one was open for 2% -> 2% of each run, Pallas kernels for 15% -> 19%
where the time goes in v3:
time: 86.6 us; the launch traced here: 86.2 us
  waiting for transfers between devices  28.9 us (33%)
  starting transfers between devices  28.8 us (33%)
  Pallas kernels  24.2 us (28%)
  local copies, waits for them, and re-layouts  4.26 us (5%)
    ppermute x8, waiting for transfers between devices, shift(): lax.ppermute(value, axis, [(i, (i + by) % count) for i in range(count)])  16.6 us
    ppermute x8, starting transfers between devices, shift(): lax.ppermute(value, axis, [(i, (i + by) % count) for i in range(count)])  12.4 us
    ppermute x7, starting transfers between devices, flip(): return lax.ppermute(value, axis, [(0, 1), (1, 0)])  11.2 us
    pallas_call x3, Pallas kernels, per_device(): pl.pallas_call(lambda *refs, steps=steps: attend_kernel(steps, True, *ref...  9.3 us
    pallas_call x1, Pallas kernels, per_device(): pl.pallas_call(lambda *refs: attend_kernel(STEPS, False, *refs), out_shap...  7.05 us
    ppermute x7, waiting for transfers between devices, flip(): return lax.ppermute(value, axis, [(0, 1), (1, 0)])  5.69 us
    ppermute x1, waiting for transfers between devices, per_device(): v_far = lax.ppermute(pair[feats:], ('z', 'yh'), slant)  4.69 us
    pallas_call x1, Pallas kernels, per_device(): pl.pallas_call(prepare_kernel, out_shape=[jax.ShapeDtypeStruct((size, TOK...  3.53 us
  transfers between devices with their start and end apart: 17, of which 8 were waited for; matrix products, arithmetic and copies ran while one was open for 2% of the time, Pallas kernels for 19%

profile of v3, /device:TPU:1, one launch (start us, length us, event | category | flops | bytes accessed | tf_op | source)
XLA Modules:
  0.0 86.2 jit_solution(5587265890575346290)
XLA Ops:
  0.0 3.5 %prepare.1 = (bf16[384,512]{1,0:T(8,128)(2,1)}, bf16[768,512]{1,0:T(8,128)(2,1)}) custom-call(s32[12]{0:T(128)} %refs_0_.7, bf16[512,384]{1,0:T(8,128)(2,1)} %q_hbm.1, bf16[512,384]{1,0:T(8,128)(2,1)} %k_hbm.1, bf16[512,384]{1,0:T(8,128)(2,1)} %v_hbm.1, f32[2,256,128]{2,1,0:T(8,128)} %constant.28.clone.space_hbm, f32[2,16,128]{2,1,0:T(8,128)} %constant.29.clone.time_hbm, ...), custom_call_target="tpu_custom_call" | custom-call | flops 200000000 | bytes 3000000 | tf_op jit(solution)/shard_map/prepare/pallas_call | solution.py:351
  3.5 0.0 copy-start.2
  3.6 2.1 %collective-permute-start.3 = (bf16[384,512]{1,0:T(8,128)(2,1)}, bf16[384,512]{1,0:T(8,128)(2,1)S(1)}, u32[]{:S(2)}, u32[]{:S(2)}) collective-permute-start(bf16[384,512]{1,0:T(8,128)(2,1)} %get-tuple-element.30.q_hbm), channel_id=1, source_target_pairs={{0,4},{4,8},{8,12},{12,0},{1,5},{5,9},{9,13},{13,1},{2,6},{6,10},{... | collective-permute-start | bytes 1179656 | tf_op jit(solution)/shard_map/ppermute | solution.py:340
  5.7 1.3 %collective-permute-start.4 = (bf16[384,512]{1,0:T(8,128)(2,1)}, bf16[384,512]{1,0:T(8,128)(2,1)}, u32[]{:S(2)}, u32[]{:S(2)}) collective-permute-start(bf16[384,512]{1,0:T(8,128)(2,1)} %get-tuple-element.30.q_hbm), channel_id=1, source_target_pairs={{0,12},{4,0},{8,4},{12,8},{1,13},{5,1},{9,5},{13,9},{2,14},{6,2},{... | collective-permute-start | bytes 1179656 | tf_op jit(solution)/shard_map/ppermute | solution.py:340
  7.0 3.0 %collective-permute-start = (bf16[768,512]{1,0:T(8,128)(2,1)}, bf16[768,512]{1,0:T(8,128)(2,1)S(1)}, u32[]{:S(2)}, u32[]{:S(2)}) collective-permute-start(bf16[768,512]{1,0:T(8,128)(2,1)} %get-tuple-element.29.kv_hbm), channel_id=1, source_target_pairs={{0,16},{16,0},{1,17},{17,1},{2,18},{18,2},{3,19},{19,3},{4,20},{20... | collective-permute-start | bytes 2359304 | tf_op jit(solution)/shard_map/ppermute | solution.py:344
  10.1 1.6 %collective-permute-start.1 = (bf16[768,512]{1,0:T(8,128)(2,1)}, bf16[768,512]{1,0:T(8,128)(2,1)S(1)}, u32[]{:S(2)}, u32[]{:S(2)}) collective-permute-start(bf16[768,512]{1,0:T(8,128)(2,1)} %get-tuple-element.29.kv_hbm), channel_id=1, source_target_pairs={{0,32},{32,64},{64,96},{96,128},{128,160},{160,192},{192,224},{224... | collective-permute-start | bytes 2359304 | tf_op jit(solution)/shard_map/ppermute | solution.py:340
  11.7 3.9 %collective-permute-start.2 = (bf16[768,512]{1,0:T(8,128)(2,1)}, bf16[768,512]{1,0:T(8,128)(2,1)S(1)}, u32[]{:S(2)}, u32[]{:S(2)}) collective-permute-start(bf16[768,512]{1,0:T(8,128)(2,1)} %get-tuple-element.29.kv_hbm), channel_id=1, source_target_pairs={{0,224},{32,0},{64,32},{96,64},{128,96},{160,128},{192,160},{224,1... | collective-permute-start | bytes 2359304 | tf_op jit(solution)/shard_map/ppermute | solution.py:340
  15.6 1.9 %constant_dynamic-slice_fusion.3 = bf16[384,768]{1,0:T(8,128)(2,1)} fusion(bf16[384,3072]{1,0:T(8,128)(2,1)} %param.12, s32[]{:T(128)S(6)} %select_n.20), kind=kLoop, calls=%fused_computation.4 | loop fusion | bytes 1179652 | tf_op jit(solution)/shard_map/dynamic_slice | solution.py:392
  17.5 0.0 collective-permute-done.3.refs_2_.refs_1_
  17.5 1.8 %collective-permute-start.6 = (bf16[384,768]{1,0:T(8,128)(2,1)}, bf16[384,768]{1,0:T(8,128)(2,1)S(1)}, u32[]{:S(2)}, u32[]{:S(2)}) collective-permute-start(bf16[384,768]{1,0:T(8,128)(2,1)} %constant_dynamic-slice_fusion.3), channel_id=1, source_target_pairs={{0,1},{1,0},{2,3},{3,2},{4,5},{5,4},{6,7},{7,6},{8,9},{9,8},{10,11... | collective-permute-start | bytes 1769480 | tf_op jit(solution)/shard_map/ppermute | solution.py:344
  19.4 0.0 collective-permute-done.4.refs_3_.refs_2_
  19.4 1.6 %collective-permute-start.5 = (bf16[384,512]{1,0:T(8,128)(2,1)}, bf16[384,512]{1,0:T(8,128)(2,1)}, u32[]{:S(2)}, u32[]{:S(2)}) collective-permute-start(bf16[384,512]{1,0:T(8,128)(2,1)} %get-tuple-element.30.q_hbm), channel_id=1, source_target_pairs={{0,8},{4,12},{8,0},{12,4},{1,9},{5,13},{9,1},{13,5},{2,10},{6,14},... | collective-permute-start | bytes 1179656 | tf_op jit(solution)/shard_map/ppermute | solution.py:340
  20.9 0.0 copy-start
  20.9 1.1 %copy-done = bf16[768,512]{1,0:T(8,128)(2,1)S(1)} copy-done((bf16[768,512]{1,0:T(8,128)(2,1)S(1)}, bf16[768,512]{1,0:T(8,128)(2,1)}, u32[]{:S(2)}) %copy-start) | copy-done | bytes 786456
  22.1 0.0 copy-start.1
  22.1 1.0 %copy-done.1 = bf16[384,512]{1,0:T(8,128)(2,1)S(1)} copy-done((bf16[384,512]{1,0:T(8,128)(2,1)S(1)}, bf16[384,512]{1,0:T(8,128)(2,1)}, u32[]{:S(2)}) %copy-start.1) | copy-done | bytes 393240
  23.0 0.3 stage.1
  23.3 8.6 %collective-permute-done.5.refs_4_.refs_1_ = bf16[384,512]{1,0:T(8,128)(2,1)} collective-permute-done((bf16[384,512]{1,0:T(8,128)(2,1)}, bf16[384,512]{1,0:T(8,128)(2,1)}, u32[]{:S(2)}, u32[]{:S(2)}) %collective-permute-start.5) | collective-permute-done | bytes 393248 | tf_op jit(solution)/shard_map/ppermute | solution.py:340
  31.9 0.0 collective-permute-done.6.refs_3_
  31.9 0.0 collective-permute-done.refs_2_.refs_3_
  31.9 0.4 collective-permute-done.1.refs_5_
  32.3 0.0 collective-permute-done.2.refs_7_
  32.3 0.7 collective-permute-start.7
  33.0 1.9 %collective-permute-start.8 = (bf16[384,512]{1,0:T(8,128)(2,1)S(1)}, bf16[384,512]{1,0:T(8,128)(2,1)S(1)}, u32[]{:S(2)}, u32[]{:S(2)}) collective-permute-start(bf16[384,512]{1,0:T(8,128)(2,1)S(1)} %slice.11), channel_id=1, source_target_pairs={{0,32},{32,64},{64,96},{96,128},{128,160},{160,192},{192,224},{224... | collective-permute-start | bytes 1179656 | tf_op jit(solution)/shard_map/ppermute | solution.py:400
  34.9 0.0 copy-done.2
  34.9 7.0 %attend_near.1.refs_5_.refs_6_ = f32[4,408,512]{2,1,0:T(8,128)S(1)} custom-call(s32[12]{0:T(128)S(1)} %copy-done.2, bf16[384,512]{1,0:T(8,128)(2,1)S(1)} %get-tuple-element.33.refs_1_, bf16[384,512]{1,0:T(8,128)(2,1)S(1)} %collective-permute-done.3.refs_2_.refs_1_, bf16[384,512]{1,0:T(8,128)(2,1)} %collective-permute-done.4.refs_3_.refs_2_, ...), custom_call_target="tpu_custom_call" | custom-call | flops 7000000000 | bytes 5000000 | tf_op jit(solution)/shard_map/attend_near/pallas_call | solution.py:405
  42.0 0.5 collective-permute-done.7.refs_3_.refs_4_
  42.5 4.7 %collective-permute-done.8.refs_4_.refs_5_ = bf16[384,512]{1,0:T(8,128)(2,1)S(1)} collective-permute-done((bf16[384,512]{1,0:T(8,128)(2,1)S(1)}, bf16[384,512]{1,0:T(8,128)(2,1)S(1)}, u32[]{:S(2)}, u32[]{:S(2)}) %collective-permute-start.8) | collective-permute-done | bytes 393248 | tf_op jit(solution)/shard_map/ppermute | solution.py:400
  47.1 2.8 %attend_far.3 = bf16[400,512]{1,0:T(8,128)(2,1)S(1)} custom-call(s32[12]{0:T(128)S(1)} %copy-done.2, bf16[384,512]{1,0:T(8,128)(2,1)} %collective-permute-done.5.refs_4_.refs_1_, bf16[768,512]{1,0:T(8,128)(2,1)S(1)} %collective-permute-done.refs_2_.refs_3_, bf16[384,512]{1,0:T(8,128)(2,1)S(1)} %collective-permute-done.7.refs_3_.refs_4_, ...), custom_call_target="tpu_custom_call" | custom-call | flops 2000000000 | bytes 100000 | tf_op jit(solution)/shard_map/attend_far/pallas_call | solution.py:421
  49.9 0.1 collective-permute-start.9
  50.0 4.2 %attend_far.4 = (bf16[400,512]{1,0:T(8,128)(2,1)S(1)}, bf16[400,512]{1,0:T(8,128)(2,1)S(1)}) custom-call(s32[12]{0:T(128)S(1)} %copy-done.2, bf16[384,512]{1,0:T(8,128)(2,1)S(1)} %collective-permute-done.3.refs_2_.refs_1_, bf16[384,512]{1,0:T(8,128)(2,1)} %collective-permute-done.4.refs_3_.refs_2_, ...), custom_call_target="tpu_custom_call" | custom-call | flops 5000000000 | bytes 100000 | tf_op jit(solution)/shard_map/attend_far/pallas_call | solution.py:421
  54.2 0.0 copy-start.3
  54.2 2.3 %attend_far.5.p0 = bf16[400,512]{1,0:T(8,128)(2,1)S(1)} custom-call(s32[12]{0:T(128)S(1)} %copy-done.2, bf16[384,512]{1,0:T(8,128)(2,1)S(1)} %get-tuple-element.33.refs_1_, bf16[768,512]{1,0:T(8,128)(2,1)S(1)} %collective-permute-done.refs_2_.refs_3_, bf16[384,512]{1,0:T(8,128)(2,1)S(1)} %collective-permute-done.7.refs_3_.refs_4_, ...), custom_call_target="tpu_custom_call" | custom-call | flops 10000000 | bytes 100000 | tf_op jit(solution)/shard_map/attend_far/pallas_call | solution.py:421
  56.6 0.3 collective-permute-start.10
  56.9 1.5 %collective-permute-start.11 = (bf16[400,512]{1,0:T(8,128)(2,1)S(1)}, bf16[400,512]{1,0:T(8,128)(2,1)S(1)}, u32[]{:S(2)}, u32[]{:S(2)}) collective-permute-start(bf16[400,512]{1,0:T(8,128)(2,1)S(1)} %get-tuple-element.47), channel_id=1, source_target_pairs={{0,4},{4,8},{8,12},{12,0},{1,5},{5,9},{9,13},{13,1},{2,6},{6,10},{... | collective-permute-start | bytes 1228808 | tf_op jit(solution)/shard_map/ppermute | solution.py:340
  58.3 0.0 copy-done.3
  58.3 0.2 constant_dynamic-slice_fusion
  58.5 0.5 collective-permute-start.14
  59.0 3.3 %collective-permute-start.15 = (bf16[384,768]{1,0:T(8,128)(2,1)S(1)}, bf16[384,768]{1,0:T(8,128)(2,1)S(1)}, u32[]{:S(2)}, u32[]{:S(2)}) collective-permute-start(bf16[384,768]{1,0:T(8,128)(2,1)S(1)} %get-tuple-element.53), channel_id=1, source_target_pairs={{0,19},{1,18},{2,17},{3,16},{16,3},{17,2},{18,1},{19,0},{4,23},{5,... | collective-permute-start | bytes 1769480 | tf_op jit(solution)/shard_map/ppermute | solution.py:438
  62.3 0.0 collective-permute-done.9.p1
  62.3 0.2 merge_two.1.m
  62.5 2.8 %collective-permute-done.10.p0 = bf16[400,512]{1,0:T(8,128)(2,1)S(1)} collective-permute-done((bf16[400,512]{1,0:T(8,128)(2,1)S(1)}, bf16[400,512]{1,0:T(8,128)(2,1)S(1)}, u32[]{:S(2)}, u32[]{:S(2)}) %collective-permute-start.10) | collective-permute-done | bytes 409632 | tf_op jit(solution)/shard_map/ppermute | solution.py:340
  65.3 4.8 %collective-permute-done.11.p1 = bf16[400,512]{1,0:T(8,128)(2,1)S(1)} collective-permute-done((bf16[400,512]{1,0:T(8,128)(2,1)S(1)}, bf16[400,512]{1,0:T(8,128)(2,1)S(1)}, u32[]{:S(2)}, u32[]{:S(2)}) %collective-permute-start.11) | collective-permute-done | bytes 409632 | tf_op jit(solution)/shard_map/ppermute | solution.py:340
  70.2 0.4 merge_last.1.refs_0_
  70.5 0.5 collective-permute-start.13
  71.0 2.3 %collective-permute-start.12 = (bf16[512,384]{1,0:T(8,128)(2,1)S(1)}, bf16[512,384]{1,0:T(8,128)(2,1)S(1)}, u32[]{:S(2)}, u32[]{:S(2)}) collective-permute-start(bf16[512,384]{1,0:T(8,128)(2,1)S(1)} %merge_last.1.refs_0_), channel_id=1, source_target_pairs={{0,1},{1,0},{2,3},{3,2},{4,5},{5,4},{6,7},{7,6},{8,9},{9,8},{10,11... | collective-permute-start | bytes 1179656 | tf_op jit(solution)/shard_map/ppermute | solution.py:344
  73.3 0.0 collective-permute-done.14.refs_2_
  73.3 1.9 %collective-permute-done.15.refs_2_ = bf16[384,768]{1,0:T(8,128)(2,1)S(1)} collective-permute-done((bf16[384,768]{1,0:T(8,128)(2,1)S(1)}, bf16[384,768]{1,0:T(8,128)(2,1)S(1)}, u32[]{:S(2)}, u32[]{:S(2)}) %collective-permute-start.15) | collective-permute-done | bytes 589856 | tf_op jit(solution)/shard_map/ppermute | solution.py:438
  75.2 5.2 %collective-permute-done.13.refs_1_ = bf16[512,384]{1,0:T(8,128)(2,1)S(1)} collective-permute-done((bf16[512,384]{1,0:T(8,128)(2,1)S(1)}, bf16[512,384]{1,0:T(8,128)(2,1)S(1)}, u32[]{:S(2)}, u32[]{:S(2)}) %collective-permute-start.13) | collective-permute-done | bytes 393248 | tf_op jit(solution)/shard_map/ppermute | solution.py:344
  80.4 2.4 %collective-permute-start.16 = (bf16[512,384]{1,0:T(8,128)(2,1)S(1)}, bf16[512,384]{1,0:T(8,128)(2,1)S(1)}, u32[]{:S(2)}, u32[]{:S(2)}) collective-permute-start(bf16[512,384]{1,0:T(8,128)(2,1)S(1)} %collective-permute-done.13.refs_1_), channel_id=1, source_target_pairs={{0,1},{1,0},{2,3},{3,2},{4,5},{5,4},{6,7},{7,6},{8,9},{9,8},{10,11... | collective-permute-start | bytes 1179656 | tf_op jit(solution)/shard_map/ppermute | solution.py:344
  82.8 0.0 collective-permute-done.12.refs_2_
  82.8 1.2 %project.3.refs_0_ = f32[512,768]{1,0:T(8,128)S(1)} custom-call(bf16[512,384]{1,0:T(8,128)(2,1)S(1)} %merge_last.1.refs_0_, bf16[384,768]{1,0:T(8,128)(2,1)S(1)} %get-tuple-element.55.refs_1_, bf16[512,384]{1,0:T(8,128)(2,1)S(1)} %collective-permute-done.12.refs_2_, bf16[384,768]{1,0:T(8,128)(2,1)S(1)} %collective-permute-done.6.refs_3_), custom_call_target="tpu_custom_call" | custom-call | flops 1200000000 | bytes 1000000 | tf_op jit(solution)/shard_map/project/pallas_call | solution.py:471
  83.9 0.8 project.4.refs_0_
  84.7 0.0 collective-permute-done.16.refs_1_
  84.7 1.5 %project.5 = bf16[512,768]{1,0:T(8,128)(2,1)} custom-call(f32[512,768]{1,0:T(8,128)S(1)} %project.4.refs_0_, bf16[512,384]{1,0:T(8,128)(2,1)S(1)} %collective-permute-done.16.refs_1_, bf16[384,768]{1,0:T(8,128)(2,1)S(1)} %collective-permute-done.15.refs_2_), custom_call_target="tpu_custom_call" | custom-call | flops 600000000 | bytes 1000000 | tf_op jit(solution)/shard_map/project/pallas_call | solution.py:471
  (2 shorter events, 0.1 us)
Async XLA Ops:
  3.5 31.4 %copy-start.2 = (s32[12]{0:T(128)S(1)}, s32[12]{0:T(128)}, u32[]{:S(2)}) copy-start(s32[12]{0:T(128)} %refs_0_.7) | copy-start | bytes 148
  3.6 14.0 %collective-permute-start.3 = (bf16[384,512]{1,0:T(8,128)(2,1)}, bf16[384,512]{1,0:T(8,128)(2,1)S(1)}, u32[]{:S(2)}, u32[]{:S(2)}) collective-permute-start(bf16[384,512]{1,0:T(8,128)(2,1)} %get-tuple-element.30.q_hbm), channel_id=1, source_target_pairs={{0,4},{4,8},{8,12},{12,0},{1,5},{5,9},{9,13},{13,1},{2,6},{6,10},{... | collective-permute-start | bytes 1179656 | tf_op jit(solution)/shard_map/ppermute | solution.py:340
  5.7 13.7 %collective-permute-start.4 = (bf16[384,512]{1,0:T(8,128)(2,1)}, bf16[384,512]{1,0:T(8,128)(2,1)}, u32[]{:S(2)}, u32[]{:S(2)}) collective-permute-start(bf16[384,512]{1,0:T(8,128)(2,1)} %get-tuple-element.30.q_hbm), channel_id=1, source_target_pairs={{0,12},{4,0},{8,4},{12,8},{1,13},{5,1},{9,5},{13,9},{2,14},{6,2},{... | collective-permute-start | bytes 1179656 | tf_op jit(solution)/shard_map/ppermute | solution.py:340
  7.0 24.9 %collective-permute-start = (bf16[768,512]{1,0:T(8,128)(2,1)}, bf16[768,512]{1,0:T(8,128)(2,1)S(1)}, u32[]{:S(2)}, u32[]{:S(2)}) collective-permute-start(bf16[768,512]{1,0:T(8,128)(2,1)} %get-tuple-element.29.kv_hbm), channel_id=1, source_target_pairs={{0,16},{16,0},{1,17},{17,1},{2,18},{18,2},{3,19},{19,3},{4,20},{20... | collective-permute-start | bytes 2359304 | tf_op jit(solution)/shard_map/ppermute | solution.py:344
  10.1 22.2 %collective-permute-start.1 = (bf16[768,512]{1,0:T(8,128)(2,1)}, bf16[768,512]{1,0:T(8,128)(2,1)S(1)}, u32[]{:S(2)}, u32[]{:S(2)}) collective-permute-start(bf16[768,512]{1,0:T(8,128)(2,1)} %get-tuple-element.29.kv_hbm), channel_id=1, source_target_pairs={{0,32},{32,64},{64,96},{96,128},{128,160},{160,192},{192,224},{224... | collective-permute-start | bytes 2359304 | tf_op jit(solution)/shard_map/ppermute | solution.py:340
  11.7 20.6 %collective-permute-start.2 = (bf16[768,512]{1,0:T(8,128)(2,1)}, bf16[768,512]{1,0:T(8,128)(2,1)S(1)}, u32[]{:S(2)}, u32[]{:S(2)}) collective-permute-start(bf16[768,512]{1,0:T(8,128)(2,1)} %get-tuple-element.29.kv_hbm), channel_id=1, source_target_pairs={{0,224},{32,0},{64,32},{96,64},{128,96},{160,128},{192,160},{224,1... | collective-permute-start | bytes 2359304 | tf_op jit(solution)/shard_map/ppermute | solution.py:340
  17.5 14.3 %collective-permute-start.6 = (bf16[384,768]{1,0:T(8,128)(2,1)}, bf16[384,768]{1,0:T(8,128)(2,1)S(1)}, u32[]{:S(2)}, u32[]{:S(2)}) collective-permute-start(bf16[384,768]{1,0:T(8,128)(2,1)} %constant_dynamic-slice_fusion.3), channel_id=1, source_target_pairs={{0,1},{1,0},{2,3},{3,2},{4,5},{5,4},{6,7},{7,6},{8,9},{9,8},{10,11... | collective-permute-start | bytes 1769480 | tf_op jit(solution)/shard_map/ppermute | solution.py:344
  19.4 12.5 %collective-permute-start.5 = (bf16[384,512]{1,0:T(8,128)(2,1)}, bf16[384,512]{1,0:T(8,128)(2,1)}, u32[]{:S(2)}, u32[]{:S(2)}) collective-permute-start(bf16[384,512]{1,0:T(8,128)(2,1)} %get-tuple-element.30.q_hbm), channel_id=1, source_target_pairs={{0,8},{4,12},{8,0},{12,4},{1,9},{5,13},{9,1},{13,5},{2,10},{6,14},... | collective-permute-start | bytes 1179656 | tf_op jit(solution)/shard_map/ppermute | solution.py:340
  20.9 1.1 %copy-start = (bf16[768,512]{1,0:T(8,128)(2,1)S(1)}, bf16[768,512]{1,0:T(8,128)(2,1)}, u32[]{:S(2)}) copy-start(bf16[768,512]{1,0:T(8,128)(2,1)} %get-tuple-element.29.kv_hbm) | copy-start | bytes 2359300
  22.1 1.0 %copy-start.1 = (bf16[384,512]{1,0:T(8,128)(2,1)S(1)}, bf16[384,512]{1,0:T(8,128)(2,1)}, u32[]{:S(2)}) copy-start(bf16[384,512]{1,0:T(8,128)(2,1)} %get-tuple-element.30.q_hbm) | copy-start | bytes 1179652
  32.3 10.1 %collective-permute-start.7 = (bf16[384,512]{1,0:T(8,128)(2,1)S(1)}, bf16[384,512]{1,0:T(8,128)(2,1)S(1)}, u32[]{:S(2)}, u32[]{:S(2)}) collective-permute-start(bf16[384,512]{1,0:T(8,128)(2,1)S(1)} %slice_select_fusion), channel_id=1, source_target_pairs={{0,16},{16,0},{1,17},{17,1},{2,18},{18,2},{3,19},{19,3},{4,20},{20... | collective-permute-start | bytes 1179656 | tf_op jit(solution)/shard_map/ppermute | solution.py:344
  33.0 14.1 %collective-permute-start.8 = (bf16[384,512]{1,0:T(8,128)(2,1)S(1)}, bf16[384,512]{1,0:T(8,128)(2,1)S(1)}, u32[]{:S(2)}, u32[]{:S(2)}) collective-permute-start(bf16[384,512]{1,0:T(8,128)(2,1)S(1)} %slice.11), channel_id=1, source_target_pairs={{0,32},{32,64},{64,96},{96,128},{128,160},{160,192},{192,224},{224... | collective-permute-start | bytes 1179656 | tf_op jit(solution)/shard_map/ppermute | solution.py:400
  49.9 12.3 %collective-permute-start.9 = (bf16[400,512]{1,0:T(8,128)(2,1)S(1)}, bf16[400,512]{1,0:T(8,128)(2,1)S(1)}, u32[]{:S(2)}, u32[]{:S(2)}) collective-permute-start(bf16[400,512]{1,0:T(8,128)(2,1)S(1)} %attend_far.3), channel_id=1, source_target_pairs={{0,8},{4,12},{8,0},{12,4},{1,9},{5,13},{9,1},{13,5},{2,10},{6,14},... | collective-permute-start | bytes 1228808 | tf_op jit(solution)/shard_map/ppermute | solution.py:340
  54.2 4.1 %copy-start.3 = (bf16[384,3072]{1,0:T(8,128)(2,1)S(1)}, bf16[384,3072]{1,0:T(8,128)(2,1)}, u32[]{:S(2)}) copy-start(bf16[384,3072]{1,0:T(8,128)(2,1)} %param.12) | copy-start | bytes 7077892
  56.6 8.8 %collective-permute-start.10 = (bf16[400,512]{1,0:T(8,128)(2,1)S(1)}, bf16[400,512]{1,0:T(8,128)(2,1)S(1)}, u32[]{:S(2)}, u32[]{:S(2)}) collective-permute-start(bf16[400,512]{1,0:T(8,128)(2,1)S(1)} %get-tuple-element.46), channel_id=1, source_target_pairs={{0,12},{4,0},{8,4},{12,8},{1,13},{5,1},{9,5},{13,9},{2,14},{6,2},{... | collective-permute-start | bytes 1228808 | tf_op jit(solution)/shard_map/ppermute | solution.py:340
  56.9 13.3 %collective-permute-start.11 = (bf16[400,512]{1,0:T(8,128)(2,1)S(1)}, bf16[400,512]{1,0:T(8,128)(2,1)S(1)}, u32[]{:S(2)}, u32[]{:S(2)}) collective-permute-start(bf16[400,512]{1,0:T(8,128)(2,1)S(1)} %get-tuple-element.47), channel_id=1, source_target_pairs={{0,4},{4,8},{8,12},{12,0},{1,5},{5,9},{9,13},{13,1},{2,6},{6,10},{... | collective-permute-start | bytes 1228808 | tf_op jit(solution)/shard_map/ppermute | solution.py:340
  58.5 14.8 %collective-permute-start.14 = (bf16[384,768]{1,0:T(8,128)(2,1)S(1)}, bf16[384,768]{1,0:T(8,128)(2,1)S(1)}, u32[]{:S(2)}, u32[]{:S(2)}) collective-permute-start(bf16[384,768]{1,0:T(8,128)(2,1)S(1)} %get-tuple-element.54), channel_id=1, source_target_pairs={{0,2},{2,0},{1,3},{3,1},{4,6},{6,4},{5,7},{7,5},{8,10},{10,8},{9,1... | collective-permute-start | bytes 1769480 | tf_op jit(solution)/shard_map/ppermute | solution.py:344
  59.0 16.2 %collective-permute-start.15 = (bf16[384,768]{1,0:T(8,128)(2,1)S(1)}, bf16[384,768]{1,0:T(8,128)(2,1)S(1)}, u32[]{:S(2)}, u32[]{:S(2)}) collective-permute-start(bf16[384,768]{1,0:T(8,128)(2,1)S(1)} %get-tuple-element.53), channel_id=1, source_target_pairs={{0,19},{1,18},{2,17},{3,16},{16,3},{17,2},{18,1},{19,0},{4,23},{5,... | collective-permute-start | bytes 1769480 | tf_op jit(solution)/shard_map/ppermute | solution.py:438
  70.5 9.9 %collective-permute-start.13 = (bf16[512,384]{1,0:T(8,128)(2,1)S(1)}, bf16[512,384]{1,0:T(8,128)(2,1)S(1)}, u32[]{:S(2)}, u32[]{:S(2)}) collective-permute-start(bf16[512,384]{1,0:T(8,128)(2,1)S(1)} %merge_last.1.refs_0_), channel_id=1, source_target_pairs={{0,2},{2,0},{1,3},{3,1},{4,6},{6,4},{5,7},{7,5},{8,10},{10,8},{9,1... | collective-permute-start | bytes 1179656 | tf_op jit(solution)/shard_map/ppermute | solution.py:344
  71.0 11.7 %collective-permute-start.12 = (bf16[512,384]{1,0:T(8,128)(2,1)S(1)}, bf16[512,384]{1,0:T(8,128)(2,1)S(1)}, u32[]{:S(2)}, u32[]{:S(2)}) collective-permute-start(bf16[512,384]{1,0:T(8,128)(2,1)S(1)} %merge_last.1.refs_0_), channel_id=1, source_target_pairs={{0,1},{1,0},{2,3},{3,2},{4,5},{5,4},{6,7},{7,6},{8,9},{9,8},{10,11... | collective-permute-start | bytes 1179656 | tf_op jit(solution)/shard_map/ppermute | solution.py:344
  80.4 4.3 %collective-permute-start.16 = (bf16[512,384]{1,0:T(8,128)(2,1)S(1)}, bf16[512,384]{1,0:T(8,128)(2,1)S(1)}, u32[]{:S(2)}, u32[]{:S(2)}) collective-permute-start(bf16[512,384]{1,0:T(8,128)(2,1)S(1)} %collective-permute-done.13.refs_1_), channel_id=1, source_target_pairs={{0,1},{1,0},{2,3},{3,2},{4,5},{5,4},{6,7},{7,6},{8,9},{9,8},{10,11... | collective-permute-start | bytes 1179656 | tf_op jit(solution)/shard_map/ppermute | solution.py:344

commit v4 on v3

--- a/solution.py
+++ b/solution.py
@@ -391,9 +391,8 @@
     def mine(j):
         return lax.dynamic_slice_in_dim(out_weight, j * cols, cols, 1)
 
-    w_core = flip(mine(tp ^ 1), "core")
-    pair, below, above, q_left, q_right, q_across, q, kv, w_core = lax.optimization_barrier(
-        (pair, below, above, q_left, q_right, q_across, q, kv, w_core)
+    pair, below, above, q_left, q_right, q_across, q, kv = lax.optimization_barrier(
+        (pair, below, above, q_left, q_right, q_across, q, kv)
     )
     slant = [(zi * 2, (zi + 1) % 8 * 2) for zi in range(8)]
     slant += [(zi * 2 + 1, (zi - 1) % 8 * 2 + 1) for zi in range(8)]
@@ -413,6 +412,8 @@
         name="attend_near",
     )(frame_counts, *qs, below, kv, above)
 
+    near, early_weight = lax.optimization_barrier((near, out_weight))
+    w_core = flip(lax.dynamic_slice_in_dim(early_weight, (tp ^ 1) * cols, cols, 1), "core")
     out = jax.ShapeDtypeStruct((feats + 16, TOK), jnp.bfloat16)
     partial = {}
     for block in CALLS:
@@ -448,6 +449,7 @@
         cost_estimate=cost(6_000_000_000, 2_000_000),
         name="merge_two",
     )(partial[0], across)
+    merged, w_core = lax.optimization_barrier((merged, w_core))
     att = pl.pallas_call(
         merge_last_kernel,
         out_shape=jax.ShapeDtypeStruct((TOK, feats), jnp.bfloat16),

time: 86.6 us -> 83.6 us (0.965)
  waiting for transfers between devices: 28.9 us -> 20.3 us
  starting transfers between devices: 28.8 us -> 37.1 us
  local copies, waits for them, and re-layouts: 4.26 us -> 2.39 us
  Pallas kernels: 24.2 us -> 22.5 us
    ppermute x7, starting transfers between devices: 11.2 us -> 16.1 us  [flip(): return lax.ppermute(value, axis, [(0, 1), (1, 0)])]
    ppermute x7, waiting for transfers between devices: 5.69 us -> 0.82 us  [flip(): return lax.ppermute(value, axis, [(0, 1), (1, 0)])]
    ppermute x1, waiting for transfers between devices: 4.69 us -> 0.56 us  [per_device(): v_far = lax.ppermute(pair[feats:], ('z', 'yh'), slant)]
    ppermute x1, waiting for transfers between devices: 1.86 us -> 5.53 us  [per_device(): lax.ppermute(mine(tp ^ 3), ('yh', 'yl', 'core'), [(i, 7 - i) for i in ran...]
    ppermute x8, waiting for transfers between devices: 16.6 us -> 13.4 us  [shift(): lax.ppermute(value, axis, [(i, (i + by) % count) for i in range(count)])]
    ppermute x8, starting transfers between devices: 12.4 us -> 15.1 us  [shift(): lax.ppermute(value, axis, [(i, (i + by) % count) for i in range(count)])]
    ppermute x1, starting transfers between devices: 3.29 us -> 5.63 us  [per_device(): lax.ppermute(mine(tp ^ 3), ('yh', 'yl', 'core'), [(i, 7 - i) for i in ran...]
    dynamic_slice x2 -> x1, local copies, waits for them, and re-layouts: 2.09 us -> 0.16 us  [mine(): return lax.dynamic_slice_in_dim(out_weight, j * cols, cols, 1)]
  transfers between devices with their start and end apart: 17 -> 17, of which waited for: 8 -> 8; matrix products, arithmetic and copies ran while one was open for 2% -> 0% of each run, Pallas kernels for 19% -> 21%
where the time goes in v4:
time: 83.6 us; the launch traced here: 82.4 us
  starting transfers between devices  37.1 us (44%)
  Pallas kernels  22.5 us (27%)
  waiting for transfers between devices  20.3 us (24%)
  local copies, waits for them, and re-layouts  2.39 us (3%)
    ppermute x7, starting transfers between devices, flip(): return lax.ppermute(value, axis, [(0, 1), (1, 0)])  16.1 us
    ppermute x8, starting transfers between devices, shift(): lax.ppermute(value, axis, [(i, (i + by) % count) for i in range(count)])  15.1 us
    ppermute x8, waiting for transfers between devices, shift(): lax.ppermute(value, axis, [(i, (i + by) % count) for i in range(count)])  13.4 us
    pallas_call x3, Pallas kernels, per_device(): pl.pallas_call(lambda *refs, steps=steps: attend_kernel(steps, True, *ref...  8.27 us
    pallas_call x1, Pallas kernels, per_device(): pl.pallas_call(lambda *refs: attend_kernel(STEPS, False, *refs), out_shap...  6.35 us
    ppermute x1, starting transfers between devices, per_device(): lax.ppermute(mine(tp ^ 3), ('yh', 'yl', 'core'), [(i, 7 - i) for i in ran...  5.63 us
    ppermute x1, waiting for transfers between devices, per_device(): lax.ppermute(mine(tp ^ 3), ('yh', 'yl', 'core'), [(i, 7 - i) for i in ran...  5.53 us
    pallas_call x1, Pallas kernels, per_device(): pl.pallas_call(prepare_kernel, out_shape=[jax.ShapeDtypeStruct((size, TOK...  3.66 us
  transfers between devices with their start and end apart: 17, of which 8 were waited for; matrix products, arithmetic and copies ran while one was open for 0% of the time, Pallas kernels for 21%

profile of v4, /device:TPU:1, one launch (start us, length us, event | category | flops | bytes accessed | tf_op | source)
XLA Modules:
  0.0 82.4 jit_solution(11386454688023958568)
XLA Ops:
  0.0 0.0 copy-start.2
  0.0 3.7 %prepare.1 = (bf16[384,512]{1,0:T(8,128)(2,1)}, bf16[768,512]{1,0:T(8,128)(2,1)}) custom-call(s32[12]{0:T(128)} %refs_0_.7, bf16[512,384]{1,0:T(8,128)(2,1)} %q_hbm.1, bf16[512,384]{1,0:T(8,128)(2,1)} %k_hbm.1, bf16[512,384]{1,0:T(8,128)(2,1)} %v_hbm.1, f32[2,256,128]{2,1,0:T(8,128)} %constant.28.clone.space_hbm, f32[2,16,128]{2,1,0:T(8,128)} %constant.29.clone.time_hbm, ...), custom_call_target="tpu_custom_call" | custom-call | flops 200000000 | bytes 3000000 | tf_op jit(solution)/shard_map/prepare/pallas_call | solution.py:351
  3.7 2.1 %collective-permute-start.3 = (bf16[384,512]{1,0:T(8,128)(2,1)}, bf16[384,512]{1,0:T(8,128)(2,1)S(1)}, u32[]{:S(2)}, u32[]{:S(2)}) collective-permute-start(bf16[384,512]{1,0:T(8,128)(2,1)} %get-tuple-element.33.q_hbm), channel_id=1, source_target_pairs={{0,4},{4,8},{8,12},{12,0},{1,5},{5,9},{9,13},{13,1},{2,6},{6,10},{... | collective-permute-start | bytes 1179656 | tf_op jit(solution)/shard_map/ppermute | solution.py:340
  5.8 2.9 %collective-permute-start = (bf16[768,512]{1,0:T(8,128)(2,1)}, bf16[768,512]{1,0:T(8,128)(2,1)S(1)}, u32[]{:S(2)}, u32[]{:S(2)}) collective-permute-start(bf16[768,512]{1,0:T(8,128)(2,1)} %get-tuple-element.32.kv_hbm), channel_id=1, source_target_pairs={{0,16},{16,0},{1,17},{17,1},{2,18},{18,2},{3,19},{19,3},{4,20},{20... | collective-permute-start | bytes 2359304 | tf_op jit(solution)/shard_map/ppermute | solution.py:344
  8.7 1.6 %collective-permute-start.1 = (bf16[768,512]{1,0:T(8,128)(2,1)}, bf16[768,512]{1,0:T(8,128)(2,1)S(1)}, u32[]{:S(2)}, u32[]{:S(2)}) collective-permute-start(bf16[768,512]{1,0:T(8,128)(2,1)} %get-tuple-element.32.kv_hbm), channel_id=1, source_target_pairs={{0,32},{32,64},{64,96},{96,128},{128,160},{160,192},{192,224},{224... | collective-permute-start | bytes 2359304 | tf_op jit(solution)/shard_map/ppermute | solution.py:340
  10.3 3.9 %collective-permute-start.2 = (bf16[768,512]{1,0:T(8,128)(2,1)}, bf16[768,512]{1,0:T(8,128)(2,1)S(1)}, u32[]{:S(2)}, u32[]{:S(2)}) collective-permute-start(bf16[768,512]{1,0:T(8,128)(2,1)} %get-tuple-element.32.kv_hbm), channel_id=1, source_target_pairs={{0,224},{32,0},{64,32},{96,64},{128,96},{160,128},{192,160},{224,1... | collective-permute-start | bytes 2359304 | tf_op jit(solution)/shard_map/ppermute | solution.py:340
  14.3 1.5 %collective-permute-start.4 = (bf16[384,512]{1,0:T(8,128)(2,1)}, bf16[384,512]{1,0:T(8,128)(2,1)S(1)}, u32[]{:S(2)}, u32[]{:S(2)}) collective-permute-start(bf16[384,512]{1,0:T(8,128)(2,1)} %get-tuple-element.33.q_hbm), channel_id=1, source_target_pairs={{0,12},{4,0},{8,4},{12,8},{1,13},{5,1},{9,5},{13,9},{2,14},{6,2},{... | collective-permute-start | bytes 1179656 | tf_op jit(solution)/shard_map/ppermute | solution.py:340
  15.7 0.0 collective-permute-done.3.refs_2_.refs_1_
  15.7 1.8 %collective-permute-start.5 = (bf16[384,512]{1,0:T(8,128)(2,1)}, bf16[384,512]{1,0:T(8,128)(2,1)S(1)}, u32[]{:S(2)}, u32[]{:S(2)}) collective-permute-start(bf16[384,512]{1,0:T(8,128)(2,1)} %get-tuple-element.33.q_hbm), channel_id=1, source_target_pairs={{0,8},{4,12},{8,0},{12,4},{1,9},{5,13},{9,1},{13,5},{2,10},{6,14},... | collective-permute-start | bytes 1179656 | tf_op jit(solution)/shard_map/ppermute | solution.py:340
  17.5 0.0 copy-start
  17.5 1.1 %copy-done = bf16[768,512]{1,0:T(8,128)(2,1)S(1)} copy-done((bf16[768,512]{1,0:T(8,128)(2,1)S(1)}, bf16[768,512]{1,0:T(8,128)(2,1)}, u32[]{:S(2)}) %copy-start) | copy-done | bytes 786456
  18.7 0.0 copy-start.1
  18.7 1.0 %copy-done.1 = bf16[384,512]{1,0:T(8,128)(2,1)S(1)} copy-done((bf16[384,512]{1,0:T(8,128)(2,1)S(1)}, bf16[384,512]{1,0:T(8,128)(2,1)}, u32[]{:S(2)}) %copy-start.1) | copy-done | bytes 393240
  19.7 0.3 stage.1
  19.9 3.6 %collective-permute-done.4.refs_3_.refs_2_ = bf16[384,512]{1,0:T(8,128)(2,1)S(1)} collective-permute-done((bf16[384,512]{1,0:T(8,128)(2,1)}, bf16[384,512]{1,0:T(8,128)(2,1)S(1)}, u32[]{:S(2)}, u32[]{:S(2)}) %collective-permute-start.4) | collective-permute-done | bytes 393248 | tf_op jit(solution)/shard_map/ppermute | solution.py:340
  23.6 2.7 %collective-permute-done.5.refs_4_.refs_1_ = bf16[384,512]{1,0:T(8,128)(2,1)S(1)} collective-permute-done((bf16[384,512]{1,0:T(8,128)(2,1)}, bf16[384,512]{1,0:T(8,128)(2,1)S(1)}, u32[]{:S(2)}, u32[]{:S(2)}) %collective-permute-start.5) | collective-permute-done | bytes 393248 | tf_op jit(solution)/shard_map/ppermute | solution.py:340
  26.2 0.0 collective-permute-done.refs_2_.refs_3_
  26.2 4.9 %collective-permute-done.1.refs_5_ = bf16[768,512]{1,0:T(8,128)(2,1)S(1)} collective-permute-done((bf16[768,512]{1,0:T(8,128)(2,1)}, bf16[768,512]{1,0:T(8,128)(2,1)S(1)}, u32[]{:S(2)}, u32[]{:S(2)}) %collective-permute-start.1) | collective-permute-done | bytes 786464 | tf_op jit(solution)/shard_map/ppermute | solution.py:340
  31.1 0.0 collective-permute-done.2.refs_7_
  31.2 0.1 collective-permute-start.6
  31.4 0.0 copy-start.3
  31.4 0.2 collective-permute-start.7
  31.6 0.0 copy-done.2
  31.6 6.3 %attend_near.1.refs_5_.refs_6_ = f32[4,408,512]{2,1,0:T(8,128)S(1)} custom-call(s32[12]{0:T(128)S(1)} %copy-done.2, bf16[384,512]{1,0:T(8,128)(2,1)S(1)} %get-tuple-element.36.refs_1_, bf16[384,512]{1,0:T(8,128)(2,1)S(1)} %collective-permute-done.3.refs_2_.refs_1_, bf16[384,512]{1,0:T(8,128)(2,1)S(1)} %collective-permute-done.4.refs_3_.refs_2_, ...), custom_call_target="tpu_custom_call" | custom-call | flops 7000000000 | bytes 5000000 | tf_op jit(solution)/shard_map/attend_near/pallas_call | solution.py:404
  37.9 0.0 copy-done.3
  37.9 0.1 constant_dynamic-slice_fusion.3
  38.0 3.3 %collective-permute-start.9 = (bf16[384,768]{1,0:T(8,128)(2,1)S(1)}, bf16[384,768]{1,0:T(8,128)(2,1)S(1)}, u32[]{:S(2)}, u32[]{:S(2)}) collective-permute-start(bf16[384,768]{1,0:T(8,128)(2,1)S(1)} %constant_dynamic-slice_fusion.3), channel_id=1, source_target_pairs={{0,1},{1,0},{2,3},{3,2},{4,5},{5,4},{6,7},{7,6},{8,9},{9,8},{10,11... | collective-permute-start | bytes 1769480 | tf_op jit(solution)/shard_map/ppermute | solution.py:344
  41.3 0.2 collective-permute-done.6.refs_3_.refs_4_
  41.5 0.6 collective-permute-done.7.refs_4_.refs_5_
  42.1 2.3 %attend_far.3 = bf16[400,512]{1,0:T(8,128)(2,1)S(1)} custom-call(s32[12]{0:T(128)S(1)} %copy-done.2, bf16[384,512]{1,0:T(8,128)(2,1)S(1)} %collective-permute-done.5.refs_4_.refs_1_, bf16[768,512]{1,0:T(8,128)(2,1)S(1)} %collective-permute-done.refs_2_.refs_3_, bf16[384,512]{1,0:T(8,128)(2,1)S(1)} %collective-permute-done.6.refs_3_.refs_4_, ...), custom_call_target="tpu_custom_call" | custom-call | flops 2000000000 | bytes 100000 | tf_op jit(solution)/shard_map/attend_far/pallas_call | solution.py:422
  44.4 2.0 %collective-permute-start.8 = (bf16[400,512]{1,0:T(8,128)(2,1)S(1)}, bf16[400,512]{1,0:T(8,128)(2,1)S(1)}, u32[]{:S(2)}, u32[]{:S(2)}) collective-permute-start(bf16[400,512]{1,0:T(8,128)(2,1)S(1)} %attend_far.3), channel_id=1, source_target_pairs={{0,8},{4,12},{8,0},{12,4},{1,9},{5,13},{9,1},{13,5},{2,10},{6,14},... | collective-permute-start | bytes 1228808 | tf_op jit(solution)/shard_map/ppermute | solution.py:340
  46.4 3.7 %attend_far.4 = (bf16[400,512]{1,0:T(8,128)(2,1)S(1)}, bf16[400,512]{1,0:T(8,128)(2,1)S(1)}) custom-call(s32[12]{0:T(128)S(1)} %copy-done.2, bf16[384,512]{1,0:T(8,128)(2,1)S(1)} %collective-permute-done.3.refs_2_.refs_1_, bf16[384,512]{1,0:T(8,128)(2,1)S(1)} %collective-permute-done.4.refs_3_.refs_2_, ...), custom_call_target="tpu_custom_call" | custom-call | flops 5000000000 | bytes 100000 | tf_op jit(solution)/shard_map/attend_far/pallas_call | solution.py:422
  50.1 2.3 %attend_far.5.p0 = bf16[400,512]{1,0:T(8,128)(2,1)S(1)} custom-call(s32[12]{0:T(128)S(1)} %copy-done.2, bf16[384,512]{1,0:T(8,128)(2,1)S(1)} %get-tuple-element.36.refs_1_, bf16[768,512]{1,0:T(8,128)(2,1)S(1)} %collective-permute-done.refs_2_.refs_3_, bf16[384,512]{1,0:T(8,128)(2,1)S(1)} %collective-permute-done.6.refs_3_.refs_4_, ...), custom_call_target="tpu_custom_call" | custom-call | flops 10000000 | bytes 100000 | tf_op jit(solution)/shard_map/attend_far/pallas_call | solution.py:422
  52.4 2.2 %collective-permute-start.10 = (bf16[400,512]{1,0:T(8,128)(2,1)S(1)}, bf16[400,512]{1,0:T(8,128)(2,1)S(1)}, u32[]{:S(2)}, u32[]{:S(2)}) collective-permute-start(bf16[400,512]{1,0:T(8,128)(2,1)S(1)} %get-tuple-element.52), channel_id=1, source_target_pairs={{0,12},{4,0},{8,4},{12,8},{1,13},{5,1},{9,5},{13,9},{2,14},{6,2},{... | collective-permute-start | bytes 1228808 | tf_op jit(solution)/shard_map/ppermute | solution.py:340
  54.6 0.0 collective-permute-start.11
  54.6 0.2 constant_dynamic-slice_fusion
  54.7 1.3 %collective-permute-start.14 = (bf16[384,768]{1,0:T(8,128)(2,1)S(1)}, bf16[384,768]{1,0:T(8,128)(2,1)S(1)}, u32[]{:S(2)}, u32[]{:S(2)}) collective-permute-start(bf16[384,768]{1,0:T(8,128)(2,1)S(1)} %get-tuple-element.60), channel_id=1, source_target_pairs={{0,2},{2,0},{1,3},{3,1},{4,6},{6,4},{5,7},{7,5},{8,10},{10,8},{9,1... | collective-permute-start | bytes 1769480 | tf_op jit(solution)/shard_map/ppermute | solution.py:344
  56.0 0.0 collective-permute-done.8.p1
  56.0 5.6 %collective-permute-start.15 = (bf16[384,768]{1,0:T(8,128)(2,1)S(1)}, bf16[384,768]{1,0:T(8,128)(2,1)S(1)}, u32[]{:S(2)}, u32[]{:S(2)}) collective-permute-start(bf16[384,768]{1,0:T(8,128)(2,1)S(1)} %get-tuple-element.59), channel_id=1, source_target_pairs={{0,19},{1,18},{2,17},{3,16},{16,3},{17,2},{18,1},{19,0},{4,23},{5,... | collective-permute-start | bytes 1769480 | tf_op jit(solution)/shard_map/ppermute | solution.py:439
  61.6 0.2 merge_two.1.m
  61.9 0.0 collective-permute-done.9.refs_3_
  61.9 2.1 %collective-permute-done.10.p0 = bf16[400,512]{1,0:T(8,128)(2,1)S(1)} collective-permute-done((bf16[400,512]{1,0:T(8,128)(2,1)S(1)}, bf16[400,512]{1,0:T(8,128)(2,1)S(1)}, u32[]{:S(2)}, u32[]{:S(2)}) %collective-permute-start.10) | collective-permute-done | bytes 409632 | tf_op jit(solution)/shard_map/ppermute | solution.py:340
  64.0 0.0 collective-permute-done.11.p1
  64.0 0.4 merge_last.1.refs_0_
  64.4 1.1 %collective-permute-start.13 = (bf16[512,384]{1,0:T(8,128)(2,1)S(1)}, bf16[512,384]{1,0:T(8,128)(2,1)S(1)}, u32[]{:S(2)}, u32[]{:S(2)}) collective-permute-start(bf16[512,384]{1,0:T(8,128)(2,1)S(1)} %merge_last.1.refs_0_), channel_id=1, source_target_pairs={{0,2},{2,0},{1,3},{3,1},{4,6},{6,4},{5,7},{7,5},{8,10},{10,8},{9,1... | collective-permute-start | bytes 1179656 | tf_op jit(solution)/shard_map/ppermute | solution.py:344
  65.5 4.1 %collective-permute-start.12 = (bf16[512,384]{1,0:T(8,128)(2,1)S(1)}, bf16[512,384]{1,0:T(8,128)(2,1)S(1)}, u32[]{:S(2)}, u32[]{:S(2)}) collective-permute-start(bf16[512,384]{1,0:T(8,128)(2,1)S(1)} %merge_last.1.refs_0_), channel_id=1, source_target_pairs={{0,1},{1,0},{2,3},{3,2},{4,5},{5,4},{6,7},{7,6},{8,9},{9,8},{10,11... | collective-permute-start | bytes 1179656 | tf_op jit(solution)/shard_map/ppermute | solution.py:344
  69.6 0.0 collective-permute-done.14.refs_2_
  69.6 5.5 %collective-permute-done.15.refs_2_ = bf16[384,768]{1,0:T(8,128)(2,1)S(1)} collective-permute-done((bf16[384,768]{1,0:T(8,128)(2,1)S(1)}, bf16[384,768]{1,0:T(8,128)(2,1)S(1)}, u32[]{:S(2)}, u32[]{:S(2)}) %collective-permute-start.15) | collective-permute-done | bytes 589856 | tf_op jit(solution)/shard_map/ppermute | solution.py:439
  75.1 0.6 collective-permute-done.13.refs_1_
  75.7 3.3 %collective-permute-start.16 = (bf16[512,384]{1,0:T(8,128)(2,1)S(1)}, bf16[512,384]{1,0:T(8,128)(2,1)S(1)}, u32[]{:S(2)}, u32[]{:S(2)}) collective-permute-start(bf16[512,384]{1,0:T(8,128)(2,1)S(1)} %collective-permute-done.13.refs_1_), channel_id=1, source_target_pairs={{0,1},{1,0},{2,3},{3,2},{4,5},{5,4},{6,7},{7,6},{8,9},{9,8},{10,11... | collective-permute-start | bytes 1179656 | tf_op jit(solution)/shard_map/ppermute | solution.py:344
  79.0 0.0 collective-permute-done.12.refs_2_
  79.0 1.1 %project.3.refs_0_ = f32[512,768]{1,0:T(8,128)S(1)} custom-call(bf16[512,384]{1,0:T(8,128)(2,1)S(1)} %merge_last.1.refs_0_, bf16[384,768]{1,0:T(8,128)(2,1)S(1)} %get-tuple-element.61.refs_1_, bf16[512,384]{1,0:T(8,128)(2,1)S(1)} %collective-permute-done.12.refs_2_, bf16[384,768]{1,0:T(8,128)(2,1)S(1)} %collective-permute-done.9.refs_3_), custom_call_target="tpu_custom_call" | custom-call | flops 1200000000 | bytes 1000000 | tf_op jit(solution)/shard_map/project/pallas_call | solution.py:473
  80.1 0.8 project.4.refs_0_
  80.9 0.0 collective-permute-done.16.refs_1_
  80.9 1.5 %project.5 = bf16[512,768]{1,0:T(8,128)(2,1)} custom-call(f32[512,768]{1,0:T(8,128)S(1)} %project.4.refs_0_, bf16[512,384]{1,0:T(8,128)(2,1)S(1)} %collective-permute-done.16.refs_1_, bf16[384,768]{1,0:T(8,128)(2,1)S(1)} %collective-permute-done.15.refs_2_), custom_call_target="tpu_custom_call" | custom-call | flops 600000000 | bytes 1000000 | tf_op jit(solution)/shard_map/project/pallas_call | solution.py:473
  (2 shorter events, 0.1 us)
Async XLA Ops:
  0.0 31.6 %copy-start.2 = (s32[12]{0:T(128)S(1)}, s32[12]{0:T(128)}, u32[]{:S(2)}) copy-start(s32[12]{0:T(128)} %refs_0_.7) | copy-start | bytes 148
  3.7 12.1 %collective-permute-start.3 = (bf16[384,512]{1,0:T(8,128)(2,1)}, bf16[384,512]{1,0:T(8,128)(2,1)S(1)}, u32[]{:S(2)}, u32[]{:S(2)}) collective-permute-start(bf16[384,512]{1,0:T(8,128)(2,1)} %get-tuple-element.33.q_hbm), channel_id=1, source_target_pairs={{0,4},{4,8},{8,12},{12,0},{1,5},{5,9},{9,13},{13,1},{2,6},{6,10},{... | collective-permute-start | bytes 1179656 | tf_op jit(solution)/shard_map/ppermute | solution.py:340
  5.8 20.5 %collective-permute-start = (bf16[768,512]{1,0:T(8,128)(2,1)}, bf16[768,512]{1,0:T(8,128)(2,1)S(1)}, u32[]{:S(2)}, u32[]{:S(2)}) collective-permute-start(bf16[768,512]{1,0:T(8,128)(2,1)} %get-tuple-element.32.kv_hbm), channel_id=1, source_target_pairs={{0,16},{16,0},{1,17},{17,1},{2,18},{18,2},{3,19},{19,3},{4,20},{20... | collective-permute-start | bytes 2359304 | tf_op jit(solution)/shard_map/ppermute | solution.py:344
  8.7 22.5 %collective-permute-start.1 = (bf16[768,512]{1,0:T(8,128)(2,1)}, bf16[768,512]{1,0:T(8,128)(2,1)S(1)}, u32[]{:S(2)}, u32[]{:S(2)}) collective-permute-start(bf16[768,512]{1,0:T(8,128)(2,1)} %get-tuple-element.32.kv_hbm), channel_id=1, source_target_pairs={{0,32},{32,64},{64,96},{96,128},{128,160},{160,192},{192,224},{224... | collective-permute-start | bytes 2359304 | tf_op jit(solution)/shard_map/ppermute | solution.py:340
  10.3 20.8 %collective-permute-start.2 = (bf16[768,512]{1,0:T(8,128)(2,1)}, bf16[768,512]{1,0:T(8,128)(2,1)S(1)}, u32[]{:S(2)}, u32[]{:S(2)}) collective-permute-start(bf16[768,512]{1,0:T(8,128)(2,1)} %get-tuple-element.32.kv_hbm), channel_id=1, source_target_pairs={{0,224},{32,0},{64,32},{96,64},{128,96},{160,128},{192,160},{224,1... | collective-permute-start | bytes 2359304 | tf_op jit(solution)/shard_map/ppermute | solution.py:340
  14.3 9.3 %collective-permute-start.4 = (bf16[384,512]{1,0:T(8,128)(2,1)}, bf16[384,512]{1,0:T(8,128)(2,1)S(1)}, u32[]{:S(2)}, u32[]{:S(2)}) collective-permute-start(bf16[384,512]{1,0:T(8,128)(2,1)} %get-tuple-element.33.q_hbm), channel_id=1, source_target_pairs={{0,12},{4,0},{8,4},{12,8},{1,13},{5,1},{9,5},{13,9},{2,14},{6,2},{... | collective-permute-start | bytes 1179656 | tf_op jit(solution)/shard_map/ppermute | solution.py:340
  15.7 10.5 %collective-permute-start.5 = (bf16[384,512]{1,0:T(8,128)(2,1)}, bf16[384,512]{1,0:T(8,128)(2,1)S(1)}, u32[]{:S(2)}, u32[]{:S(2)}) collective-permute-start(bf16[384,512]{1,0:T(8,128)(2,1)} %get-tuple-element.33.q_hbm), channel_id=1, source_target_pairs={{0,8},{4,12},{8,0},{12,4},{1,9},{5,13},{9,1},{13,5},{2,10},{6,14},... | collective-permute-start | bytes 1179656 | tf_op jit(solution)/shard_map/ppermute | solution.py:340
  17.5 1.1 %copy-start = (bf16[768,512]{1,0:T(8,128)(2,1)S(1)}, bf16[768,512]{1,0:T(8,128)(2,1)}, u32[]{:S(2)}) copy-start(bf16[768,512]{1,0:T(8,128)(2,1)} %get-tuple-element.32.kv_hbm) | copy-start | bytes 2359300
  18.7 1.0 %copy-start.1 = (bf16[384,512]{1,0:T(8,128)(2,1)S(1)}, bf16[384,512]{1,0:T(8,128)(2,1)}, u32[]{:S(2)}) copy-start(bf16[384,512]{1,0:T(8,128)(2,1)} %get-tuple-element.33.q_hbm) | copy-start | bytes 1179652
  31.2 10.3 %collective-permute-start.6 = (bf16[384,512]{1,0:T(8,128)(2,1)S(1)}, bf16[384,512]{1,0:T(8,128)(2,1)S(1)}, u32[]{:S(2)}, u32[]{:S(2)}) collective-permute-start(bf16[384,512]{1,0:T(8,128)(2,1)S(1)} %slice_select_fusion), channel_id=1, source_target_pairs={{0,16},{16,0},{1,17},{17,1},{2,18},{18,2},{3,19},{19,3},{4,20},{20... | collective-permute-start | bytes 1179656 | tf_op jit(solution)/shard_map/ppermute | solution.py:344
  31.4 6.5 %copy-start.3 = (bf16[384,3072]{1,0:T(8,128)(2,1)S(1)}, bf16[384,3072]{1,0:T(8,128)(2,1)}, u32[]{:S(2)}) copy-start(bf16[384,3072]{1,0:T(8,128)(2,1)} %param.12) | copy-start | bytes 7077892
  31.4 10.7 %collective-permute-start.7 = (bf16[384,512]{1,0:T(8,128)(2,1)S(1)}, bf16[384,512]{1,0:T(8,128)(2,1)S(1)}, u32[]{:S(2)}, u32[]{:S(2)}) collective-permute-start(bf16[384,512]{1,0:T(8,128)(2,1)S(1)} %slice.11), channel_id=1, source_target_pairs={{0,32},{32,64},{64,96},{96,128},{128,160},{160,192},{192,224},{224... | collective-permute-start | bytes 1179656 | tf_op jit(solution)/shard_map/ppermute | solution.py:399
  38.0 23.9 %collective-permute-start.9 = (bf16[384,768]{1,0:T(8,128)(2,1)S(1)}, bf16[384,768]{1,0:T(8,128)(2,1)S(1)}, u32[]{:S(2)}, u32[]{:S(2)}) collective-permute-start(bf16[384,768]{1,0:T(8,128)(2,1)S(1)} %constant_dynamic-slice_fusion.3), channel_id=1, source_target_pairs={{0,1},{1,0},{2,3},{3,2},{4,5},{5,4},{6,7},{7,6},{8,9},{9,8},{10,11... | collective-permute-start | bytes 1769480 | tf_op jit(solution)/shard_map/ppermute | solution.py:344
  44.4 11.6 %collective-permute-start.8 = (bf16[400,512]{1,0:T(8,128)(2,1)S(1)}, bf16[400,512]{1,0:T(8,128)(2,1)S(1)}, u32[]{:S(2)}, u32[]{:S(2)}) collective-permute-start(bf16[400,512]{1,0:T(8,128)(2,1)S(1)} %attend_far.3), channel_id=1, source_target_pairs={{0,8},{4,12},{8,0},{12,4},{1,9},{5,13},{9,1},{13,5},{2,10},{6,14},... | collective-permute-start | bytes 1228808 | tf_op jit(solution)/shard_map/ppermute | solution.py:340
  52.4 11.6 %collective-permute-start.10 = (bf16[400,512]{1,0:T(8,128)(2,1)S(1)}, bf16[400,512]{1,0:T(8,128)(2,1)S(1)}, u32[]{:S(2)}, u32[]{:S(2)}) collective-permute-start(bf16[400,512]{1,0:T(8,128)(2,1)S(1)} %get-tuple-element.52), channel_id=1, source_target_pairs={{0,12},{4,0},{8,4},{12,8},{1,13},{5,1},{9,5},{13,9},{2,14},{6,2},{... | collective-permute-start | bytes 1228808 | tf_op jit(solution)/shard_map/ppermute | solution.py:340
  54.6 9.5 %collective-permute-start.11 = (bf16[400,512]{1,0:T(8,128)(2,1)S(1)}, bf16[400,512]{1,0:T(8,128)(2,1)S(1)}, u32[]{:S(2)}, u32[]{:S(2)}) collective-permute-start(bf16[400,512]{1,0:T(8,128)(2,1)S(1)} %get-tuple-element.53), channel_id=1, source_target_pairs={{0,4},{4,8},{8,12},{12,0},{1,5},{5,9},{9,13},{13,1},{2,6},{6,10},{... | collective-permute-start | bytes 1228808 | tf_op jit(solution)/shard_map/ppermute | solution.py:340
  54.7 14.9 %collective-permute-start.14 = (bf16[384,768]{1,0:T(8,128)(2,1)S(1)}, bf16[384,768]{1,0:T(8,128)(2,1)S(1)}, u32[]{:S(2)}, u32[]{:S(2)}) collective-permute-start(bf16[384,768]{1,0:T(8,128)(2,1)S(1)} %get-tuple-element.60), channel_id=1, source_target_pairs={{0,2},{2,0},{1,3},{3,1},{4,6},{6,4},{5,7},{7,5},{8,10},{10,8},{9,1... | collective-permute-start | bytes 1769480 | tf_op jit(solution)/shard_map/ppermute | solution.py:344
  56.0 19.1 %collective-permute-start.15 = (bf16[384,768]{1,0:T(8,128)(2,1)S(1)}, bf16[384,768]{1,0:T(8,128)(2,1)S(1)}, u32[]{:S(2)}, u32[]{:S(2)}) collective-permute-start(bf16[384,768]{1,0:T(8,128)(2,1)S(1)} %get-tuple-element.59), channel_id=1, source_target_pairs={{0,19},{1,18},{2,17},{3,16},{16,3},{17,2},{18,1},{19,0},{4,23},{5,... | collective-permute-start | bytes 1769480 | tf_op jit(solution)/shard_map/ppermute | solution.py:439
  64.4 11.3 %collective-permute-start.13 = (bf16[512,384]{1,0:T(8,128)(2,1)S(1)}, bf16[512,384]{1,0:T(8,128)(2,1)S(1)}, u32[]{:S(2)}, u32[]{:S(2)}) collective-permute-start(bf16[512,384]{1,0:T(8,128)(2,1)S(1)} %merge_last.1.refs_0_), channel_id=1, source_target_pairs={{0,2},{2,0},{1,3},{3,1},{4,6},{6,4},{5,7},{7,5},{8,10},{10,8},{9,1... | collective-permute-start | bytes 1179656 | tf_op jit(solution)/shard_map/ppermute | solution.py:344
  65.5 13.5 %collective-permute-start.12 = (bf16[512,384]{1,0:T(8,128)(2,1)S(1)}, bf16[512,384]{1,0:T(8,128)(2,1)S(1)}, u32[]{:S(2)}, u32[]{:S(2)}) collective-permute-start(bf16[512,384]{1,0:T(8,128)(2,1)S(1)} %merge_last.1.refs_0_), channel_id=1, source_target_pairs={{0,1},{1,0},{2,3},{3,2},{4,5},{5,4},{6,7},{7,6},{8,9},{9,8},{10,11... | collective-permute-start | bytes 1179656 | tf_op jit(solution)/shard_map/ppermute | solution.py:344
  75.7 5.2 %collective-permute-start.16 = (bf16[512,384]{1,0:T(8,128)(2,1)S(1)}, bf16[512,384]{1,0:T(8,128)(2,1)S(1)}, u32[]{:S(2)}, u32[]{:S(2)}) collective-permute-start(bf16[512,384]{1,0:T(8,128)(2,1)S(1)} %collective-permute-done.13.refs_1_), channel_id=1, source_target_pairs={{0,1},{1,0},{2,3},{3,2},{4,5},{5,4},{6,7},{7,6},{8,9},{9,8},{10,11... | collective-permute-start | bytes 1179656 | tf_op jit(solution)/shard_map/ppermute | solution.py:344

commit v5 on v4

--- a/solution.py
+++ b/solution.py
@@ -461,9 +461,6 @@
     )(merged, left, right)
     att_yl = flip(att, "yl")
     att_core = flip(att, "core")
-    att_yl, w_yl, w_far = lax.optimization_barrier((att_yl, w_yl, w_far))
-    att_far = flip(att_yl, "core")
-
     def add_terms(before, pairs, dtype):
         operands = ([] if before is None else [before]) + [v for pair in pairs for v in pair]
         tile = 256
@@ -482,6 +479,8 @@
         )(*operands)
 
     total = add_terms(None, [(att, w_own), (att_core, w_core)], jnp.float32)
+    att_yl, w_yl, w_far, total = lax.optimization_barrier((att_yl, w_yl, w_far, total))
+    att_far = flip(att_yl, "core")
     total = add_terms(total, [(att_yl, w_yl)], jnp.float32)
     return add_terms(total, [(att_far, w_far)], jnp.bfloat16)
 

time: 83.6 us -> 83.5 us (level)
  waiting for transfers between devices: 20.3 us -> 23.1 us
  starting transfers between devices: 37.1 us -> 34.4 us
    ppermute x7, waiting for transfers between devices: 0.82 us -> 4.7 us  [flip(): return lax.ppermute(value, axis, [(0, 1), (1, 0)])]
    ppermute x7, starting transfers between devices: 16.1 us -> 13.4 us  [flip(): return lax.ppermute(value, axis, [(0, 1), (1, 0)])]
    ppermute x1, waiting for transfers between devices: 5.53 us -> 4.45 us  [per_device(): lax.ppermute(mine(tp ^ 3), ('yh', 'yl', 'core'), [(i, 7 - i) for i in ran...]
  transfers between devices with their start and end apart: 17 -> 17, of which waited for: 8 -> 10; matrix products, arithmetic and copies ran while one was open for 0% -> 0% of each run, Pallas kernels for 21% -> 21%
where the time goes in v5:
time: 83.5 us; the launch traced here: 82.5 us
  starting transfers between devices  34.4 us (41%)
  waiting for transfers between devices  23.1 us (28%)
  Pallas kernels  22.5 us (27%)
  local copies, waits for them, and re-layouts  2.39 us (3%)
    ppermute x8, starting transfers between devices, shift(): lax.ppermute(value, axis, [(i, (i + by) % count) for i in range(count)])  15.1 us
    ppermute x7, starting transfers between devices, flip(): return lax.ppermute(value, axis, [(0, 1), (1, 0)])  13.4 us
    ppermute x8, waiting for transfers between devices, shift(): lax.ppermute(value, axis, [(i, (i + by) % count) for i in range(count)])  13.4 us
    pallas_call x3, Pallas kernels, per_device(): pl.pallas_call(lambda *refs, steps=steps: attend_kernel(steps, True, *ref...  8.25 us
    pallas_call x1, Pallas kernels, per_device(): pl.pallas_call(lambda *refs: attend_kernel(STEPS, False, *refs), out_shap...  6.35 us
    ppermute x1, starting transfers between devices, per_device(): lax.ppermute(mine(tp ^ 3), ('yh', 'yl', 'core'), [(i, 7 - i) for i in ran...  5.63 us
    ppermute x7, waiting for transfers between devices, flip(): return lax.ppermute(value, axis, [(0, 1), (1, 0)])  4.7 us
    ppermute x1, waiting for transfers between devices, per_device(): lax.ppermute(mine(tp ^ 3), ('yh', 'yl', 'core'), [(i, 7 - i) for i in ran...  4.45 us
  transfers between devices with their start and end apart: 17, of which 10 were waited for; matrix products, arithmetic and copies ran while one was open for 0% of the time, Pallas kernels for 21%

profile of v5, /device:TPU:1, one launch (start us, length us, event | category | flops | bytes accessed | tf_op | source)
XLA Modules:
  0.0 82.5 jit_solution(4970551245529059558)
XLA Ops:
  0.0 0.0 copy-start.2
  0.0 3.7 %prepare.1 = (bf16[384,512]{1,0:T(8,128)(2,1)}, bf16[768,512]{1,0:T(8,128)(2,1)}) custom-call(s32[12]{0:T(128)} %refs_0_.7, bf16[512,384]{1,0:T(8,128)(2,1)} %q_hbm.1, bf16[512,384]{1,0:T(8,128)(2,1)} %k_hbm.1, bf16[512,384]{1,0:T(8,128)(2,1)} %v_hbm.1, f32[2,256,128]{2,1,0:T(8,128)} %constant.28.clone.space_hbm, f32[2,16,128]{2,1,0:T(8,128)} %constant.29.clone.time_hbm, ...), custom_call_target="tpu_custom_call" | custom-call | flops 200000000 | bytes 3000000 | tf_op jit(solution)/shard_map/prepare/pallas_call | solution.py:351
  3.7 2.1 %collective-permute-start.3 = (bf16[384,512]{1,0:T(8,128)(2,1)}, bf16[384,512]{1,0:T(8,128)(2,1)S(1)}, u32[]{:S(2)}, u32[]{:S(2)}) collective-permute-start(bf16[384,512]{1,0:T(8,128)(2,1)} %get-tuple-element.34.q_hbm), channel_id=1, source_target_pairs={{0,4},{4,8},{8,12},{12,0},{1,5},{5,9},{9,13},{13,1},{2,6},{6,10},{... | collective-permute-start | bytes 1179656 | tf_op jit(solution)/shard_map/ppermute | solution.py:340
  5.8 2.9 %collective-permute-start = (bf16[768,512]{1,0:T(8,128)(2,1)}, bf16[768,512]{1,0:T(8,128)(2,1)S(1)}, u32[]{:S(2)}, u32[]{:S(2)}) collective-permute-start(bf16[768,512]{1,0:T(8,128)(2,1)} %get-tuple-element.33.kv_hbm), channel_id=1, source_target_pairs={{0,16},{16,0},{1,17},{17,1},{2,18},{18,2},{3,19},{19,3},{4,20},{20... | collective-permute-start | bytes 2359304 | tf_op jit(solution)/shard_map/ppermute | solution.py:344
  8.7 1.6 %collective-permute-start.1 = (bf16[768,512]{1,0:T(8,128)(2,1)}, bf16[768,512]{1,0:T(8,128)(2,1)S(1)}, u32[]{:S(2)}, u32[]{:S(2)}) collective-permute-start(bf16[768,512]{1,0:T(8,128)(2,1)} %get-tuple-element.33.kv_hbm), channel_id=1, source_target_pairs={{0,32},{32,64},{64,96},{96,128},{128,160},{160,192},{192,224},{224... | collective-permute-start | bytes 2359304 | tf_op jit(solution)/shard_map/ppermute | solution.py:340
  10.3 3.9 %collective-permute-start.2 = (bf16[768,512]{1,0:T(8,128)(2,1)}, bf16[768,512]{1,0:T(8,128)(2,1)S(1)}, u32[]{:S(2)}, u32[]{:S(2)}) collective-permute-start(bf16[768,512]{1,0:T(8,128)(2,1)} %get-tuple-element.33.kv_hbm), channel_id=1, source_target_pairs={{0,224},{32,0},{64,32},{96,64},{128,96},{160,128},{192,160},{224,1... | collective-permute-start | bytes 2359304 | tf_op jit(solution)/shard_map/ppermute | solution.py:340
  14.3 1.5 %collective-permute-start.4 = (bf16[384,512]{1,0:T(8,128)(2,1)}, bf16[384,512]{1,0:T(8,128)(2,1)S(1)}, u32[]{:S(2)}, u32[]{:S(2)}) collective-permute-start(bf16[384,512]{1,0:T(8,128)(2,1)} %get-tuple-element.34.q_hbm), channel_id=1, source_target_pairs={{0,12},{4,0},{8,4},{12,8},{1,13},{5,1},{9,5},{13,9},{2,14},{6,2},{... | collective-permute-start | bytes 1179656 | tf_op jit(solution)/shard_map/ppermute | solution.py:340
  15.7 0.0 collective-permute-done.3.refs_2_.refs_1_
  15.7 1.8 %collective-permute-start.5 = (bf16[384,512]{1,0:T(8,128)(2,1)}, bf16[384,512]{1,0:T(8,128)(2,1)S(1)}, u32[]{:S(2)}, u32[]{:S(2)}) collective-permute-start(bf16[384,512]{1,0:T(8,128)(2,1)} %get-tuple-element.34.q_hbm), channel_id=1, source_target_pairs={{0,8},{4,12},{8,0},{12,4},{1,9},{5,13},{9,1},{13,5},{2,10},{6,14},... | collective-permute-start | bytes 1179656 | tf_op jit(solution)/shard_map/ppermute | solution.py:340
  17.5 0.0 copy-start
  17.5 1.1 %copy-done = bf16[768,512]{1,0:T(8,128)(2,1)S(1)} copy-done((bf16[768,512]{1,0:T(8,128)(2,1)S(1)}, bf16[768,512]{1,0:T(8,128)(2,1)}, u32[]{:S(2)}) %copy-start) | copy-done | bytes 786456
  18.7 0.0 copy-start.1
  18.7 1.0 %copy-done.1 = bf16[384,512]{1,0:T(8,128)(2,1)S(1)} copy-done((bf16[384,512]{1,0:T(8,128)(2,1)S(1)}, bf16[384,512]{1,0:T(8,128)(2,1)}, u32[]{:S(2)}) %copy-start.1) | copy-done | bytes 393240
  19.7 0.3 stage.1
  19.9 3.6 %collective-permute-done.4.refs_3_.refs_2_ = bf16[384,512]{1,0:T(8,128)(2,1)S(1)} collective-permute-done((bf16[384,512]{1,0:T(8,128)(2,1)}, bf16[384,512]{1,0:T(8,128)(2,1)S(1)}, u32[]{:S(2)}, u32[]{:S(2)}) %collective-permute-start.4) | collective-permute-done | bytes 393248 | tf_op jit(solution)/shard_map/ppermute | solution.py:340
  23.6 2.7 %collective-permute-done.5.refs_4_.refs_1_ = bf16[384,512]{1,0:T(8,128)(2,1)S(1)} collective-permute-done((bf16[384,512]{1,0:T(8,128)(2,1)}, bf16[384,512]{1,0:T(8,128)(2,1)S(1)}, u32[]{:S(2)}, u32[]{:S(2)}) %collective-permute-start.5) | collective-permute-done | bytes 393248 | tf_op jit(solution)/shard_map/ppermute | solution.py:340
  26.2 0.0 collective-permute-done.refs_2_.refs_3_
  26.2 4.9 %collective-permute-done.1.refs_5_ = bf16[768,512]{1,0:T(8,128)(2,1)S(1)} collective-permute-done((bf16[768,512]{1,0:T(8,128)(2,1)}, bf16[768,512]{1,0:T(8,128)(2,1)S(1)}, u32[]{:S(2)}, u32[]{:S(2)}) %collective-permute-start.1) | collective-permute-done | bytes 786464 | tf_op jit(solution)/shard_map/ppermute | solution.py:340
  31.1 0.0 collective-permute-done.2.refs_7_
  31.2 0.2 collective-permute-start.6
  31.4 0.0 copy-start.3
  31.4 0.2 collective-permute-start.7
  31.6 0.0 copy-done.2
  31.6 6.3 %attend_near.1.refs_5_.refs_6_ = f32[4,408,512]{2,1,0:T(8,128)S(1)} custom-call(s32[12]{0:T(128)S(1)} %copy-done.2, bf16[384,512]{1,0:T(8,128)(2,1)S(1)} %get-tuple-element.37.refs_1_, bf16[384,512]{1,0:T(8,128)(2,1)S(1)} %collective-permute-done.3.refs_2_.refs_1_, bf16[384,512]{1,0:T(8,128)(2,1)S(1)} %collective-permute-done.4.refs_3_.refs_2_, ...), custom_call_target="tpu_custom_call" | custom-call | flops 7000000000 | bytes 5000000 | tf_op jit(solution)/shard_map/attend_near/pallas_call | solution.py:404
  37.9 0.0 copy-done.3
  37.9 0.1 constant_dynamic-slice_fusion.3
  38.0 3.3 %collective-permute-start.9 = (bf16[384,768]{1,0:T(8,128)(2,1)S(1)}, bf16[384,768]{1,0:T(8,128)(2,1)S(1)}, u32[]{:S(2)}, u32[]{:S(2)}) collective-permute-start(bf16[384,768]{1,0:T(8,128)(2,1)S(1)} %constant_dynamic-slice_fusion.3), channel_id=1, source_target_pairs={{0,1},{1,0},{2,3},{3,2},{4,5},{5,4},{6,7},{7,6},{8,9},{9,8},{10,11... | collective-permute-start | bytes 1769480 | tf_op jit(solution)/shard_map/ppermute | solution.py:344
  41.3 0.2 collective-permute-done.6.refs_3_.refs_4_
  41.5 0.6 collective-permute-done.7.refs_4_.refs_5_
  42.1 2.3 %attend_far.3 = bf16[400,512]{1,0:T(8,128)(2,1)S(1)} custom-call(s32[12]{0:T(128)S(1)} %copy-done.2, bf16[384,512]{1,0:T(8,128)(2,1)S(1)} %collective-permute-done.5.refs_4_.refs_1_, bf16[768,512]{1,0:T(8,128)(2,1)S(1)} %collective-permute-done.refs_2_.refs_3_, bf16[384,512]{1,0:T(8,128)(2,1)S(1)} %collective-permute-done.6.refs_3_.refs_4_, ...), custom_call_target="tpu_custom_call" | custom-call | flops 2000000000 | bytes 100000 | tf_op jit(solution)/shard_map/attend_far/pallas_call | solution.py:422
  44.4 2.0 %collective-permute-start.8 = (bf16[400,512]{1,0:T(8,128)(2,1)S(1)}, bf16[400,512]{1,0:T(8,128)(2,1)S(1)}, u32[]{:S(2)}, u32[]{:S(2)}) collective-permute-start(bf16[400,512]{1,0:T(8,128)(2,1)S(1)} %attend_far.3), channel_id=1, source_target_pairs={{0,8},{4,12},{8,0},{12,4},{1,9},{5,13},{9,1},{13,5},{2,10},{6,14},... | collective-permute-start | bytes 1228808 | tf_op jit(solution)/shard_map/ppermute | solution.py:340
  46.4 3.7 %attend_far.4 = (bf16[400,512]{1,0:T(8,128)(2,1)S(1)}, bf16[400,512]{1,0:T(8,128)(2,1)S(1)}) custom-call(s32[12]{0:T(128)S(1)} %copy-done.2, bf16[384,512]{1,0:T(8,128)(2,1)S(1)} %collective-permute-done.3.refs_2_.refs_1_, bf16[384,512]{1,0:T(8,128)(2,1)S(1)} %collective-permute-done.4.refs_3_.refs_2_, ...), custom_call_target="tpu_custom_call" | custom-call | flops 5000000000 | bytes 100000 | tf_op jit(solution)/shard_map/attend_far/pallas_call | solution.py:422
  50.1 2.3 %attend_far.5.p0 = bf16[400,512]{1,0:T(8,128)(2,1)S(1)} custom-call(s32[12]{0:T(128)S(1)} %copy-done.2, bf16[384,512]{1,0:T(8,128)(2,1)S(1)} %get-tuple-element.37.refs_1_, bf16[768,512]{1,0:T(8,128)(2,1)S(1)} %collective-permute-done.refs_2_.refs_3_, bf16[384,512]{1,0:T(8,128)(2,1)S(1)} %collective-permute-done.6.refs_3_.refs_4_, ...), custom_call_target="tpu_custom_call" | custom-call | flops 10000000 | bytes 100000 | tf_op jit(solution)/shard_map/attend_far/pallas_call | solution.py:422
  52.4 2.2 %collective-permute-start.10 = (bf16[400,512]{1,0:T(8,128)(2,1)S(1)}, bf16[400,512]{1,0:T(8,128)(2,1)S(1)}, u32[]{:S(2)}, u32[]{:S(2)}) collective-permute-start(bf16[400,512]{1,0:T(8,128)(2,1)S(1)} %get-tuple-element.53), channel_id=1, source_target_pairs={{0,12},{4,0},{8,4},{12,8},{1,13},{5,1},{9,5},{13,9},{2,14},{6,2},{... | collective-permute-start | bytes 1228808 | tf_op jit(solution)/shard_map/ppermute | solution.py:340
  54.6 0.0 collective-permute-start.11
  54.6 0.2 constant_dynamic-slice_fusion
  54.7 1.3 %collective-permute-start.13 = (bf16[384,768]{1,0:T(8,128)(2,1)S(1)}, bf16[384,768]{1,0:T(8,128)(2,1)S(1)}, u32[]{:S(2)}, u32[]{:S(2)}) collective-permute-start(bf16[384,768]{1,0:T(8,128)(2,1)S(1)} %get-tuple-element.63), channel_id=1, source_target_pairs={{0,2},{2,0},{1,3},{3,1},{4,6},{6,4},{5,7},{7,5},{8,10},{10,8},{9,1... | collective-permute-start | bytes 1769480 | tf_op jit(solution)/shard_map/ppermute | solution.py:344
  56.0 0.0 collective-permute-done.8.p1
  56.0 5.6 %collective-permute-start.14 = (bf16[384,768]{1,0:T(8,128)(2,1)S(1)}, bf16[384,768]{1,0:T(8,128)(2,1)S(1)}, u32[]{:S(2)}, u32[]{:S(2)}) collective-permute-start(bf16[384,768]{1,0:T(8,128)(2,1)S(1)} %get-tuple-element.62), channel_id=1, source_target_pairs={{0,19},{1,18},{2,17},{3,16},{16,3},{17,2},{18,1},{19,0},{4,23},{5,... | collective-permute-start | bytes 1769480 | tf_op jit(solution)/shard_map/ppermute | solution.py:439
  61.6 0.2 merge_two.1.m
  61.8 0.0 collective-permute-done.9.refs_3_
  61.9 2.2 %collective-permute-done.10.p0 = bf16[400,512]{1,0:T(8,128)(2,1)S(1)} collective-permute-done((bf16[400,512]{1,0:T(8,128)(2,1)S(1)}, bf16[400,512]{1,0:T(8,128)(2,1)S(1)}, u32[]{:S(2)}, u32[]{:S(2)}) %collective-permute-start.10) | collective-permute-done | bytes 409632 | tf_op jit(solution)/shard_map/ppermute | solution.py:340
  64.0 0.0 collective-permute-done.11.p1
  64.0 0.4 merge_last.1.refs_0_
  64.4 3.7 %collective-permute-start.15 = (bf16[512,384]{1,0:T(8,128)(2,1)S(1)}, bf16[512,384]{1,0:T(8,128)(2,1)S(1)}, u32[]{:S(2)}, u32[]{:S(2)}) collective-permute-start(bf16[512,384]{1,0:T(8,128)(2,1)S(1)} %merge_last.1.refs_0_), channel_id=1, source_target_pairs={{0,1},{1,0},{2,3},{3,2},{4,5},{5,4},{6,7},{7,6},{8,9},{9,8},{10,11... | collective-permute-start | bytes 1179656 | tf_op jit(solution)/shard_map/ppermute | solution.py:344
  68.1 1.2 %collective-permute-start.12 = (bf16[512,384]{1,0:T(8,128)(2,1)S(1)}, bf16[512,384]{1,0:T(8,128)(2,1)S(1)}, u32[]{:S(2)}, u32[]{:S(2)}) collective-permute-start(bf16[512,384]{1,0:T(8,128)(2,1)S(1)} %merge_last.1.refs_0_), channel_id=1, source_target_pairs={{0,2},{2,0},{1,3},{3,1},{4,6},{6,4},{5,7},{7,5},{8,10},{10,8},{9,1... | collective-permute-start | bytes 1179656 | tf_op jit(solution)/shard_map/ppermute | solution.py:344
  69.3 0.2 collective-permute-done.15.refs_2_
  69.5 1.2 %project.3.refs_0_ = f32[512,768]{1,0:T(8,128)S(1)} custom-call(bf16[512,384]{1,0:T(8,128)(2,1)S(1)} %merge_last.1.refs_0_, bf16[384,768]{1,0:T(8,128)(2,1)S(1)} %get-tuple-element.61.refs_1_, bf16[512,384]{1,0:T(8,128)(2,1)S(1)} %collective-permute-done.15.refs_2_, bf16[384,768]{1,0:T(8,128)(2,1)S(1)} %collective-permute-done.9.refs_3_), custom_call_target="tpu_custom_call" | custom-call | flops 1200000000 | bytes 1000000 | tf_op jit(solution)/shard_map/project/pallas_call | solution.py:470
  70.6 0.0 collective-permute-done.13.refs_2_
  70.7 4.4 %collective-permute-done.14.refs_2_ = bf16[384,768]{1,0:T(8,128)(2,1)S(1)} collective-permute-done((bf16[384,768]{1,0:T(8,128)(2,1)S(1)}, bf16[384,768]{1,0:T(8,128)(2,1)S(1)}, u32[]{:S(2)}, u32[]{:S(2)}) %collective-permute-start.14) | collective-permute-done | bytes 589856 | tf_op jit(solution)/shard_map/ppermute | solution.py:439
  75.1 3.7 %collective-permute-done.12.refs_1_ = bf16[512,384]{1,0:T(8,128)(2,1)S(1)} collective-permute-done((bf16[512,384]{1,0:T(8,128)(2,1)S(1)}, bf16[512,384]{1,0:T(8,128)(2,1)S(1)}, u32[]{:S(2)}, u32[]{:S(2)}) %collective-permute-start.12) | collective-permute-done | bytes 393248 | tf_op jit(solution)/shard_map/ppermute | solution.py:344
  78.8 0.9 %collective-permute-start.16 = (bf16[512,384]{1,0:T(8,128)(2,1)S(1)}, bf16[512,384]{1,0:T(8,128)(2,1)S(1)}, u32[]{:S(2)}, u32[]{:S(2)}) collective-permute-start(bf16[512,384]{1,0:T(8,128)(2,1)S(1)} %collective-permute-done.12.refs_1_), channel_id=1, source_target_pairs={{0,1},{1,0},{2,3},{3,2},{4,5},{5,4},{6,7},{7,6},{8,9},{9,8},{10,11... | collective-permute-start | bytes 1179656 | tf_op jit(solution)/shard_map/ppermute | solution.py:344
  79.7 0.8 project.4.refs_0_
  80.4 0.6 collective-permute-done.16.refs_1_
  81.0 1.5 %project.5 = bf16[512,768]{1,0:T(8,128)(2,1)} custom-call(f32[512,768]{1,0:T(8,128)S(1)} %project.4.refs_0_, bf16[512,384]{1,0:T(8,128)(2,1)S(1)} %collective-permute-done.16.refs_1_, bf16[384,768]{1,0:T(8,128)(2,1)S(1)} %collective-permute-done.14.refs_2_), custom_call_target="tpu_custom_call" | custom-call | flops 600000000 | bytes 1000000 | tf_op jit(solution)/shard_map/project/pallas_call | solution.py:470
  (2 shorter events, 0.1 us)
Async XLA Ops:
  0.0 31.6 %copy-start.2 = (s32[12]{0:T(128)S(1)}, s32[12]{0:T(128)}, u32[]{:S(2)}) copy-start(s32[12]{0:T(128)} %refs_0_.7) | copy-start | bytes 148
  3.7 12.1 %collective-permute-start.3 = (bf16[384,512]{1,0:T(8,128)(2,1)}, bf16[384,512]{1,0:T(8,128)(2,1)S(1)}, u32[]{:S(2)}, u32[]{:S(2)}) collective-permute-start(bf16[384,512]{1,0:T(8,128)(2,1)} %get-tuple-element.34.q_hbm), channel_id=1, source_target_pairs={{0,4},{4,8},{8,12},{12,0},{1,5},{5,9},{9,13},{13,1},{2,6},{6,10},{... | collective-permute-start | bytes 1179656 | tf_op jit(solution)/shard_map/ppermute | solution.py:340
  5.8 20.5 %collective-permute-start = (bf16[768,512]{1,0:T(8,128)(2,1)}, bf16[768,512]{1,0:T(8,128)(2,1)S(1)}, u32[]{:S(2)}, u32[]{:S(2)}) collective-permute-start(bf16[768,512]{1,0:T(8,128)(2,1)} %get-tuple-element.33.kv_hbm), channel_id=1, source_target_pairs={{0,16},{16,0},{1,17},{17,1},{2,18},{18,2},{3,19},{19,3},{4,20},{20... | collective-permute-start | bytes 2359304 | tf_op jit(solution)/shard_map/ppermute | solution.py:344
  8.7 22.5 %collective-permute-start.1 = (bf16[768,512]{1,0:T(8,128)(2,1)}, bf16[768,512]{1,0:T(8,128)(2,1)S(1)}, u32[]{:S(2)}, u32[]{:S(2)}) collective-permute-start(bf16[768,512]{1,0:T(8,128)(2,1)} %get-tuple-element.33.kv_hbm), channel_id=1, source_target_pairs={{0,32},{32,64},{64,96},{96,128},{128,160},{160,192},{192,224},{224... | collective-permute-start | bytes 2359304 | tf_op jit(solution)/shard_map/ppermute | solution.py:340
  10.3 20.8 %collective-permute-start.2 = (bf16[768,512]{1,0:T(8,128)(2,1)}, bf16[768,512]{1,0:T(8,128)(2,1)S(1)}, u32[]{:S(2)}, u32[]{:S(2)}) collective-permute-start(bf16[768,512]{1,0:T(8,128)(2,1)} %get-tuple-element.33.kv_hbm), channel_id=1, source_target_pairs={{0,224},{32,0},{64,32},{96,64},{128,96},{160,128},{192,160},{224,1... | collective-permute-start | bytes 2359304 | tf_op jit(solution)/shard_map/ppermute | solution.py:340
  14.3 9.3 %collective-permute-start.4 = (bf16[384,512]{1,0:T(8,128)(2,1)}, bf16[384,512]{1,0:T(8,128)(2,1)S(1)}, u32[]{:S(2)}, u32[]{:S(2)}) collective-permute-start(bf16[384,512]{1,0:T(8,128)(2,1)} %get-tuple-element.34.q_hbm), channel_id=1, source_target_pairs={{0,12},{4,0},{8,4},{12,8},{1,13},{5,1},{9,5},{13,9},{2,14},{6,2},{... | collective-permute-start | bytes 1179656 | tf_op jit(solution)/shard_map/ppermute | solution.py:340
  15.7 10.5 %collective-permute-start.5 = (bf16[384,512]{1,0:T(8,128)(2,1)}, bf16[384,512]{1,0:T(8,128)(2,1)S(1)}, u32[]{:S(2)}, u32[]{:S(2)}) collective-permute-start(bf16[384,512]{1,0:T(8,128)(2,1)} %get-tuple-element.34.q_hbm), channel_id=1, source_target_pairs={{0,8},{4,12},{8,0},{12,4},{1,9},{5,13},{9,1},{13,5},{2,10},{6,14},... | collective-permute-start | bytes 1179656 | tf_op jit(solution)/shard_map/ppermute | solution.py:340
  17.5 1.1 %copy-start = (bf16[768,512]{1,0:T(8,128)(2,1)S(1)}, bf16[768,512]{1,0:T(8,128)(2,1)}, u32[]{:S(2)}) copy-start(bf16[768,512]{1,0:T(8,128)(2,1)} %get-tuple-element.33.kv_hbm) | copy-start | bytes 2359300
  18.7 1.0 %copy-start.1 = (bf16[384,512]{1,0:T(8,128)(2,1)S(1)}, bf16[384,512]{1,0:T(8,128)(2,1)}, u32[]{:S(2)}) copy-start(bf16[384,512]{1,0:T(8,128)(2,1)} %get-tuple-element.34.q_hbm) | copy-start | bytes 1179652
  31.2 10.3 %collective-permute-start.6 = (bf16[384,512]{1,0:T(8,128)(2,1)S(1)}, bf16[384,512]{1,0:T(8,128)(2,1)S(1)}, u32[]{:S(2)}, u32[]{:S(2)}) collective-permute-start(bf16[384,512]{1,0:T(8,128)(2,1)S(1)} %slice_select_fusion), channel_id=1, source_target_pairs={{0,16},{16,0},{1,17},{17,1},{2,18},{18,2},{3,19},{19,3},{4,20},{20... | collective-permute-start | bytes 1179656 | tf_op jit(solution)/shard_map/ppermute | solution.py:344
  31.4 6.5 %copy-start.3 = (bf16[384,3072]{1,0:T(8,128)(2,1)S(1)}, bf16[384,3072]{1,0:T(8,128)(2,1)}, u32[]{:S(2)}) copy-start(bf16[384,3072]{1,0:T(8,128)(2,1)} %param.12) | copy-start | bytes 7077892
  31.4 10.7 %collective-permute-start.7 = (bf16[384,512]{1,0:T(8,128)(2,1)S(1)}, bf16[384,512]{1,0:T(8,128)(2,1)S(1)}, u32[]{:S(2)}, u32[]{:S(2)}) collective-permute-start(bf16[384,512]{1,0:T(8,128)(2,1)S(1)} %slice.11), channel_id=1, source_target_pairs={{0,32},{32,64},{64,96},{96,128},{128,160},{160,192},{192,224},{224... | collective-permute-start | bytes 1179656 | tf_op jit(solution)/shard_map/ppermute | solution.py:399
  38.0 23.9 %collective-permute-start.9 = (bf16[384,768]{1,0:T(8,128)(2,1)S(1)}, bf16[384,768]{1,0:T(8,128)(2,1)S(1)}, u32[]{:S(2)}, u32[]{:S(2)}) collective-permute-start(bf16[384,768]{1,0:T(8,128)(2,1)S(1)} %constant_dynamic-slice_fusion.3), channel_id=1, source_target_pairs={{0,1},{1,0},{2,3},{3,2},{4,5},{5,4},{6,7},{7,6},{8,9},{9,8},{10,11... | collective-permute-start | bytes 1769480 | tf_op jit(solution)/shard_map/ppermute | solution.py:344
  44.4 11.6 %collective-permute-start.8 = (bf16[400,512]{1,0:T(8,128)(2,1)S(1)}, bf16[400,512]{1,0:T(8,128)(2,1)S(1)}, u32[]{:S(2)}, u32[]{:S(2)}) collective-permute-start(bf16[400,512]{1,0:T(8,128)(2,1)S(1)} %attend_far.3), channel_id=1, source_target_pairs={{0,8},{4,12},{8,0},{12,4},{1,9},{5,13},{9,1},{13,5},{2,10},{6,14},... | collective-permute-start | bytes 1228808 | tf_op jit(solution)/shard_map/ppermute | solution.py:340
  52.4 11.6 %collective-permute-start.10 = (bf16[400,512]{1,0:T(8,128)(2,1)S(1)}, bf16[400,512]{1,0:T(8,128)(2,1)S(1)}, u32[]{:S(2)}, u32[]{:S(2)}) collective-permute-start(bf16[400,512]{1,0:T(8,128)(2,1)S(1)} %get-tuple-element.53), channel_id=1, source_target_pairs={{0,12},{4,0},{8,4},{12,8},{1,13},{5,1},{9,5},{13,9},{2,14},{6,2},{... | collective-permute-start | bytes 1228808 | tf_op jit(solution)/shard_map/ppermute | solution.py:340
  54.6 9.4 %collective-permute-start.11 = (bf16[400,512]{1,0:T(8,128)(2,1)S(1)}, bf16[400,512]{1,0:T(8,128)(2,1)S(1)}, u32[]{:S(2)}, u32[]{:S(2)}) collective-permute-start(bf16[400,512]{1,0:T(8,128)(2,1)S(1)} %get-tuple-element.54), channel_id=1, source_target_pairs={{0,4},{4,8},{8,12},{12,0},{1,5},{5,9},{9,13},{13,1},{2,6},{6,10},{... | collective-permute-start | bytes 1228808 | tf_op jit(solution)/shard_map/ppermute | solution.py:340
  54.7 15.9 %collective-permute-start.13 = (bf16[384,768]{1,0:T(8,128)(2,1)S(1)}, bf16[384,768]{1,0:T(8,128)(2,1)S(1)}, u32[]{:S(2)}, u32[]{:S(2)}) collective-permute-start(bf16[384,768]{1,0:T(8,128)(2,1)S(1)} %get-tuple-element.63), channel_id=1, source_target_pairs={{0,2},{2,0},{1,3},{3,1},{4,6},{6,4},{5,7},{7,5},{8,10},{10,8},{9,1... | collective-permute-start | bytes 1769480 | tf_op jit(solution)/shard_map/ppermute | solution.py:344
  56.0 19.1 %collective-permute-start.14 = (bf16[384,768]{1,0:T(8,128)(2,1)S(1)}, bf16[384,768]{1,0:T(8,128)(2,1)S(1)}, u32[]{:S(2)}, u32[]{:S(2)}) collective-permute-start(bf16[384,768]{1,0:T(8,128)(2,1)S(1)} %get-tuple-element.62), channel_id=1, source_target_pairs={{0,19},{1,18},{2,17},{3,16},{16,3},{17,2},{18,1},{19,0},{4,23},{5,... | collective-permute-start | bytes 1769480 | tf_op jit(solution)/shard_map/ppermute | solution.py:439
  64.4 5.1 %collective-permute-start.15 = (bf16[512,384]{1,0:T(8,128)(2,1)S(1)}, bf16[512,384]{1,0:T(8,128)(2,1)S(1)}, u32[]{:S(2)}, u32[]{:S(2)}) collective-permute-start(bf16[512,384]{1,0:T(8,128)(2,1)S(1)} %merge_last.1.refs_0_), channel_id=1, source_target_pairs={{0,1},{1,0},{2,3},{3,2},{4,5},{5,4},{6,7},{7,6},{8,9},{9,8},{10,11... | collective-permute-start | bytes 1179656 | tf_op jit(solution)/shard_map/ppermute | solution.py:344
  68.1 10.7 %collective-permute-start.12 = (bf16[512,384]{1,0:T(8,128)(2,1)S(1)}, bf16[512,384]{1,0:T(8,128)(2,1)S(1)}, u32[]{:S(2)}, u32[]{:S(2)}) collective-permute-start(bf16[512,384]{1,0:T(8,128)(2,1)S(1)} %merge_last.1.refs_0_), channel_id=1, source_target_pairs={{0,2},{2,0},{1,3},{3,1},{4,6},{6,4},{5,7},{7,5},{8,10},{10,8},{9,1... | collective-permute-start | bytes 1179656 | tf_op jit(solution)/shard_map/ppermute | solution.py:344
  78.8 2.2 %collective-permute-start.16 = (bf16[512,384]{1,0:T(8,128)(2,1)S(1)}, bf16[512,384]{1,0:T(8,128)(2,1)S(1)}, u32[]{:S(2)}, u32[]{:S(2)}) collective-permute-start(bf16[512,384]{1,0:T(8,128)(2,1)S(1)} %collective-permute-done.12.refs_1_), channel_id=1, source_target_pairs={{0,1},{1,0},{2,3},{3,2},{4,5},{5,4},{6,7},{7,6},{8,9},{9,8},{10,11... | collective-permute-start | bytes 1179656 | tf_op jit(solution)/shard_map/ppermute | solution.py:344
